TPU v7x, 512 devices: a whole 4x8x8 slice. The times are simulated.
512 devices in a mesh: row: 64 (over z, y_hi, x), col: 8 (over y_lo, core).
Axes of the slice: x: 4, y: 8 (y_hi: 2, y_lo: 4; y = y_hi * 4 + y_lo), z: 8, core: 2. Of those that a mesh axis runs over, the one named last changes fastest.
Arguments:
- a_tiles: bfloat16 [4096, 48, 64, 64], P('row', 'col'), may hold values from -4 to 4
- a_cols: int32 [4096, 48], P('row', 'col'), may hold values from 0 to 511
- a_count: int32 [4096, 8], P('row', 'col'), may hold values from 1 to 6
- a_slot: int32 [4096, 48], P('row', 'col'), may hold values from 0 to 26
- agg: int32 [4096], P('row'), may hold values from 0 to 3
- p_tiles: bfloat16 [8, 512, 64, 64], P('col', 'row'), may hold values from -0.75 to 0.75
Outputs:
- coarse: float32 [128, 27, 64, 64], P('row', None, 'col')
All inputs are finite; a program needn't handle non-finite values.
Results may differ from a plain program's by a relative error of at most 0.0065.
Values may be sent and summed in bfloat16 or wider, within the bound.
No kernel may reach another device: no remote copies, remote signals or barrier semaphores. Data moves between devices by JAX's collectives and lax.ppermute only.
A program may use at most 128 MiB of HBM per device.

v0:
```python
import jax
import jax.numpy as jnp
from jax import lax
from jax.sharding import PartitionSpec as P

KC = 27
CR = 2


def from_behind(value, axis, by):
    count = lax.axis_size(axis)
    return lax.ppermute(value, axis, [(i, (i + by) % count) for i in range(count)])


def body(a_tiles, a_cols, a_count, a_slot, agg, p_tiles):
    rows, slots, tile, _ = a_tiles.shape
    share = p_tiles.shape[1]
    area = tile * tile
    flat_p = p_tiles.reshape(share, area)
    wanted = a_cols.reshape(rows * slots)
    mine = lax.axis_index("row") * share + jnp.arange(share, dtype=jnp.int32)
    piece = lax.all_gather(flat_p, "row", axis=0, tiled=True)
    local = jnp.arange(piece.shape[0], dtype=jnp.int32)
    pick = (wanted[:, None] == local[None, :]).astype(jnp.bfloat16)
    pick_own = (mine[:, None] == local[None, :]).astype(jnp.bfloat16)
    chosen = jnp.dot(pick, piece, preferred_element_type=jnp.float32)
    own_f = jnp.dot(pick_own, piece, preferred_element_type=jnp.float32)
    chosen = chosen.astype(jnp.bfloat16).reshape(rows, slots, tile, tile)
    own_b = own_f.astype(jnp.bfloat16).reshape(1, share, area)
    own_all = lax.all_gather(own_b, "col", axis=0, tiled=True)
    own_p = own_all.transpose(1, 0, 2).reshape(rows, tile, tile)
    product = jnp.einsum(
        "bkxy,bkyz->bkxz", a_tiles, chosen, preferred_element_type=jnp.float32
    ).astype(jnp.bfloat16)
    term = jnp.einsum("byx,bkyz->bkxz", own_p, product, preferred_element_type=jnp.float32)
    term = term.reshape(rows * slots, area)
    targets = 2 * CR * KC
    dest = (agg[:, None] * KC + a_slot).reshape(-1)
    live = (jnp.arange(slots, dtype=jnp.int32)[None, :] < a_count).reshape(-1)
    onehot = (
        (dest[:, None] == jnp.arange(targets, dtype=jnp.int32)[None, :]) & live[:, None]
    ).astype(jnp.bfloat16)
    term_high = term.astype(jnp.bfloat16)
    term_low = (term - term_high.astype(jnp.float32)).astype(jnp.bfloat16)
    partial_value = jnp.einsum(
        "nd,na->da", onehot, term_high, preferred_element_type=jnp.float32
    ) + jnp.einsum("nd,na->da", onehot, term_low, preferred_element_type=jnp.float32)
    partial_value = partial_value.reshape(2, CR, KC, tile, tile)
    moved = from_behind(partial_value[1], "row", 1)
    result = lax.psum_scatter(partial_value[0] + moved, "col", scatter_dimension=2, tiled=True)
    return result


def solution(mesh):
    return jax.shard_map(
        body,
        mesh=mesh,
        in_specs=(
            P("row", "col", None, None),
            P("row", "col"),
            P("row", "col"),
            P("row", "col"),
            P("row"),
            P("col", "row", None, None),
        ),
        out_specs=P("row", None, "col", None),
        check_vma=False,
    )
```

profile of v0, /device:TPU:1, one launch (start us, length us, event | category | flops | bytes accessed | tf_op | source)
XLA Modules:
  0.0 375.2 jit_solution(16938738150631090432)
XLA Ops:
  6.5 0.0 all-gather.3.cloned.1.call-start
  6.5 1.7 reshape.42
  8.2 0.0 all-gather.3.cloned.1.call-update
  8.3 0.0 reduce-scatter.2.cloned.1.call-start
  8.3 0.8 copy.9
  9.1 0.1 eq.47
  9.3 0.7 broadcast_multiply_fusion
  9.9 0.7 broadcast_add_fusion
  10.6 0.1 copy.8
  10.7 0.1 eq.43
  10.8 0.7 iota_compare_fusion.3
  11.6 0.1 lt.26
  11.7 150.2 %all-gather.3.cloned.1.call-done = bf16[512,4096]{1,0:T(8,128)(2,1)} async-done(((bf16[8,4096]{1,0:T(8,128)(2,1)}), bf16[512,4096]{1,0:T(8,128)(2,1)}) %all-gather.3.cloned.1.call-update) | async-done | bytes 4194320 | tf_op jit(solution)/shard_map/all_gather | solution.py:22
  161.9 4.0 %convolution_convert_fusion = bf16[384,4096]{1,0:T(8,128)(2,1)S(1)} fusion(bf16[512,4096]{1,0:T(8,128)(2,1)} %all-gather.3.cloned.1.call-done, s32[384]{0:T(512)S(1)} %eq.47), kind=kOutput, calls=%fused_computation.4 | convolution fusion | flops 1612382208 | bytes 7341568 | tf_op jit(solution)/shard_map/dot_general | solution.py:26
  165.9 7.9 %reshape.43 = bf16[64,6,64,64]{3,2,1,0:T(8,128)(2,1)} reshape(bf16[384,4096]{1,0:T(8,128)(2,1)S(1)} %convolution_convert_fusion) | data formatting | bytes 6291456 | tf_op jit(solution)/shard_map/reshape | solution.py:28
  173.9 2.9 convolution_convert_fusion.1
  176.7 25.5 %all-gather = bf16[64,4096]{1,0:T(8,128)(2,1)S(1)} all-gather(bf16[8,4096]{1,0:T(8,128)(2,1)S(1)} %convolution_convert_fusion.1), channel_id=2, replica_groups=mesh['row'=64,'col'=8] {'col'}, dimensions={0}, use_global_device_ids=true | all-gather | bytes 589824 | tf_op jit(solution)/shard_map/all_gather | solution.py:30
  202.2 0.3 copy.10
  202.5 1.1 reshape.48
  203.7 10.8 %fusion.3 = f32[64,6,64,64]{2,3,1,0:T(8,128)} fusion(bf16[64,6,64,64]{3,2,1,0:T(8,128)(2,1)} %reshape.43, bf16[64,6,64,64]{3,2,1,0:T(8,128)(2,1)} %param.6, bf16[64,64,64,1]{2,1,0,3:T(8,128)(2,1)S(1)} %reshape.48), kind=kOutput, calls=%fused_computation.7 | convolution fusion | flops 404226048 | bytes 13107200 | tf_op jit(solution)/shard_map/byx,bkyz->bkxz/dot_general | solution.py:35
  214.4 12.6 %copy.11 = f32[64,6,64,64]{3,2,1,0:T(8,128)} copy(f32[64,6,64,64]{2,3,1,0:T(8,128)} %fusion.3) | data formatting | bytes 12582912 | tf_op jit(solution)/shard_map/byx,bkyz->bkxz/transpose | solution.py:35
  227.0 10.8 %reshape.46 = f32[384,4096]{1,0:T(8,128)} reshape(f32[64,6,64,64]{3,2,1,0:T(8,128)} %copy.11) | data formatting | bytes 12582912 | tf_op jit(solution)/shard_map/reshape | solution.py:36
  237.9 0.0 copy-start
  237.9 3.8 %fusion.9 = f32[108,4096]{1,0:T(8,128)S(1)} fusion(f32[384,4096]{1,0:T(8,128)} %reshape.46, s32[384]{0:T(512)S(1)} %eq.43, pred[384]{0:T(512)(128)(4,1)S(1)} %lt.26), kind=kOutput, calls=%fused_computation.10 | convolution fusion | flops 341394432 | bytes 8062848 | tf_op jit(solution)/shard_map/nd,na->da/dot_general | solution.py:45
  241.6 0.8 copy-done
  242.5 0.8 convolution_add_fusion
  243.3 0.1 fusion.21
  243.4 1.9 squeeze.7
  245.3 3.1 collective-permute-start
  248.4 0.7 squeeze.6
  249.1 78.5 %collective-permute-done = f32[2,27,64,64]{3,2,1,0:T(8,128)} collective-permute-done((f32[2,27,64,64]{3,2,1,0:T(8,128)}, f32[2,27,64,64]{3,2,1,0:T(8,128)}, u32[]{:S(2)}, u32[]{:S(2)}) %collective-permute-start) | collective-permute-done | bytes 884768 | tf_op jit(solution)/shard_map/ppermute | solution.py:12
  327.6 3.0 add.31
  330.6 0.0 reduce-scatter.2.cloned.1.call-update
  330.6 37.7 %reduce-scatter.2.cloned.1.call-done = f32[2,27,8,64]{3,2,1,0:T(8,128)} async-done(((f32[2,27,64,64]{3,2,1,0:T(8,128)}), f32[2,27,8,64]{3,2,1,0:T(8,128)}) %reduce-scatter.2.cloned.1.call-update) | async-done | bytes 110608 | tf_op jit(solution)/shard_map/reduce_scatter | solution.py:50
  (1 shorter events, 0.0 us)
Async XLA Ops:
  6.5 155.4 %all-gather.3.cloned.1.call-start = ((), (), s32[]{:S(2)}) async-start(), calls=%async_computation.1 | async-start | bytes 4259840 | tf_op jit(solution)/shard_map/all_gather | solution.py:22
  8.3 360.1 %reduce-scatter.2.cloned.1.call-start = ((), (), s32[]{:S(2)}) async-start(), calls=%async_computation.2 | async-start | bytes 1990656 | tf_op jit(solution)/shard_map/reduce_scatter | solution.py:50
  237.9 4.6 %copy-start = (f32[384,4096]{1,0:T(8,128)S(1)}, f32[384,4096]{1,0:T(8,128)}, u32[]{:S(2)}) copy-start(f32[384,4096]{1,0:T(8,128)} %reshape.46) | copy-start | bytes 18874372
  245.3 82.3 %collective-permute-start = (f32[2,27,64,64]{3,2,1,0:T(8,128)}, f32[2,27,64,64]{3,2,1,0:T(8,128)}, u32[]{:S(2)}, u32[]{:S(2)}) collective-permute-start(f32[2,27,64,64]{3,2,1,0:T(8,128)} %squeeze.7), channel_id=1, source_target_pairs={{0,8},{8,16},{16,24},{24,32},{32,40},{40,48},{48,56},{56,64},{64,7... | collective-permute-start | bytes 2654216 | tf_op jit(solution)/shard_map/ppermute | solution.py:12
Sparse Core Ops, SparseCore 0:
  11.9 150.0 all-gather.2
  330.7 37.5 reduce-scatter.1
where the time goes:
time: 377 us; the launch traced here: 375 us
  waiting for transfers between devices  266 us (71%)
  local copies, waits for them, and re-layouts  39.3 us (10%)
  blocking collectives  25.5 us (7%)
  matrix products  22.3 us (6%)
  between operations  13.5 us (4%)
  other arithmetic  5.07 us (1%)
    all_gather x1, waiting for transfers between devices, body(): piece = lax.all_gather(flat_p, 'row', axis=0, tiled=True)  150 us
    ppermute x1, waiting for transfers between devices, from_behind(): lax.ppermute(value, axis, [(i, (i + by) % count) for i in range(count)])  78.5 us
    reduce_scatter x1, waiting for transfers between devices, body(): lax.psum_scatter(partial_value[0] + moved, 'col', scatter_dimension=2, ti...  37.7 us
    all_gather x1, blocking collectives, body(): own_all = lax.all_gather(own_b, 'col', axis=0, tiled=True)  25.5 us
    transpose x1, local copies, waits for them, and re-layouts, body(): jnp.einsum('byx,bkyz->bkxz', own_p, product, preferred_element_type=jnp.f...  12.6 us
    reshape x1, local copies, waits for them, and re-layouts, body(): term = term.reshape(rows * slots, area)  10.8 us
    dot_general x1, matrix products, body(): jnp.einsum('byx,bkyz->bkxz', own_p, product, preferred_element_type=jnp.f...  10.8 us
    reshape x1, local copies, waits for them, and re-layouts, body(): chosen = chosen.astype(jnp.bfloat16).reshape(rows, slots, tile, tile)  7.93 us
  transfers between devices with their start and end apart: 3, of which 3 were waited for; matrix products, arithmetic and copies ran while one was open for 1% of the time, Pallas kernels for 0%

commit v1 on v0

v1 whole, which is shorter than its diff:
```python
import jax
import jax.numpy as jnp
from jax import lax
from jax.experimental import pallas as pl
from jax.experimental.pallas import tpu as pltpu
from jax.sharding import Mesh, PartitionSpec as P

KC = 27
CR = 2
T = 64
NY = 4
ROW = ("z", "yh", "x")
COL = ("yl", "core")
UNROLL = 8
F32 = jnp.float32
BF16 = jnp.bfloat16


def spread(value, axis):
    count = lax.axis_size(axis)
    copies = jnp.broadcast_to(value[None], (count,) + value.shape)
    return lax.all_to_all(copies, axis, 0, 0, tiled=True)


def left_kernel(own_ref, a_ref, b_ref):
    for c in range(8):
        both = own_ref[c, 0].astype(F32).T.astype(BF16)
        for h in range(2):
            left = both[h * T:(h + 1) * T]
            for s in range(a_ref.shape[3]):
                b_ref[h, 0, c, s] = jnp.dot(left, a_ref[h, 0, c, s], preferred_element_type=F32).astype(BF16)


def left_products(own, a_tiles):
    rows, slots = a_tiles.shape[:2]
    a = a_tiles.reshape(2, 4, 8, slots, T, T)
    b = pl.pallas_call(
        left_kernel,
        grid=(4,),
        in_specs=[
            pl.BlockSpec((8, 1, T, 2 * T), lambda v: (0, v, 0, 0)),
            pl.BlockSpec((2, 1, 8, slots, T, T), lambda v: (0, v, 0, 0, 0, 0)),
        ],
        out_specs=pl.BlockSpec((2, 1, 8, slots, T, T), lambda v: (0, v, 0, 0, 0, 0)),
        out_shape=jax.ShapeDtypeStruct(a.shape, BF16),
        compiler_params=pltpu.CompilerParams(vmem_limit_bytes=40 * 2**20),
        cost_estimate=pl.CostEstimate(flops=2 * rows * slots * T**3, bytes_accessed=16 * 2**20, transcendentals=0),
        name="left_products",
    )(own, a)
    return b.reshape(rows * slots, T, T)


def sum_kernel(which_ref, pair_ref, into_ref, info_ref, panel_ref, b_ref, out_ref, acc):
    core = info_ref[1]

    @pl.loop(0, acc.shape[0] // 2)
    def _(d):
        for e in range(2):
            acc[2 * d + e] = jnp.zeros((T, 2 * T), F32)

    @pl.loop(0, (info_ref[0] + UNROLL - 1) // UNROLL)
    def _(step):
        for half in range(2):
            base = step * UNROLL + half * (UNROLL // 2)
            terms = [
                jnp.dot(b_ref[which_ref[base + e]], panel_ref[pair_ref[base + e]], preferred_element_type=F32)
                for e in range(UNROLL // 2)
            ]
            for e in range(UNROLL // 2):
                d = into_ref[base + e]
                acc[d] = acc[d] + terms[e]

    low = lax.broadcasted_iota(jnp.int32, (T, 2 * T), 1) < T

    @pl.loop(0, KC)
    def _(k):
        parts = []
        for p in range(2):
            d0 = 2 * ((2 * p) * KC + k)
            d1 = 2 * ((2 * p + 1) * KC + k)
            parts.append(jnp.where(low, acc[d0], acc[d1 + 1]) + pltpu.roll(jnp.where(low, acc[d1], acc[d0 + 1]), T, 1))
        for o in range(8):
            tile = jnp.concatenate([parts[0][o * 8:(o + 1) * 8], parts[1][o * 8:(o + 1) * 8]], axis=0)
            out_ref[jnp.bitwise_xor(core, o % 2), o // 2, k] = tile.astype(BF16)


def panel_sums(which, pair, into, info, panel, b):
    slots = b.shape[0]
    smem = pl.BlockSpec(memory_space=pltpu.SMEM)
    vmem = pl.BlockSpec(memory_space=pltpu.VMEM)
    return pl.pallas_call(
        sum_kernel,
        in_specs=[smem, smem, smem, smem, vmem, vmem],
        out_specs=vmem,
        out_shape=jax.ShapeDtypeStruct((2, NY, KC, 16, 2 * T), BF16),
        scratch_shapes=[pltpu.VMEM((2 * (2 * CR * KC + 1), T, 2 * T), F32)],
        compiler_params=pltpu.CompilerParams(vmem_limit_bytes=40 * 2**20),
        cost_estimate=pl.CostEstimate(flops=4 * slots * T**3, bytes_accessed=16 * 2**20, transcendentals=0),
        name="panel_sums",
    )(which, pair, into, info, panel, b)


def body(a_tiles, a_cols, a_count, a_slot, agg, p_tiles):
    rows, slots = a_tiles.shape[:2]
    total = rows * slots
    packed = jnp.concatenate([p_tiles[0, :4], p_tiles[0, 4:]], axis=-1)

    own = spread(packed, COL)
    near = spread(packed, ("yh", "x"))
    panel = lax.all_gather(near, "z", axis=0, tiled=False).reshape(-1, T, 2 * T)

    live = (jnp.arange(slots, dtype=jnp.int32)[None, :] < a_count).reshape(total)
    before = jnp.cumsum(live.astype(jnp.int32)) - 1
    n_live = before[-1] + 1
    here = (before[None, :] == jnp.arange(total, dtype=jnp.int32)[:, None]) & live[None, :]

    def front(value, fill):
        value = value.reshape(total)
        kept = jnp.sum(jnp.where(here, value[None, :], 0), axis=1)
        return jnp.where(jnp.arange(total) < n_live, kept, fill).astype(jnp.int32)

    which = front(jnp.arange(total, dtype=jnp.int32), 0)
    pair = front((a_cols // 8) * 4 + a_cols % 4, 0)
    target = 2 * (agg[:, None] * KC + a_slot) + (a_cols % 8) // 4
    into = front(target, 2 * 2 * CR * KC)
    info = jnp.stack([n_live, lax.axis_index("core")]).astype(jnp.int32)

    b = left_products(own, a_tiles)
    sums = panel_sums(which, pair, into, info, panel, b)
    other = lax.ppermute(sums[1], "core", [(0, 1), (1, 0)])
    chip = (sums[0].astype(F32) + other.astype(F32)).astype(BF16)
    shares = lax.all_to_all(chip, "yl", 0, 0, tiled=True)
    done = jnp.sum(shares.astype(F32), axis=0)
    count = lax.axis_size(ROW)
    moved = lax.ppermute(done[:, 8:].astype(BF16), ROW, [(i, (i + 1) % count) for i in range(count)])
    result = done[:, :8] + moved.astype(F32)
    return jnp.stack([result[..., :T], result[..., T:]])


def solution(mesh):
    fine = Mesh(mesh.devices.reshape(8, 2, 4, 4, 2), ROW + COL)
    return jax.shard_map(
        body,
        mesh=fine,
        in_specs=(
            P(ROW, COL, None, None),
            P(ROW, COL),
            P(ROW, COL),
            P(ROW, COL),
            P(ROW),
            P(COL, ROW, None, None),
        ),
        out_specs=P(ROW, None, COL, None),
        check_vma=False,
    )
```

time: 377 us -> 151 us (0.40)
  waiting for transfers between devices: 266 us -> 51.1 us
  local copies, waits for them, and re-layouts: 39.3 us -> 13.9 us
  matrix products: 22.3 us -> 0 us
  blocking collectives: 25.5 us -> 40.3 us
  Pallas kernels: 0 us -> 12 us
  starting transfers between devices: 3.13 us -> 14.5 us
    all_gather x1, waiting for transfers between devices: 150 us -> 29.7 us  [body(): panel = lax.all_gather(near, 'z', axis=0, tiled=False).reshape(-1, T, 2 * T)]
    ppermute x1 -> x2, waiting for transfers between devices: 78.5 us -> 12 us  [the longest x1 10.6 us: body(): lax.ppermute(done[:, 8:].astype(BF16), ROW, [(i, (i + 1) % count) for i i...]
    all_to_all x0 -> x2, blocking collectives: none -> 40.3 us  [the longest x1 24.4 us: spread(): return lax.all_to_all(copies, axis, 0, 0, tiled=True)]
    reduce_scatter x1 -> x0, waiting for transfers between devices: 37.7 us -> none  [body(): lax.psum_scatter(partial_value[0] + moved, 'col', scatter_dimension=2, ti...]
    all_gather x1 -> x0, blocking collectives: 25.5 us -> none  [body(): own_all = lax.all_gather(own_b, 'col', axis=0, tiled=True)]
    dot_general x5 -> x0, matrix products: 22.3 us -> none  [the longest x1 10.8 us: body(): jnp.einsum('byx,bkyz->bkxz', own_p, product, preferred_element_type=jnp.f...]
    reshape x4 -> x0, local copies, waits for them, and re-layouts: 21.6 us -> none  [the longest x1 10.8 us: body(): term = term.reshape(rows * slots, area)]
    transpose x2 -> x0, local copies, waits for them, and re-layouts: 12.9 us -> none  [the longest x1 12.6 us: body(): jnp.einsum('byx,bkyz->bkxz', own_p, product, preferred_element_type=jnp.f...]
  transfers between devices with their start and end apart: 3 -> 4, of which waited for: 3 -> 4; matrix products, arithmetic and copies ran while one was open for 1% -> 3% of each run, Pallas kernels for 0% -> 2%
where the time goes in v1:
time: 151 us; the launch traced here: 150 us
  waiting for transfers between devices  51.1 us (34%)
  blocking collectives  40.3 us (27%)
  starting transfers between devices  14.5 us (10%)
  between operations  14.2 us (9%)
  local copies, waits for them, and re-layouts  13.9 us (9%)
  Pallas kernels  12 us (8%)
  other arithmetic  3.98 us (3%)
    all_gather x1, waiting for transfers between devices, body(): panel = lax.all_gather(near, 'z', axis=0, tiled=False).reshape(-1, T, 2 * T)  29.7 us
    all_to_all x1, blocking collectives, spread(): return lax.all_to_all(copies, axis, 0, 0, tiled=True)  24.4 us
    all_to_all x1, blocking collectives, body(): shares = lax.all_to_all(chip, 'yl', 0, 0, tiled=True)  15.9 us
    ppermute x1, waiting for transfers between devices, body(): lax.ppermute(done[:, 8:].astype(BF16), ROW, [(i, (i + 1) % count) for i i...  10.6 us
    unnamed x8, local copies, waits for them, and re-layouts  10.5 us
    all_to_all x1, waiting for transfers between devices, spread(): return lax.all_to_all(copies, axis, 0, 0, tiled=True)  9.39 us
    pallas_call x1, Pallas kernels, panel_sums(): pl.pallas_call(sum_kernel, in_specs=[smem, smem, smem, smem, vmem, vmem],...  8.64 us
    all_to_all x1, starting transfers between devices, spread(): return lax.all_to_all(copies, axis, 0, 0, tiled=True)  8.36 us
  transfers between devices with their start and end apart: 4, of which 4 were waited for; matrix products, arithmetic and copies ran while one was open for 3% of the time, Pallas kernels for 2%

profile of v1, /device:TPU:1, one launch (start us, length us, event | category | flops | bytes accessed | tf_op | source)
XLA Modules:
  0.0 150.0 jit_solution(17341922939136070588)
XLA Ops:
  6.5 0.0 all-gather.3.cloned.1.call-start
  6.5 0.9 slice_bitcast_fusion.5
  7.4 0.1 pad_maximum_fusion.1
  7.5 0.9 broadcast_in_dim.59
  8.4 24.4 %all_to_all.15 = bf16[8,4,64,128]{3,2,1,0:T(8,128)(2,1)} all-to-all(bf16[8,4,64,128]{3,2,1,0:T(8,128)(2,1)} %broadcast_in_dim.59), channel_id=1, replica_groups=mesh['z'=8,'yh'=2,'x'=4,'yl'=4,'core'=2] {'yh','x'}, dimensions={0} | all-to-all | bytes 1048576 | tf_op jit(solution)/shard_map/all_to_all | solution.py:22
  32.9 0.0 all-gather.3.cloned.1.call-update
  32.9 8.4 %all-to-all-start.1 = ((bf16[8,4,64,128]{3,2,1,0:T(8,128)(2,1)}), bf16[8,4,64,128]{3,2,1,0:T(8,128)(2,1)S(1)}, u32[]{:S(2)}, u32[]{:S(2)}) async-start(bf16[8,4,64,128]{3,2,1,0:T(8,128)(2,1)} %broadcast_in_dim.59), calls=%async_computation.1 | async-start | bytes 1048576 | tf_op jit(solution)/shard_map/all_to_all | solution.py:22
  41.2 0.7 broadcast_multiply_fusion
  41.9 0.7 fusion.3
  42.6 0.1 copy.11
  42.7 0.1 broadcast_in_dim.54
  42.9 0.1 copy.12
  43.0 0.1 broadcast_in_dim.56
  43.1 0.7 iota_compare_fusion.1
  43.8 0.1 lt.51
  44.0 0.1 reshape.69
  44.1 0.3 reduce-window.9
  44.4 0.1 slice.35
  44.5 0.1 slice_reduce_fusion
  44.7 0.1 add_bitcast_fusion
  44.7 0.6 slice.37
  46.0 0.1 pad_add_fusion.info_ref
  46.1 0.4 select_reduce_fusion
  46.5 9.4 %all-to-all-done.1.own_ref = bf16[8,4,64,128]{3,2,1,0:T(8,128)(2,1)S(1)} async-done(((bf16[8,4,64,128]{3,2,1,0:T(8,128)(2,1)}), bf16[8,4,64,128]{3,2,1,0:T(8,128)(2,1)S(1)}, u32[]{:S(2)}, u32[]{:S(2)}) %all-to-all-start.1) | async-done | bytes 524320 | tf_op jit(solution)/shard_map/all_to_all | solution.py:22
  55.8 0.0 copy-start.2
  55.8 2.8 %copy-done.2 = bf16[64,6,64,64]{3,2,1,0:T(8,128)(2,1)S(1)} copy-done((bf16[64,6,64,64]{3,2,1,0:T(8,128)(2,1)S(1)}, bf16[64,6,64,64]{3,2,1,0:T(8,128)(2,1)}, u32[]{:S(2)}) %copy-start.2) | copy-done | bytes 3145752
  58.7 3.4 %left_products.1 = bf16[2,4,8,6,64,64]{5,4,3,2,1,0:T(8,128)(2,1)S(1)} custom-call(bf16[8,4,64,128]{3,2,1,0:T(8,128)(2,1)S(1)} %all-to-all-done.1.own_ref, bf16[2,4,8,6,64,64]{5,4,3,2,1,0:T(8,128)(2,1)S(1)} %bitcast.24), custom_call_target="tpu_custom_call" | custom-call | flops 201326592 | bytes 16777216 | tf_op jit(solution)/shard_map/left_products/pallas_call | solution.py:37
  62.0 0.0 copy-start
  62.1 2.7 %copy-done = bf16[2,4,8,6,64,64]{5,4,3,2,1,0:T(8,128)(2,1)} copy-done((bf16[2,4,8,6,64,64]{5,4,3,2,1,0:T(8,128)(2,1)}, bf16[2,4,8,6,64,64]{5,4,3,2,1,0:T(8,128)(2,1)S(1)}, u32[]{:S(2)}) %copy-start) | copy-done | bytes 3145752
  64.7 29.7 %all-gather.3.cloned.1.call-done = bf16[64,4,64,128]{3,2,1,0:T(8,128)(2,1)} async-done(((bf16[8,4,64,128]{3,2,1,0:T(8,128)(2,1)}), bf16[64,4,64,128]{3,2,1,0:T(8,128)(2,1)}) %all-gather.3.cloned.1.call-update) | async-done | bytes 4194320 | tf_op jit(solution)/shard_map/all_gather | solution.py:110
  94.4 0.0 copy-start.1
  94.4 2.8 %copy-done.1 = bf16[2,4,8,6,64,64]{5,4,3,2,1,0:T(8,128)(2,1)S(1)} copy-done((bf16[2,4,8,6,64,64]{5,4,3,2,1,0:T(8,128)(2,1)S(1)}, bf16[2,4,8,6,64,64]{5,4,3,2,1,0:T(8,128)(2,1)}, u32[]{:S(2)}) %copy-start.1) | copy-done | bytes 3145752
  97.2 0.0 copy-start.3
  97.2 2.2 %copy-done.3 = bf16[64,4,64,128]{3,2,1,0:T(8,128)(2,1)S(1)} copy-done((bf16[64,4,64,128]{3,2,1,0:T(8,128)(2,1)S(1)}, bf16[64,4,64,128]{3,2,1,0:T(8,128)(2,1)}, u32[]{:S(2)}) %copy-start.3) | copy-done | bytes 4194328
  99.4 8.6 %panel_sums.1 = bf16[2,4,27,16,128]{4,3,2,1,0:T(8,128)(2,1)S(1)} custom-call(s32[384]{0:T(512)S(1)} %fusion.12.which_ref, s32[384]{0:T(512)S(1)} %get-tuple-element.17.pair_ref, s32[384]{0:T(512)S(1)} %get-tuple-element.16.into_ref, s32[2]{0:T(128)S(1)} %pad_add_fusion.info_ref, bf16[256,64,128]{2,1,0:T(8,128)(2,1)S(1)} %bitcast.25, ...), custom_call_target="tpu_custom_call" | custom-call | flops 402653184 | bytes 16777216 | tf_op jit(solution)/shard_map/panel_sums/pallas_call | solution.py:91
  108.1 3.1 %collective-permute-start = (bf16[4,27,16,128]{3,2,1,0:T(8,128)(2,1)S(1)}, bf16[4,27,16,128]{3,2,1,0:T(8,128)(2,1)S(1)}, u32[]{:S(2)}, u32[]{:S(2)}) collective-permute-start(bf16[4,27,16,128]{3,2,1,0:T(8,128)(2,1)S(1)} %slice_bitcast_fusion), channel_id=1, source_target_pairs={{0,1},{1,0},{2,3},{3,2},{4,5},{5,4},{6,7},{7,6},{8,9},{9,8},{10,11... | collective-permute-start | bytes 1327112 | tf_op jit(solution)/shard_map/ppermute | solution.py:130
  111.2 1.4 collective-permute-done
  112.6 0.1 fusion
  112.7 15.9 %all_to_all.16 = bf16[4,27,16,128]{3,2,1,0:T(8,128)(2,1)S(1)} all-to-all(bf16[4,27,16,128]{3,2,1,0:T(8,128)(2,1)S(1)} %fusion), channel_id=1, replica_groups=mesh['z'=8,'yh'=2,'x'=4,'yl'=4,'core'=2] {'yl'}, dimensions={0} | all-to-all | bytes 884736 | tf_op jit(solution)/shard_map/all_to_all | solution.py:132
  128.7 0.1 convert_reduce_fusion
  128.7 3.0 %collective-permute-start.1 = (bf16[27,8,128]{2,1,0:T(8,128)(2,1)S(1)}, bf16[27,8,128]{2,1,0:T(8,128)(2,1)S(1)}, u32[]{:S(2)}, u32[]{:S(2)}) collective-permute-start(bf16[27,8,128]{2,1,0:T(8,128)(2,1)S(1)} %slice.63), channel_id=1, source_target_pairs={{0,8},{8,16},{16,24},{24,32},{32,40},{40,48},{48,56},{56,64},{64,7... | collective-permute-start | bytes 165896 | tf_op jit(solution)/shard_map/ppermute | solution.py:135
  131.8 10.6 %collective-permute-done.1 = bf16[27,8,128]{2,1,0:T(8,128)(2,1)S(1)} collective-permute-done((bf16[27,8,128]{2,1,0:T(8,128)(2,1)S(1)}, bf16[27,8,128]{2,1,0:T(8,128)(2,1)S(1)}, u32[]{:S(2)}, u32[]{:S(2)}) %collective-permute-start.1) | collective-permute-done | bytes 55328 | tf_op jit(solution)/shard_map/ppermute | solution.py:135
  142.4 0.1 slice_bitcast_fusion.3
  142.5 0.7 pad_maximum_fusion
  (6 shorter events, 0.1 us)
Async XLA Ops:
  6.5 87.9 %all-gather.3.cloned.1.call-start = ((), (), s32[]{:S(2)}) async-start(), calls=%async_computation.3 | async-start | bytes 4718592 | tf_op jit(solution)/shard_map/all_gather | solution.py:110
  32.9 23.0 %all-to-all-start.1 = ((bf16[8,4,64,128]{3,2,1,0:T(8,128)(2,1)}), bf16[8,4,64,128]{3,2,1,0:T(8,128)(2,1)S(1)}, u32[]{:S(2)}, u32[]{:S(2)}) async-start(bf16[8,4,64,128]{3,2,1,0:T(8,128)(2,1)} %broadcast_in_dim.59), calls=%async_computation.1 | async-start | bytes 1048576 | tf_op jit(solution)/shard_map/all_to_all | solution.py:22
  55.8 2.8 %copy-start.2 = (bf16[64,6,64,64]{3,2,1,0:T(8,128)(2,1)S(1)}, bf16[64,6,64,64]{3,2,1,0:T(8,128)(2,1)}, u32[]{:S(2)}) copy-start(bf16[64,6,64,64]{3,2,1,0:T(8,128)(2,1)} %param.6) | copy-start | bytes 9437188
  62.0 2.7 %copy-start = (bf16[2,4,8,6,64,64]{5,4,3,2,1,0:T(8,128)(2,1)}, bf16[2,4,8,6,64,64]{5,4,3,2,1,0:T(8,128)(2,1)S(1)}, u32[]{:S(2)}) copy-start(bf16[2,4,8,6,64,64]{5,4,3,2,1,0:T(8,128)(2,1)S(1)} %left_products.1) | copy-start | bytes 9437188
  94.4 2.8 %copy-start.1 = (bf16[2,4,8,6,64,64]{5,4,3,2,1,0:T(8,128)(2,1)S(1)}, bf16[2,4,8,6,64,64]{5,4,3,2,1,0:T(8,128)(2,1)}, u32[]{:S(2)}) copy-start(bf16[2,4,8,6,64,64]{5,4,3,2,1,0:T(8,128)(2,1)} %copy-done) | copy-start | bytes 9437188
  97.2 2.2 %copy-start.3 = (bf16[64,4,64,128]{3,2,1,0:T(8,128)(2,1)S(1)}, bf16[64,4,64,128]{3,2,1,0:T(8,128)(2,1)}, u32[]{:S(2)}) copy-start(bf16[64,4,64,128]{3,2,1,0:T(8,128)(2,1)} %all-gather.3.cloned.1.call-done) | copy-start | bytes 12582916
  108.1 4.5 %collective-permute-start = (bf16[4,27,16,128]{3,2,1,0:T(8,128)(2,1)S(1)}, bf16[4,27,16,128]{3,2,1,0:T(8,128)(2,1)S(1)}, u32[]{:S(2)}, u32[]{:S(2)}) collective-permute-start(bf16[4,27,16,128]{3,2,1,0:T(8,128)(2,1)S(1)} %slice_bitcast_fusion), channel_id=1, source_target_pairs={{0,1},{1,0},{2,3},{3,2},{4,5},{5,4},{6,7},{7,6},{8,9},{9,8},{10,11... | collective-permute-start | bytes 1327112 | tf_op jit(solution)/shard_map/ppermute | solution.py:130
  128.7 13.6 %collective-permute-start.1 = (bf16[27,8,128]{2,1,0:T(8,128)(2,1)S(1)}, bf16[27,8,128]{2,1,0:T(8,128)(2,1)S(1)}, u32[]{:S(2)}, u32[]{:S(2)}) collective-permute-start(bf16[27,8,128]{2,1,0:T(8,128)(2,1)S(1)} %slice.63), channel_id=1, source_target_pairs={{0,8},{8,16},{16,24},{24,32},{32,40},{40,48},{48,56},{56,64},{64,7... | collective-permute-start | bytes 165896 | tf_op jit(solution)/shard_map/ppermute | solution.py:135
Sparse Core Ops, SparseCore 0:
  33.0 61.3 all-gather.2

commit v2 on v1

v2 whole, which is shorter than its diff:
```python
import functools

import jax
import jax.numpy as jnp
from jax import lax
from jax.experimental import pallas as pl
from jax.experimental.pallas import tpu as pltpu
from jax.sharding import Mesh, PartitionSpec as P

KC = 27
KP = 28
CR = 2
T = 64
NY = 4
HALF = CR * KC
ROW = ("z", "yh", "x")
COL = ("yl", "core")
UNROLL = 8
F32 = jnp.float32
BF16 = jnp.bfloat16
I32 = jnp.int32
MIB = 2**20


def shifted(value, axis, by):
    count = lax.axis_size(axis)
    return lax.ppermute(value, axis, [(i, (i + by) % count) for i in range(count)])


def spread(value, axis):
    count = lax.axis_size(axis)
    copies = jnp.broadcast_to(value[None], (count,) + value.shape)
    return lax.all_to_all(copies, axis, 0, 0, tiled=True)


def left_kernel(info_ref, own_ref, a_ref, b_ref):
    core = info_ref[8]
    for c in range(8):
        both = own_ref[c // 2, jnp.bitwise_xor(core, c % 2), 0].astype(F32).T.astype(BF16)
        for h in range(2):
            left = both[h * T:(h + 1) * T]
            for s in range(a_ref.shape[3]):
                b_ref[h, 0, c, s] = jnp.dot(left, a_ref[h, 0, c, s], preferred_element_type=F32).astype(BF16)


def left_products(info, own, a_tiles):
    rows, slots = a_tiles.shape[:2]
    a = a_tiles.reshape(2, 4, 8, slots, T, T)
    b = pl.pallas_call(
        left_kernel,
        grid=(4,),
        in_specs=[
            pl.BlockSpec(memory_space=pltpu.SMEM),
            pl.BlockSpec((4, 2, 1, T, 2 * T), lambda v: (0, 0, v, 0, 0)),
            pl.BlockSpec((2, 1, 8, slots, T, T), lambda v: (0, v, 0, 0, 0, 0)),
        ],
        out_specs=pl.BlockSpec((2, 1, 8, slots, T, T), lambda v: (0, v, 0, 0, 0, 0)),
        out_shape=jax.ShapeDtypeStruct(a.shape, BF16),
        compiler_params=pltpu.CompilerParams(vmem_limit_bytes=16 * MIB),
        cost_estimate=pl.CostEstimate(flops=2 * rows * slots * T**3, bytes_accessed=16 * MIB, transcendentals=0),
        name="left_products",
    )(info, own, a)
    return b.reshape(rows * slots, T, T)


def sum_kernel(group, sides, n_chunks, n_before, *refs):
    code_ref, info_ref = refs[:2]
    chunks = refs[2:2 + n_chunks]
    b_ref = refs[2 + n_chunks]
    before = refs[3 + n_chunks:3 + n_chunks + n_before * len(sides)]
    outs = refs[3 + n_chunks + n_before * len(sides):-3]
    panel, acc, sems = refs[-3:]
    core = info_ref[8]
    copies, at = [], 0
    for n, chunk in enumerate(chunks):
        size = chunk.shape[0]
        copies.append(pltpu.make_async_copy(chunk, panel.at[pl.ds(at, size)], sems.at[n]))
        at += size
    for copy in copies:
        copy.start()

    @pl.loop(0, acc.shape[0] // 2)
    def _(d):
        for e in range(2):
            acc[2 * d + e] = jnp.zeros((T, 2 * T), F32)

    for copy in copies:
        copy.wait()
    first = info_ref[group]

    @pl.loop(0, info_ref[4 + group])
    def _(step):
        for half in range(2):
            base = first + step * UNROLL + half * (UNROLL // 2)
            codes = [code_ref[base + e] for e in range(UNROLL // 2)]
            terms = [
                jnp.dot(
                    b_ref[jnp.bitwise_and(code, 511)],
                    panel[jnp.bitwise_and(jnp.right_shift(code, 9), 127)],
                    preferred_element_type=F32,
                )
                for code in codes
            ]
            for code, term in zip(codes, terms):
                d = jnp.right_shift(code, 16)
                acc[d] = acc[d] + term

    low = lax.broadcasted_iota(I32, (T, 2 * T), 1) < T

    @pl.loop(0, KP // 2)
    def _(m):
        for n in range(len(sides)):
            values = []
            for e in range(2):
                d0 = 2 * (n * HALF + 2 * m + e)
                d1 = d0 + 2 * KC
                values.append(
                    jnp.where(low, acc[d0], acc[d1 + 1]) + pltpu.roll(jnp.where(low, acc[d1], acc[d0 + 1]), T, 1)
                )
            for o in range(8):
                tile = jnp.concatenate([v[o * 8:(o + 1) * 8] for v in values], axis=0)
                place = (jnp.bitwise_xor(core, o % 2), o // 2, m)
                for q in range(n_before):
                    tile = tile + before[q * len(sides) + n][place].astype(F32)
                outs[n][place] = tile.astype(BF16)


def panel_sums(group, sides, code, info, chunks, b, before=()):
    smem = pl.BlockSpec(memory_space=pltpu.SMEM)
    vmem = pl.BlockSpec(memory_space=pltpu.VMEM)
    anyw = pl.BlockSpec(memory_space=pl.ANY)
    n = len(sides)
    shape = jax.ShapeDtypeStruct((2, NY, KP // 2, 16, 2 * T), BF16)
    pairs = sum(c.shape[0] for c in chunks)
    return pl.pallas_call(
        functools.partial(sum_kernel, group, sides, len(chunks), len(before) // n),
        in_specs=[smem, smem] + [anyw] * len(chunks) + [vmem] * (1 + len(before)),
        out_specs=[vmem] * n,
        out_shape=[shape] * n,
        scratch_shapes=[
            pltpu.VMEM((pairs, T, 2 * T), BF16),
            pltpu.VMEM((2 * (n * HALF + 1), T, 2 * T), F32),
            pltpu.SemaphoreType.DMA((len(chunks),)),
        ],
        compiler_params=pltpu.CompilerParams(vmem_limit_bytes=24 * MIB),
        cost_estimate=pl.CostEstimate(flops=pairs * 2**20, bytes_accessed=8 * MIB, transcendentals=0),
        name=f"panel_sums_{group}",
    )(code, info, *chunks, b, *before)


def body(a_tiles, a_cols, a_count, a_slot, agg, p_tiles):
    rows, slots = a_tiles.shape[:2]
    total = rows * slots
    core, me_x = lax.axis_index("core"), lax.axis_index("x")
    packed = jnp.concatenate([p_tiles[0, :4], p_tiles[0, 4:]], axis=-1)

    column = spread(packed, ("yh", "z")).reshape(-1, T, 2 * T)
    half = column.shape[0] // 2
    left1, right1 = shifted(column, "x", 1), shifted(column, "x", -1)

    both = jnp.stack([packed, shifted(packed, "core", 1)])
    both, _ = lax.optimization_barrier((both, column))
    own = spread(both, "yl")
    left1, right1, own = lax.optimization_barrier((left1, right1, own))
    left2, right2 = shifted(left1[:half], "x", 1), shifted(right1[half:], "x", -1)

    live = jnp.arange(slots, dtype=I32)[None, :] < a_count
    owner = a_cols // 8
    far = jnp.bitwise_and(owner - me_x + 4, 3)
    pair = ((owner // 4) % 2 * 8 + owner // 8) * 4 + a_cols % 4 + jnp.where(far == 1, 64, 0)
    side = jnp.broadcast_to(agg[:, None] // CR, a_cols.shape)
    group = jnp.where(far == 0, 0, jnp.where(far == 2, 3 - side, 1))
    target = 2 * (agg[:, None] * KC + a_slot) + (a_cols % 8) // 4
    target = jnp.where((group == 2), target - 2 * HALF, target)
    code = jnp.left_shift(target, 16) + jnp.left_shift(pair, 9) + jnp.arange(total, dtype=I32).reshape(rows, slots)
    code = code.reshape(total)
    picked = (group.reshape(total)[:, None] == jnp.arange(4, dtype=I32)) & live.reshape(total)[:, None]
    lower = jnp.arange(total, dtype=I32)[:, None] > jnp.arange(total, dtype=I32)[None, :]
    rank = jnp.dot(lower.astype(BF16), picked.astype(BF16), preferred_element_type=F32).astype(I32)
    steps = (jnp.sum(picked.astype(I32), axis=0) + UNROLL - 1) // UNROLL
    first = (jnp.cumsum(steps) - steps) * UNROLL
    place = jnp.sum(jnp.where(picked, rank + first[None, :] + 1, 0), axis=1) - 1
    spots = jnp.arange(total + 4 * UNROLL, dtype=I32)
    here = spots[:, None] == place[None, :]
    empty = jnp.left_shift(jnp.where(spots < first[2], 4 * HALF, 2 * HALF), 16)
    code = jnp.where(jnp.any(here, axis=1), jnp.sum(jnp.where(here, code[None, :], 0), axis=1), empty)
    info = jnp.concatenate([first, steps, core[None]]).astype(I32)

    b = left_products(info, own, a_tiles)
    sums0 = panel_sums(0, (0, 1), code, info, [column], b)
    sums1 = panel_sums(1, (0, 1), code, info, [left1, right1], b)
    (next2,) = panel_sums(2, (1,), code, info, [left2, right2], b, (sums0[1], sums1[1]))
    (own2,) = panel_sums(3, (0,), code, info, [left2, right2], b, (sums0[0], sums1[0]))

    def over_col(value):
        other = shifted(value[1], "core", 1)
        chip = (value[0].astype(F32) + other.astype(F32)).astype(BF16)
        return jnp.sum(lax.all_to_all(chip, "yl", 0, 0, tiled=True).astype(F32), axis=0)

    moved = shifted(over_col(next2).astype(BF16), ROW, 1)
    result = (over_col(own2) + moved.astype(F32)).reshape(KP, 8, 2 * T)[:KC]
    return jnp.stack([result[..., :T], result[..., T:]])


def solution(mesh):
    fine = Mesh(mesh.devices.reshape(8, 2, 4, 4, 2), ROW + COL)
    return jax.shard_map(
        body,
        mesh=fine,
        in_specs=(
            P(ROW, COL, None, None),
            P(ROW, COL),
            P(ROW, COL),
            P(ROW, COL),
            P(ROW),
            P(COL, ROW, None, None),
        ),
        out_specs=P(ROW, None, COL, None),
        check_vma=False,
    )
```

time: 151 us -> 151 us (level)
  starting transfers between devices: 14.5 us -> 63.1 us
  blocking collectives: 40.3 us -> 0 us
  between operations: 14.2 us -> 0.25 us
  Pallas kernels: 12 us -> 21.3 us
  local copies, waits for them, and re-layouts: 13.9 us -> 8.78 us
  other arithmetic: 3.98 us -> 6.01 us
  waiting for transfers between devices: 51.1 us -> 49.2 us
    all_to_all x2 -> x0, blocking collectives: 40.3 us -> none  [the longest x1 24.4 us: spread(): return lax.all_to_all(copies, axis, 0, 0, tiled=True)]
    all_gather x1 -> x0, waiting for transfers between devices: 29.7 us -> none  [body(): panel = lax.all_gather(near, 'z', axis=0, tiled=False).reshape(-1, T, 2 * T)]
    all_to_all x1 -> x2, waiting for transfers between devices: 9.39 us -> 32 us  [spread(): return lax.all_to_all(copies, axis, 0, 0, tiled=True)]
    all_to_all x1 -> x2, starting transfers between devices: 8.36 us -> 27.8 us  [spread(): return lax.all_to_all(copies, axis, 0, 0, tiled=True)]
    ppermute x2 -> x8, starting transfers between devices: 6.16 us -> 23.8 us  [shifted(): lax.ppermute(value, axis, [(i, (i + by) % count) for i in range(count)])]
    all_to_all x0 -> x2, starting transfers between devices: none -> 11.5 us  [over_col(): lax.all_to_all(chip, 'yl', 0, 0, tiled=True).astype(F32)]
    all_to_all x0 -> x2, waiting for transfers between devices: none -> 9.68 us  [over_col(): lax.all_to_all(chip, 'yl', 0, 0, tiled=True).astype(F32)]
    pallas_call x2 -> x5, Pallas kernels: 12 us -> 21.3 us  [the longest x4 17.1 us: panel_sums(): pl.pallas_call(functools.partial(sum_kernel, group, sides, len(chunks), l...]
  transfers between devices with their start and end apart: 4 -> 12, of which waited for: 4 -> 5; matrix products, arithmetic and copies ran while one was open for 3% -> 6% of each run, Pallas kernels for 2% -> 12%
where the time goes in v2:
time: 151 us; the launch traced here: 149 us
  starting transfers between devices  63.1 us (42%)
  waiting for transfers between devices  49.2 us (33%)
  Pallas kernels  21.3 us (14%)
  local copies, waits for them, and re-layouts  8.78 us (6%)
  other arithmetic  6.01 us (4%)
    all_to_all x2, waiting for transfers between devices, spread(): return lax.all_to_all(copies, axis, 0, 0, tiled=True)  32 us
    all_to_all x2, starting transfers between devices, spread(): return lax.all_to_all(copies, axis, 0, 0, tiled=True)  27.8 us
    ppermute x8, starting transfers between devices, shifted(): lax.ppermute(value, axis, [(i, (i + by) % count) for i in range(count)])  23.8 us
    pallas_call x4, Pallas kernels, panel_sums(): pl.pallas_call(functools.partial(sum_kernel, group, sides, len(chunks), l...  17.1 us
    all_to_all x2, starting transfers between devices, over_col(): lax.all_to_all(chip, 'yl', 0, 0, tiled=True).astype(F32)  11.5 us
    all_to_all x2, waiting for transfers between devices, over_col(): lax.all_to_all(chip, 'yl', 0, 0, tiled=True).astype(F32)  9.68 us
    ppermute x8, waiting for transfers between devices, shifted(): lax.ppermute(value, axis, [(i, (i + by) % count) for i in range(count)])  7.52 us
    pallas_call x1, Pallas kernels, left_products(): pl.pallas_call(left_kernel, grid=(4,), in_specs=[pl.BlockSpec(memory_spac...  4.16 us
  transfers between devices with their start and end apart: 12, of which 5 were waited for; matrix products, arithmetic and copies ran while one was open for 6% of the time, Pallas kernels for 12%

profile of v2, /device:TPU:1, one launch (start us, length us, event | category | flops | bytes accessed | tf_op | source)
XLA Modules:
  0.0 148.9 jit_solution(756837563507636533)
XLA Ops:
  0.0 0.9 slice_bitcast_fusion.7
  0.9 0.1 pad_maximum_fusion.2
  1.0 1.2 broadcast_in_dim.76
  2.2 16.2 %all-to-all-start = ((bf16[16,4,64,128]{3,2,1,0:T(8,128)(2,1)}), bf16[16,4,64,128]{3,2,1,0:T(8,128)(2,1)S(1)}, u32[]{:S(2)}, u32[]{:S(2)}) async-start(bf16[16,4,64,128]{3,2,1,0:T(8,128)(2,1)} %broadcast_in_dim.76), calls=%async_computation | async-start | bytes 2097152 | tf_op jit(solution)/shard_map/all_to_all | solution.py:33
  18.4 2.9 %collective-permute-start.2 = (bf16[4,64,128]{2,1,0:T(8,128)(2,1)S(1)}, bf16[4,64,128]{2,1,0:T(8,128)(2,1)S(1)}, u32[]{:S(2)}, u32[]{:S(2)}) collective-permute-start(bf16[4,64,128]{2,1,0:T(8,128)(2,1)S(1)} %pad_maximum_fusion.2), channel_id=1, source_target_pairs={{0,1},{1,0},{2,3},{3,2},{4,5},{5,4},{6,7},{7,6},{8,9},{9,8},{10,11... | collective-permute-start | bytes 196616 | tf_op jit(solution)/shard_map/ppermute | solution.py:27
  21.3 0.7 broadcast_multiply_fusion
  22.0 0.7 iota_compare_fusion.3
  22.7 0.7 fusion.12
  23.5 18.4 %all-to-all-done = bf16[16,4,64,128]{3,2,1,0:T(8,128)(2,1)S(1)} async-done(((bf16[16,4,64,128]{3,2,1,0:T(8,128)(2,1)}), bf16[16,4,64,128]{3,2,1,0:T(8,128)(2,1)S(1)}, u32[]{:S(2)}, u32[]{:S(2)}) %all-to-all-start) | async-done | bytes 1048608 | tf_op jit(solution)/shard_map/all_to_all | solution.py:33
  41.8 3.1 %collective-permute-start = (bf16[64,64,128]{2,1,0:T(8,128)(2,1)S(1)}, bf16[64,64,128]{2,1,0:T(8,128)(2,1)S(1)}, u32[]{:S(2)}, u32[]{:S(2)}) collective-permute-start(bf16[64,64,128]{2,1,0:T(8,128)(2,1)S(1)} %bitcast.49), channel_id=1, source_target_pairs={{0,8},{8,16},{16,24},{24,0},{1,9},{9,17},{17,25},{25,1},{2,10},{10... | collective-permute-start | bytes 3145736 | tf_op jit(solution)/shard_map/ppermute | solution.py:27
  45.0 3.4 %collective-permute-start.1 = (bf16[64,64,128]{2,1,0:T(8,128)(2,1)S(1)}, bf16[64,64,128]{2,1,0:T(8,128)(2,1)S(1)}, u32[]{:S(2)}, u32[]{:S(2)}) collective-permute-start(bf16[64,64,128]{2,1,0:T(8,128)(2,1)S(1)} %bitcast.50), channel_id=1, source_target_pairs={{0,24},{8,0},{16,8},{24,16},{1,25},{9,1},{17,9},{25,17},{2,26},{10... | collective-permute-start | bytes 3145736 | tf_op jit(solution)/shard_map/ppermute | solution.py:27
  48.3 0.1 fusion.32
  48.4 0.1 copy.9
  48.5 0.1 eq.49
  48.7 0.1 lt.46
  48.8 0.1 convert_reduce_fusion.1
  49.0 0.9 broadcast_in_dim.78
  49.9 11.6 %all-to-all-start.1 = ((bf16[4,2,4,64,128]{4,3,2,1,0:T(8,128)(2,1)}), bf16[4,2,4,64,128]{4,3,2,1,0:T(8,128)(2,1)}, u32[]{:S(2)}, u32[]{:S(2)}) async-start(bf16[4,2,4,64,128]{4,3,2,1,0:T(8,128)(2,1)} %broadcast_in_dim.78), calls=%async_computation.1 | async-start | bytes 1048576 | tf_op jit(solution)/shard_map/all_to_all | solution.py:33
  61.5 0.2 reduce-window.7
  61.7 0.2 fusion.3
  61.9 13.7 %all-to-all-done.1.own_ref = bf16[4,2,4,64,128]{4,3,2,1,0:T(8,128)(2,1)} async-done(((bf16[4,2,4,64,128]{4,3,2,1,0:T(8,128)(2,1)}), bf16[4,2,4,64,128]{4,3,2,1,0:T(8,128)(2,1)}, u32[]{:S(2)}, u32[]{:S(2)}) %all-to-all-start.1) | async-done | bytes 524320 | tf_op jit(solution)/shard_map/all_to_all | solution.py:33
  75.5 0.8 slice.39
  76.4 1.9 %collective-permute-start.3 = (bf16[32,64,128]{2,1,0:T(8,128)(2,1)}, bf16[32,64,128]{2,1,0:T(8,128)(2,1)}, u32[]{:S(2)}, u32[]{:S(2)}) collective-permute-start(bf16[32,64,128]{2,1,0:T(8,128)(2,1)} %slice.39), channel_id=1, source_target_pairs={{0,8},{8,16},{16,24},{24,0},{1,9},{9,17},{17,25},{25,1},{2,10},{10... | collective-permute-start | bytes 1572872 | tf_op jit(solution)/shard_map/ppermute | solution.py:27
  78.3 0.8 slice.40
  79.1 4.6 %collective-permute-start.4 = (bf16[32,64,128]{2,1,0:T(8,128)(2,1)}, bf16[32,64,128]{2,1,0:T(8,128)(2,1)}, u32[]{:S(2)}, u32[]{:S(2)}) collective-permute-start(bf16[32,64,128]{2,1,0:T(8,128)(2,1)} %slice.40), channel_id=1, source_target_pairs={{0,24},{8,0},{16,8},{24,16},{1,25},{9,1},{17,9},{25,17},{2,26},{10... | collective-permute-start | bytes 1572872 | tf_op jit(solution)/shard_map/ppermute | solution.py:27
  83.8 0.6 slice.36
  84.4 0.1 copy.10
  84.5 0.1 broadcast_in_dim.70
  84.6 0.2 fusion.4
  84.8 0.2 select_reduce_fusion
  84.9 0.7 shift-left_select_fusion.refs_0_
  85.6 2.8 %copy-done = bf16[64,6,64,64]{3,2,1,0:T(8,128)(2,1)S(1)} copy-done((bf16[64,6,64,64]{3,2,1,0:T(8,128)(2,1)S(1)}, bf16[64,6,64,64]{3,2,1,0:T(8,128)(2,1)}, u32[]{:S(2)}) %copy-start) | copy-done | bytes 3145752
  88.4 4.2 %left_products.1 = bf16[2,4,8,6,64,64]{5,4,3,2,1,0:T(8,128)(2,1)S(1)} custom-call(s32[9]{0:T(128)S(1)} %pad_add_fusion.info_ref.refs_1_, bf16[4,2,4,64,128]{4,3,2,1,0:T(8,128)(2,1)} %all-to-all-done.1.own_ref, bf16[2,4,8,6,64,64]{5,4,3,2,1,0:T(8,128)(2,1)S(1)} %bitcast.48), custom_call_target="tpu_custom_call" | custom-call | flops 201326592 | bytes 16777216 | tf_op jit(solution)/shard_map/left_products/pallas_call | solution.py:49
  92.6 4.2 %panel_sums_0.1 = (bf16[2,4,14,16,128]{4,3,2,1,0:T(8,128)(2,1)S(1)}, bf16[2,4,14,16,128]{4,3,2,1,0:T(8,128)(2,1)S(1)}) custom-call(s32[416]{0:T(512)S(1)} %shift-left_select_fusion.refs_0_, s32[9]{0:T(128)S(1)} %pad_add_fusion.info_ref.refs_1_, bf16[64,64,128]{2,1,0:T(8,128)(2,1)S(1)} %bitcast.51, bf16[384,64,64]{2,1,0:T(8,128)(2,1)S(1)} %bitcast.44), custom_call_target="tpu_custom_call" | custom-call | flops 67108864 | bytes 8388608 | tf_op jit(solution)/shard_map/panel_sums_0/pallas_call | solution.py:135
  96.7 5.2 %panel_sums_1.1 = (bf16[2,4,14,16,128]{4,3,2,1,0:T(8,128)(2,1)S(1)}, bf16[2,4,14,16,128]{4,3,2,1,0:T(8,128)(2,1)S(1)}) custom-call(s32[416]{0:T(512)S(1)} %shift-left_select_fusion.refs_0_, s32[9]{0:T(128)S(1)} %pad_add_fusion.info_ref.refs_1_, bf16[64,64,128]{2,1,0:T(8,128)(2,1)S(1)} %collective-permute-done.refs_2_, ...), custom_call_target="tpu_custom_call" | custom-call | flops 134217728 | bytes 8388608 | tf_op jit(solution)/shard_map/panel_sums_1/pallas_call | solution.py:135
  101.9 4.0 %panel_sums_2.1 = bf16[2,4,14,16,128]{4,3,2,1,0:T(8,128)(2,1)S(1)} custom-call(s32[416]{0:T(512)S(1)} %shift-left_select_fusion.refs_0_, s32[9]{0:T(128)S(1)} %pad_add_fusion.info_ref.refs_1_, bf16[32,64,128]{2,1,0:T(8,128)(2,1)} %collective-permute-done.3.refs_2_, bf16[32,64,128]{2,1,0:T(8,128)(2,1)} %collective-permute-done.4.refs_3_, ...), custom_call_target="tpu_custom_call" | custom-call | flops 67108864 | bytes 8388608 | tf_op jit(solution)/shard_map/panel_sums_2/pallas_call | solution.py:135
  105.9 4.1 %collective-permute-start.6 = (bf16[4,14,16,128]{3,2,1,0:T(8,128)(2,1)S(1)}, bf16[4,14,16,128]{3,2,1,0:T(8,128)(2,1)S(1)}, u32[]{:S(2)}, u32[]{:S(2)}) collective-permute-start(bf16[4,14,16,128]{3,2,1,0:T(8,128)(2,1)S(1)} %slice_bitcast_fusion), channel_id=1, source_target_pairs={{0,1},{1,0},{2,3},{3,2},{4,5},{5,4},{6,7},{7,6},{8,9},{9,8},{10,11... | collective-permute-start | bytes 688136 | tf_op jit(solution)/shard_map/ppermute | solution.py:27
  110.1 3.8 %panel_sums_3.1 = bf16[2,4,14,16,128]{4,3,2,1,0:T(8,128)(2,1)S(1)} custom-call(s32[416]{0:T(512)S(1)} %shift-left_select_fusion.refs_0_, s32[9]{0:T(128)S(1)} %pad_add_fusion.info_ref.refs_1_, bf16[32,64,128]{2,1,0:T(8,128)(2,1)} %collective-permute-done.3.refs_2_, bf16[32,64,128]{2,1,0:T(8,128)(2,1)} %collective-permute-done.4.refs_3_, ...), custom_call_target="tpu_custom_call" | custom-call | flops 67108864 | bytes 8388608 | tf_op jit(solution)/shard_map/panel_sums_3/pallas_call | solution.py:135
  113.9 1.9 %collective-permute-start.5 = (bf16[4,14,16,128]{3,2,1,0:T(8,128)(2,1)S(1)}, bf16[4,14,16,128]{3,2,1,0:T(8,128)(2,1)S(1)}, u32[]{:S(2)}, u32[]{:S(2)}) collective-permute-start(bf16[4,14,16,128]{3,2,1,0:T(8,128)(2,1)S(1)} %slice_bitcast_fusion.2), channel_id=1, source_target_pairs={{0,1},{1,0},{2,3},{3,2},{4,5},{5,4},{6,7},{7,6},{8,9},{9,8},{10,11... | collective-permute-start | bytes 688136 | tf_op jit(solution)/shard_map/ppermute | solution.py:27
  115.8 0.8 fusion.5
  116.6 6.8 %all-to-all-start.3 = ((bf16[4,14,16,128]{3,2,1,0:T(8,128)(2,1)}), bf16[4,14,16,128]{3,2,1,0:T(8,128)(2,1)S(1)}, u32[]{:S(2)}, u32[]{:S(2)}) async-start(bf16[4,14,16,128]{3,2,1,0:T(8,128)(2,1)} %fusion.5), calls=%async_computation.3 | async-start | bytes 458752 | tf_op jit(solution)/shard_map/all_to_all | solution.py:198
  123.4 0.7 fusion.6
  124.1 6.1 %all-to-all-done.3 = bf16[4,14,16,128]{3,2,1,0:T(8,128)(2,1)S(1)} async-done(((bf16[4,14,16,128]{3,2,1,0:T(8,128)(2,1)}), bf16[4,14,16,128]{3,2,1,0:T(8,128)(2,1)S(1)}, u32[]{:S(2)}, u32[]{:S(2)}) %all-to-all-start.3) | async-done | bytes 229408 | tf_op jit(solution)/shard_map/all_to_all | solution.py:198
  130.2 4.7 %all-to-all-start.2 = ((bf16[4,14,16,128]{3,2,1,0:T(8,128)(2,1)}), bf16[4,14,16,128]{3,2,1,0:T(8,128)(2,1)S(1)}, u32[]{:S(2)}, u32[]{:S(2)}) async-start(bf16[4,14,16,128]{3,2,1,0:T(8,128)(2,1)} %fusion.6), calls=%async_computation.2 | async-start | bytes 458752 | tf_op jit(solution)/shard_map/all_to_all | solution.py:198
  135.0 1.9 %collective-permute-start.7 = (bf16[14,16,128]{2,1,0:T(8,128)(2,1)S(1)}, bf16[14,16,128]{2,1,0:T(8,128)(2,1)S(1)}, u32[]{:S(2)}, u32[]{:S(2)}) collective-permute-start(bf16[14,16,128]{2,1,0:T(8,128)(2,1)S(1)} %reduce_sum.52), channel_id=1, source_target_pairs={{0,8},{8,16},{16,24},{24,32},{32,40},{40,48},{48,56},{56,64},{64,7... | collective-permute-start | bytes 172040 | tf_op jit(solution)/shard_map/ppermute | solution.py:27
  136.9 3.6 %all-to-all-done.2 = bf16[4,14,16,128]{3,2,1,0:T(8,128)(2,1)S(1)} async-done(((bf16[4,14,16,128]{3,2,1,0:T(8,128)(2,1)}), bf16[4,14,16,128]{3,2,1,0:T(8,128)(2,1)S(1)}, u32[]{:S(2)}, u32[]{:S(2)}) %all-to-all-start.2) | async-done | bytes 229408 | tf_op jit(solution)/shard_map/all_to_all | solution.py:198
  140.5 7.5 %collective-permute-done.7 = bf16[14,16,128]{2,1,0:T(8,128)(2,1)S(1)} collective-permute-done((bf16[14,16,128]{2,1,0:T(8,128)(2,1)S(1)}, bf16[14,16,128]{2,1,0:T(8,128)(2,1)S(1)}, u32[]{:S(2)}, u32[]{:S(2)}) %collective-permute-start.7) | collective-permute-done | bytes 57376 | tf_op jit(solution)/shard_map/ppermute | solution.py:27
  148.2 0.7 pad_maximum_fusion
  (19 shorter events, 0.3 us)
Async XLA Ops:
  2.2 39.6 %all-to-all-start = ((bf16[16,4,64,128]{3,2,1,0:T(8,128)(2,1)}), bf16[16,4,64,128]{3,2,1,0:T(8,128)(2,1)S(1)}, u32[]{:S(2)}, u32[]{:S(2)}) async-start(bf16[16,4,64,128]{3,2,1,0:T(8,128)(2,1)} %broadcast_in_dim.76), calls=%async_computation | async-start | bytes 2097152 | tf_op jit(solution)/shard_map/all_to_all | solution.py:33
  18.4 30.5 %collective-permute-start.2 = (bf16[4,64,128]{2,1,0:T(8,128)(2,1)S(1)}, bf16[4,64,128]{2,1,0:T(8,128)(2,1)S(1)}, u32[]{:S(2)}, u32[]{:S(2)}) collective-permute-start(bf16[4,64,128]{2,1,0:T(8,128)(2,1)S(1)} %pad_maximum_fusion.2), channel_id=1, source_target_pairs={{0,1},{1,0},{2,3},{3,2},{4,5},{5,4},{6,7},{7,6},{8,9},{9,8},{10,11... | collective-permute-start | bytes 196616 | tf_op jit(solution)/shard_map/ppermute | solution.py:27
  41.8 33.7 %collective-permute-start = (bf16[64,64,128]{2,1,0:T(8,128)(2,1)S(1)}, bf16[64,64,128]{2,1,0:T(8,128)(2,1)S(1)}, u32[]{:S(2)}, u32[]{:S(2)}) collective-permute-start(bf16[64,64,128]{2,1,0:T(8,128)(2,1)S(1)} %bitcast.49), channel_id=1, source_target_pairs={{0,8},{8,16},{16,24},{24,0},{1,9},{9,17},{17,25},{25,1},{2,10},{10... | collective-permute-start | bytes 3145736 | tf_op jit(solution)/shard_map/ppermute | solution.py:27
  45.0 30.6 %collective-permute-start.1 = (bf16[64,64,128]{2,1,0:T(8,128)(2,1)S(1)}, bf16[64,64,128]{2,1,0:T(8,128)(2,1)S(1)}, u32[]{:S(2)}, u32[]{:S(2)}) collective-permute-start(bf16[64,64,128]{2,1,0:T(8,128)(2,1)S(1)} %bitcast.50), channel_id=1, source_target_pairs={{0,24},{8,0},{16,8},{24,16},{1,25},{9,1},{17,9},{25,17},{2,26},{10... | collective-permute-start | bytes 3145736 | tf_op jit(solution)/shard_map/ppermute | solution.py:27
  49.9 25.7 %all-to-all-start.1 = ((bf16[4,2,4,64,128]{4,3,2,1,0:T(8,128)(2,1)}), bf16[4,2,4,64,128]{4,3,2,1,0:T(8,128)(2,1)}, u32[]{:S(2)}, u32[]{:S(2)}) async-start(bf16[4,2,4,64,128]{4,3,2,1,0:T(8,128)(2,1)} %broadcast_in_dim.78), calls=%async_computation.1 | async-start | bytes 1048576 | tf_op jit(solution)/shard_map/all_to_all | solution.py:33
  76.4 25.5 %collective-permute-start.3 = (bf16[32,64,128]{2,1,0:T(8,128)(2,1)}, bf16[32,64,128]{2,1,0:T(8,128)(2,1)}, u32[]{:S(2)}, u32[]{:S(2)}) collective-permute-start(bf16[32,64,128]{2,1,0:T(8,128)(2,1)} %slice.39), channel_id=1, source_target_pairs={{0,8},{8,16},{16,24},{24,0},{1,9},{9,17},{17,25},{25,1},{2,10},{10... | collective-permute-start | bytes 1572872 | tf_op jit(solution)/shard_map/ppermute | solution.py:27
  79.1 22.8 %collective-permute-start.4 = (bf16[32,64,128]{2,1,0:T(8,128)(2,1)}, bf16[32,64,128]{2,1,0:T(8,128)(2,1)}, u32[]{:S(2)}, u32[]{:S(2)}) collective-permute-start(bf16[32,64,128]{2,1,0:T(8,128)(2,1)} %slice.40), channel_id=1, source_target_pairs={{0,24},{8,0},{16,8},{24,16},{1,25},{9,1},{17,9},{25,17},{2,26},{10... | collective-permute-start | bytes 1572872 | tf_op jit(solution)/shard_map/ppermute | solution.py:27
  85.6 2.8 %copy-start = (bf16[64,6,64,64]{3,2,1,0:T(8,128)(2,1)S(1)}, bf16[64,6,64,64]{3,2,1,0:T(8,128)(2,1)}, u32[]{:S(2)}) copy-start(bf16[64,6,64,64]{3,2,1,0:T(8,128)(2,1)} %param.6) | copy-start | bytes 9437188
  105.9 9.9 %collective-permute-start.6 = (bf16[4,14,16,128]{3,2,1,0:T(8,128)(2,1)S(1)}, bf16[4,14,16,128]{3,2,1,0:T(8,128)(2,1)S(1)}, u32[]{:S(2)}, u32[]{:S(2)}) collective-permute-start(bf16[4,14,16,128]{3,2,1,0:T(8,128)(2,1)S(1)} %slice_bitcast_fusion), channel_id=1, source_target_pairs={{0,1},{1,0},{2,3},{3,2},{4,5},{5,4},{6,7},{7,6},{8,9},{9,8},{10,11... | collective-permute-start | bytes 688136 | tf_op jit(solution)/shard_map/ppermute | solution.py:27
  113.9 9.5 %collective-permute-start.5 = (bf16[4,14,16,128]{3,2,1,0:T(8,128)(2,1)S(1)}, bf16[4,14,16,128]{3,2,1,0:T(8,128)(2,1)S(1)}, u32[]{:S(2)}, u32[]{:S(2)}) collective-permute-start(bf16[4,14,16,128]{3,2,1,0:T(8,128)(2,1)S(1)} %slice_bitcast_fusion.2), channel_id=1, source_target_pairs={{0,1},{1,0},{2,3},{3,2},{4,5},{5,4},{6,7},{7,6},{8,9},{9,8},{10,11... | collective-permute-start | bytes 688136 | tf_op jit(solution)/shard_map/ppermute | solution.py:27
  116.6 13.6 %all-to-all-start.3 = ((bf16[4,14,16,128]{3,2,1,0:T(8,128)(2,1)}), bf16[4,14,16,128]{3,2,1,0:T(8,128)(2,1)S(1)}, u32[]{:S(2)}, u32[]{:S(2)}) async-start(bf16[4,14,16,128]{3,2,1,0:T(8,128)(2,1)} %fusion.5), calls=%async_computation.3 | async-start | bytes 458752 | tf_op jit(solution)/shard_map/all_to_all | solution.py:198
  130.2 10.3 %all-to-all-start.2 = ((bf16[4,14,16,128]{3,2,1,0:T(8,128)(2,1)}), bf16[4,14,16,128]{3,2,1,0:T(8,128)(2,1)S(1)}, u32[]{:S(2)}, u32[]{:S(2)}) async-start(bf16[4,14,16,128]{3,2,1,0:T(8,128)(2,1)} %fusion.6), calls=%async_computation.2 | async-start | bytes 458752 | tf_op jit(solution)/shard_map/all_to_all | solution.py:198
  135.0 13.1 %collective-permute-start.7 = (bf16[14,16,128]{2,1,0:T(8,128)(2,1)S(1)}, bf16[14,16,128]{2,1,0:T(8,128)(2,1)S(1)}, u32[]{:S(2)}, u32[]{:S(2)}) collective-permute-start(bf16[14,16,128]{2,1,0:T(8,128)(2,1)S(1)} %reduce_sum.52), channel_id=1, source_target_pairs={{0,8},{8,16},{16,24},{24,32},{32,40},{40,48},{48,56},{56,64},{64,7... | collective-permute-start | bytes 172040 | tf_op jit(solution)/shard_map/ppermute | solution.py:27

commit v3 on v2

v3 whole, which is shorter than its diff:
```python
import functools

import jax
import jax.numpy as jnp
from jax import lax
from jax.experimental import pallas as pl
from jax.experimental.pallas import tpu as pltpu
from jax.sharding import Mesh, PartitionSpec as P

KC = 27
CR = 2
T = 64
NY = 4
ROW = ("z", "yh", "x")
COL = ("yl", "core")
UNROLL = 8
F32 = jnp.float32
BF16 = jnp.bfloat16
I32 = jnp.int32
MIB = 2**20


def shifted(value, axis, by):
    count = lax.axis_size(axis)
    return lax.ppermute(value, axis, [(i, (i + by) % count) for i in range(count)])


def spread(value, axis):
    count = lax.axis_size(axis)
    copies = jnp.broadcast_to(value[None], (count,) + value.shape)
    return lax.all_to_all(copies, axis, 0, 0, tiled=True)


def left_kernel(info_ref, own_ref, a_ref, b_ref):
    core, yl = info_ref[6], info_ref[7]
    for c in range(8):
        far = jnp.bitwise_and(yl - c // 2 + NY, NY - 1)
        both = own_ref[jnp.bitwise_xor(core, c % 2), far, 0].astype(F32).T.astype(BF16)
        for h in range(2):
            left = both[h * T:(h + 1) * T]
            for s in range(a_ref.shape[3]):
                b_ref[h, 0, c, s] = jnp.dot(left, a_ref[h, 0, c, s], preferred_element_type=F32).astype(BF16)


def left_products(info, own, a_tiles):
    rows, slots = a_tiles.shape[:2]
    a = a_tiles.reshape(2, 4, 8, slots, T, T)
    b = pl.pallas_call(
        left_kernel,
        grid=(4,),
        in_specs=[
            pl.BlockSpec(memory_space=pltpu.SMEM),
            pl.BlockSpec((2, NY, 1, T, 2 * T), lambda v: (0, 0, v, 0, 0)),
            pl.BlockSpec((2, 1, 8, slots, T, T), lambda v: (0, v, 0, 0, 0, 0)),
        ],
        out_specs=pl.BlockSpec((2, 1, 8, slots, T, T), lambda v: (0, v, 0, 0, 0, 0)),
        out_shape=jax.ShapeDtypeStruct(a.shape, BF16),
        compiler_params=pltpu.CompilerParams(vmem_limit_bytes=16 * MIB),
        cost_estimate=pl.CostEstimate(flops=2 * rows * slots * T**3, bytes_accessed=16 * MIB, transcendentals=0),
        name="left_products",
    )(info, own, a)
    return b.reshape(rows * slots, T, T)


def sum_kernel(group, n_chunks, n_before, *refs):
    code_ref, info_ref = refs[:2]
    chunks = refs[2:2 + n_chunks]
    b_ref = refs[2 + n_chunks]
    before = refs[3 + n_chunks:3 + n_chunks + n_before]
    out_ref, panel, acc, sems = refs[-4:]
    core = info_ref[6]
    copies, at = [], 0
    for n, chunk in enumerate(chunks):
        size = chunk.shape[0]
        copies.append(pltpu.make_async_copy(chunk, panel.at[pl.ds(at, size)], sems.at[n]))
        at += size
    for copy in copies:
        copy.start()

    @pl.loop(0, acc.shape[0])
    def _(d):
        acc[d] = jnp.zeros((T, 2 * T), F32)

    for copy in copies:
        copy.wait()
    first = info_ref[group]
    low = lax.broadcasted_iota(I32, (T, 2 * T), 1) < T

    def placed(code):
        pairs = panel[jnp.bitwise_and(jnp.right_shift(code, 9), 127)].astype(F32)
        swap = jnp.bitwise_and(jnp.right_shift(code, 16), 1) == 1
        to_low = jnp.bitwise_and(jnp.right_shift(code, 17), 1) == 0
        pairs = jnp.where(swap, pltpu.roll(pairs, T, 1), pairs)
        return jnp.where(low == to_low, pairs, 0.0).astype(BF16)

    @pl.loop(0, info_ref[3 + group])
    def _(step):
        for half in range(2):
            base = first + step * UNROLL + half * (UNROLL // 2)
            codes = [code_ref[base + e] for e in range(UNROLL // 2)]
            terms = [
                jnp.dot(b_ref[jnp.bitwise_and(code, 511)], placed(code), preferred_element_type=F32)
                for code in codes
            ]
            for code, term in zip(codes, terms):
                d = jnp.right_shift(code, 18)
                acc[d] = acc[d] + term

    @pl.loop(0, KC)
    def _(k):
        for o in range(8):
            tile = jnp.concatenate([acc[k, o * 8:(o + 1) * 8], acc[KC + k, o * 8:(o + 1) * 8]], axis=0)
            place = (jnp.bitwise_xor(core, o % 2), o // 2, k)
            for earlier in before:
                tile = tile + earlier[place].astype(F32)
            out_ref[place] = tile.astype(BF16)


def panel_sums(group, code, info, chunks, b, before=()):
    smem = pl.BlockSpec(memory_space=pltpu.SMEM)
    vmem = pl.BlockSpec(memory_space=pltpu.VMEM)
    anyw = pl.BlockSpec(memory_space=pl.ANY)
    pairs = sum(c.shape[0] for c in chunks)
    return pl.pallas_call(
        functools.partial(sum_kernel, group, len(chunks), len(before)),
        in_specs=[smem, smem] + [anyw] * len(chunks) + [vmem] * (1 + len(before)),
        out_specs=vmem,
        out_shape=jax.ShapeDtypeStruct((2, NY, KC, 16, 2 * T), BF16),
        scratch_shapes=[
            pltpu.VMEM((pairs, T, 2 * T), BF16),
            pltpu.VMEM((2 * KC + 1, T, 2 * T), F32),
            pltpu.SemaphoreType.DMA((len(chunks),)),
        ],
        compiler_params=pltpu.CompilerParams(vmem_limit_bytes=24 * MIB),
        cost_estimate=pl.CostEstimate(flops=pairs * 2**20, bytes_accessed=8 * MIB, transcendentals=0),
        name=f"panel_sums_{group}",
    )(code, info, *chunks, b, *before)


def body(a_tiles, a_cols, a_count, a_slot, agg, p_tiles):
    rows, slots = a_tiles.shape[:2]
    total = rows * slots
    core, yl, me_x = lax.axis_index("core"), lax.axis_index("yl"), lax.axis_index("x")
    packed = jnp.concatenate([p_tiles[0, :4], p_tiles[0, 4:]], axis=-1)

    column = spread(packed, ("yh", "z"))
    own = jnp.stack([packed] + [shifted(packed, "yl", k) for k in range(1, NY)])
    column, own = lax.optimization_barrier((column, own))
    column = column.reshape(2, -1, T, 2 * T)

    left_a, right_b = shifted(column[0], "x", 1), shifted(column[1], "x", -1)
    left_b, right_a = shifted(column[1], "x", 1), shifted(column[0], "x", -1)
    left2, right2 = shifted(left_a, "x", 1), shifted(right_b, "x", -1)
    own = jnp.stack([own, shifted(own, "core", 1)])

    live = jnp.arange(slots, dtype=I32)[None, :] < a_count
    owner = a_cols // 8
    far = jnp.bitwise_and(owner - me_x + 4, 3)
    pair = ((owner // 4) % 2 * 8 + owner // 8) * 4 + a_cols % 4 + jnp.where(far == 1, 64, 0)
    group = jnp.where(far == 0, 0, jnp.where(far == 2, 2, 1))
    to_high = jnp.broadcast_to(agg[:, None] % CR, a_cols.shape)
    target = agg[:, None] // CR * KC + a_slot
    swap = ((a_cols % 8) // 4 + to_high) % 2
    code = ((target * 2 + to_high) * 2 + swap) * 2**16 + pair * 2**9 + jnp.arange(total, dtype=I32).reshape(rows, slots)
    code = code.reshape(total)
    picked = (group.reshape(total)[:, None] == jnp.arange(3, dtype=I32)) & live.reshape(total)[:, None]
    lower = jnp.arange(total, dtype=I32)[:, None] > jnp.arange(total, dtype=I32)[None, :]
    rank = jnp.dot(lower.astype(BF16), picked.astype(BF16), preferred_element_type=F32).astype(I32)
    steps = (jnp.sum(picked.astype(I32), axis=0) + UNROLL - 1) // UNROLL
    first = (jnp.cumsum(steps) - steps) * UNROLL
    place = jnp.sum(jnp.where(picked, rank + first[None, :] + 1, 0), axis=1) - 1
    here = jnp.arange(total + 3 * UNROLL, dtype=I32)[:, None] == place[None, :]
    empty = 2 * KC * 2**18
    code = jnp.sum(jnp.where(here, code[None, :] - empty, 0), axis=1) + empty
    info = jnp.concatenate([first, steps, jnp.stack([core, yl])]).astype(I32)

    b = left_products(info, own, a_tiles)
    sums0 = panel_sums(0, code, info, [column.reshape(-1, T, 2 * T)], b)
    sums1 = panel_sums(1, code, info, [left_a, left_b, right_a, right_b], b)
    sums2 = panel_sums(2, code, info, [left2, right2], b, (sums0, sums1))

    chip = (sums2[0].astype(F32) + shifted(sums2[1], "core", 1).astype(F32)).astype(BF16)
    shares = jnp.sum(lax.all_to_all(chip, "yl", 0, 0, tiled=True).astype(F32), axis=0)
    moved = shifted(shares[:, 8:].astype(BF16), ROW, 1)
    result = shares[:, :8] + moved.astype(F32)
    return jnp.stack([result[..., :T], result[..., T:]])


def solution(mesh):
    fine = Mesh(mesh.devices.reshape(8, 2, 4, 4, 2), ROW + COL)
    return jax.shard_map(
        body,
        mesh=fine,
        in_specs=(
            P(ROW, COL, None, None),
            P(ROW, COL),
            P(ROW, COL),
            P(ROW, COL),
            P(ROW),
            P(COL, ROW, None, None),
        ),
        out_specs=P(ROW, None, COL, None),
        check_vma=False,
    )
```

time: 151 us -> 135 us (0.89)
  waiting for transfers between devices: 49.2 us -> 31 us
  blocking collectives: 0 us -> 18 us
  Pallas kernels: 21.3 us -> 15.9 us
  starting transfers between devices: 63.1 us -> 58.3 us
  other arithmetic: 6.01 us -> 3.78 us
  local copies, waits for them, and re-layouts: 8.78 us -> 6.7 us
    all_to_all x2 -> x1, waiting for transfers between devices: 32 us -> 0.01 us  [spread(): return lax.all_to_all(copies, axis, 0, 0, tiled=True)]
    ppermute x8 -> x12, waiting for transfers between devices: 7.52 us -> 31 us  [shifted(): lax.ppermute(value, axis, [(i, (i + by) % count) for i in range(count)])]
    ppermute x8 -> x12, starting transfers between devices: 23.8 us -> 42.1 us  [shifted(): lax.ppermute(value, axis, [(i, (i + by) % count) for i in range(count)])]
    all_to_all x0 -> x1, blocking collectives: none -> 18 us  [body(): lax.all_to_all(chip, 'yl', 0, 0, tiled=True).astype(F32)]
    all_to_all x2 -> x1, starting transfers between devices: 27.8 us -> 16.2 us  [spread(): return lax.all_to_all(copies, axis, 0, 0, tiled=True)]
    all_to_all x2 -> x0, starting transfers between devices: 11.5 us -> none  [over_col(): lax.all_to_all(chip, 'yl', 0, 0, tiled=True).astype(F32)]
    all_to_all x2 -> x0, waiting for transfers between devices: 9.68 us -> none  [over_col(): lax.all_to_all(chip, 'yl', 0, 0, tiled=True).astype(F32)]
    pallas_call x4 -> x3, Pallas kernels: 17.1 us -> 12 us  [panel_sums(): pl.pallas_call(functools.partial(sum_kernel, group, len(chunks), len(befo...]
  transfers between devices with their start and end apart: 12 -> 13, of which waited for: 5 -> 5; matrix products, arithmetic and copies ran while one was open for 6% -> 3% of each run, Pallas kernels for 12% -> 10%
where the time goes in v3:
time: 135 us; the launch traced here: 134 us
  starting transfers between devices  58.3 us (43%)
  waiting for transfers between devices  31 us (23%)
  blocking collectives  18 us (13%)
  Pallas kernels  15.9 us (12%)
  local copies, waits for them, and re-layouts  6.7 us (5%)
  other arithmetic  3.78 us (3%)
    ppermute x12, starting transfers between devices, shifted(): lax.ppermute(value, axis, [(i, (i + by) % count) for i in range(count)])  42.1 us
    ppermute x12, waiting for transfers between devices, shifted(): lax.ppermute(value, axis, [(i, (i + by) % count) for i in range(count)])  31 us
    all_to_all x1, blocking collectives, body(): lax.all_to_all(chip, 'yl', 0, 0, tiled=True).astype(F32)  18 us
    all_to_all x1, starting transfers between devices, spread(): return lax.all_to_all(copies, axis, 0, 0, tiled=True)  16.2 us
    pallas_call x3, Pallas kernels, panel_sums(): pl.pallas_call(functools.partial(sum_kernel, group, len(chunks), len(befo...  12 us
    pallas_call x1, Pallas kernels, left_products(): pl.pallas_call(left_kernel, grid=(4,), in_specs=[pl.BlockSpec(memory_spac...  3.85 us
    unnamed x2, local copies, waits for them, and re-layouts  2.78 us
  transfers between devices with their start and end apart: 13, of which 5 were waited for; matrix products, arithmetic and copies ran while one was open for 3% of the time, Pallas kernels for 10%

profile of v3, /device:TPU:1, one launch (start us, length us, event | category | flops | bytes accessed | tf_op | source)
XLA Modules:
  0.0 134.1 jit_solution(6185303701815642632)
XLA Ops:
  0.0 0.9 slice_bitcast_fusion.5
  0.9 0.1 pad_maximum_fusion.3
  1.0 1.2 broadcast_in_dim.53
  2.2 16.2 %all-to-all-start = ((bf16[16,4,64,128]{3,2,1,0:T(8,128)(2,1)}), bf16[16,4,64,128]{3,2,1,0:T(8,128)(2,1)S(1)}, u32[]{:S(2)}, u32[]{:S(2)}) async-start(bf16[16,4,64,128]{3,2,1,0:T(8,128)(2,1)} %broadcast_in_dim.53), calls=%async_computation | async-start | bytes 2097152 | tf_op jit(solution)/shard_map/all_to_all | solution.py:31
  18.4 2.5 %collective-permute-start.2 = (bf16[4,64,128]{2,1,0:T(8,128)(2,1)S(1)}, bf16[4,64,128]{2,1,0:T(8,128)(2,1)S(1)}, u32[]{:S(2)}, u32[]{:S(2)}) collective-permute-start(bf16[4,64,128]{2,1,0:T(8,128)(2,1)S(1)} %pad_maximum_fusion.3), channel_id=1, source_target_pairs={{0,6},{2,0},{4,2},{6,4},{1,7},{3,1},{5,3},{7,5},{8,14},{10,8},{12,... | collective-permute-start | bytes 196616 | tf_op jit(solution)/shard_map/ppermute | solution.py:25
  21.0 2.7 %collective-permute-start = (bf16[4,64,128]{2,1,0:T(8,128)(2,1)S(1)}, bf16[4,64,128]{2,1,0:T(8,128)(2,1)S(1)}, u32[]{:S(2)}, u32[]{:S(2)}) collective-permute-start(bf16[4,64,128]{2,1,0:T(8,128)(2,1)S(1)} %pad_maximum_fusion.3), channel_id=1, source_target_pairs={{0,2},{2,4},{4,6},{6,0},{1,3},{3,5},{5,7},{7,1},{8,10},{10,12},{12... | collective-permute-start | bytes 196616 | tf_op jit(solution)/shard_map/ppermute | solution.py:25
  23.7 2.4 %collective-permute-start.1 = (bf16[4,64,128]{2,1,0:T(8,128)(2,1)S(1)}, bf16[4,64,128]{2,1,0:T(8,128)(2,1)S(1)}, u32[]{:S(2)}, u32[]{:S(2)}) collective-permute-start(bf16[4,64,128]{2,1,0:T(8,128)(2,1)S(1)} %pad_maximum_fusion.3), channel_id=1, source_target_pairs={{0,4},{2,6},{4,0},{6,2},{1,5},{3,7},{5,1},{7,3},{8,12},{10,14},{12... | collective-permute-start | bytes 196616 | tf_op jit(solution)/shard_map/ppermute | solution.py:25
  26.2 0.7 fusion.32
  26.8 0.7 select_select_fusion
  27.6 0.1 copy.9
  27.7 0.1 eq.49
  27.8 0.7 iota_compare_fusion.3
  28.6 0.1 lt.50
  28.7 0.1 convert_reduce_fusion.1
  28.8 0.1 copy.10
  28.9 0.1 sub.78
  29.1 0.2 reduce-window.7
  29.3 17.2 %collective-permute-done.2 = bf16[4,64,128]{2,1,0:T(8,128)(2,1)S(1)} collective-permute-done((bf16[4,64,128]{2,1,0:T(8,128)(2,1)S(1)}, bf16[4,64,128]{2,1,0:T(8,128)(2,1)S(1)}, u32[]{:S(2)}, u32[]{:S(2)}) %collective-permute-start.2) | collective-permute-done | bytes 65568 | tf_op jit(solution)/shard_map/ppermute | solution.py:25
  46.5 0.0 collective-permute-done.1
  46.5 1.1 fusion.33
  47.6 3.1 %collective-permute-start.3 = (bf16[32,64,128]{2,1,0:T(8,128)(2,1)}, bf16[32,64,128]{2,1,0:T(8,128)(2,1)S(1)}, u32[]{:S(2)}, u32[]{:S(2)}) collective-permute-start(bf16[32,64,128]{2,1,0:T(8,128)(2,1)} %bitcast.11), channel_id=1, source_target_pairs={{0,8},{8,16},{16,24},{24,0},{1,9},{9,17},{17,25},{25,1},{2,10},{10... | collective-permute-start | bytes 1572872 | tf_op jit(solution)/shard_map/ppermute | solution.py:25
  50.7 3.4 %collective-permute-start.5 = (bf16[32,64,128]{2,1,0:T(8,128)(2,1)}, bf16[32,64,128]{2,1,0:T(8,128)(2,1)S(1)}, u32[]{:S(2)}, u32[]{:S(2)}) collective-permute-start(bf16[32,64,128]{2,1,0:T(8,128)(2,1)} %bitcast.12), channel_id=1, source_target_pairs={{0,24},{8,0},{16,8},{24,16},{1,25},{9,1},{17,9},{25,17},{2,26},{10... | collective-permute-start | bytes 1572872 | tf_op jit(solution)/shard_map/ppermute | solution.py:25
  54.1 0.2 fusion.3
  54.3 1.9 %collective-permute-start.8 = (bf16[32,64,128]{2,1,0:T(8,128)(2,1)}, bf16[32,64,128]{2,1,0:T(8,128)(2,1)}, u32[]{:S(2)}, u32[]{:S(2)}) collective-permute-start(bf16[32,64,128]{2,1,0:T(8,128)(2,1)} %bitcast.12), channel_id=1, source_target_pairs={{0,8},{8,16},{16,24},{24,0},{1,9},{9,17},{17,25},{25,1},{2,10},{10... | collective-permute-start | bytes 1572872 | tf_op jit(solution)/shard_map/ppermute | solution.py:25
  56.3 4.6 %collective-permute-start.9 = (bf16[32,64,128]{2,1,0:T(8,128)(2,1)}, bf16[32,64,128]{2,1,0:T(8,128)(2,1)}, u32[]{:S(2)}, u32[]{:S(2)}) collective-permute-start(bf16[32,64,128]{2,1,0:T(8,128)(2,1)} %bitcast.11), channel_id=1, source_target_pairs={{0,24},{8,0},{16,8},{24,16},{1,25},{9,1},{17,9},{25,17},{2,26},{10... | collective-permute-start | bytes 1572872 | tf_op jit(solution)/shard_map/ppermute | solution.py:25
  60.8 0.1 collective-permute-done.3.refs_2_
  60.9 1.9 %collective-permute-start.4 = (bf16[32,64,128]{2,1,0:T(8,128)(2,1)S(1)}, bf16[32,64,128]{2,1,0:T(8,128)(2,1)S(1)}, u32[]{:S(2)}, u32[]{:S(2)}) collective-permute-start(bf16[32,64,128]{2,1,0:T(8,128)(2,1)S(1)} %collective-permute-done.3.refs_2_), channel_id=1, source_target_pairs={{0,8},{8,16},{16,24},{24,0},{1,9},{9,17},{17,25},{25,1},{2,10},{10... | collective-permute-start | bytes 1572872 | tf_op jit(solution)/shard_map/ppermute | solution.py:25
  62.9 4.6 %collective-permute-start.6 = (bf16[32,64,128]{2,1,0:T(8,128)(2,1)S(1)}, bf16[32,64,128]{2,1,0:T(8,128)(2,1)S(1)}, u32[]{:S(2)}, u32[]{:S(2)}) collective-permute-start(bf16[32,64,128]{2,1,0:T(8,128)(2,1)S(1)} %collective-permute-done.5.refs_5_), channel_id=1, source_target_pairs={{0,24},{8,0},{16,8},{24,16},{1,25},{9,1},{17,9},{25,17},{2,26},{10... | collective-permute-start | bytes 1572872 | tf_op jit(solution)/shard_map/ppermute | solution.py:25
  67.4 0.2 select_reduce_fusion
  67.6 10.7 %collective-permute-start.7 = (bf16[4,4,64,128]{3,2,1,0:T(8,128)(2,1)S(1)}, bf16[4,4,64,128]{3,2,1,0:T(8,128)(2,1)S(1)}, u32[]{:S(2)}, u32[]{:S(2)}) collective-permute-start(bf16[4,4,64,128]{3,2,1,0:T(8,128)(2,1)S(1)} %pad_maximum_fusion.1), channel_id=1, source_target_pairs={{0,1},{1,0},{2,3},{3,2},{4,5},{5,4},{6,7},{7,6},{8,9},{9,8},{10,11... | collective-permute-start | bytes 786440 | tf_op jit(solution)/shard_map/ppermute | solution.py:25
  78.3 0.1 pad_add_fusion.info_ref.refs_1_
  78.4 1.1 collective-permute-done.7
  79.5 0.1 pad_maximum_fusion.own_ref
  79.5 0.0 copy-start
  79.5 2.8 %copy-done = bf16[64,6,64,64]{3,2,1,0:T(8,128)(2,1)S(1)} copy-done((bf16[64,6,64,64]{3,2,1,0:T(8,128)(2,1)S(1)}, bf16[64,6,64,64]{3,2,1,0:T(8,128)(2,1)}, u32[]{:S(2)}) %copy-start) | copy-done | bytes 3145752
  82.3 3.8 %left_products.1 = bf16[2,4,8,6,64,64]{5,4,3,2,1,0:T(8,128)(2,1)S(1)} custom-call(s32[8]{0:T(128)S(1)} %pad_add_fusion.info_ref.refs_1_, bf16[2,4,4,64,128]{4,3,2,1,0:T(8,128)(2,1)S(1)} %pad_maximum_fusion.own_ref, bf16[2,4,8,6,64,64]{5,4,3,2,1,0:T(8,128)(2,1)S(1)} %bitcast.45), custom_call_target="tpu_custom_call" | custom-call | flops 201326592 | bytes 16777216 | tf_op jit(solution)/shard_map/left_products/pallas_call | solution.py:48
  86.1 3.0 %panel_sums_0.1.refs_5_ = bf16[2,4,27,16,128]{4,3,2,1,0:T(8,128)(2,1)S(1)} custom-call(s32[408]{0:T(512)S(1)} %broadcast_add_fusion.refs_0_, s32[8]{0:T(128)S(1)} %pad_add_fusion.info_ref.refs_1_, bf16[64,64,128]{2,1,0:T(8,128)(2,1)S(1)} %bitcast.44, bf16[384,64,64]{2,1,0:T(8,128)(2,1)S(1)} %bitcast.41), custom_call_target="tpu_custom_call" | custom-call | flops 67108864 | bytes 8388608 | tf_op jit(solution)/shard_map/panel_sums_0/pallas_call | solution.py:124
  89.2 6.0 %panel_sums_1.1.refs_6_ = bf16[2,4,27,16,128]{4,3,2,1,0:T(8,128)(2,1)S(1)} custom-call(s32[408]{0:T(512)S(1)} %broadcast_add_fusion.refs_0_, s32[8]{0:T(128)S(1)} %pad_add_fusion.info_ref.refs_1_, bf16[32,64,128]{2,1,0:T(8,128)(2,1)S(1)} %collective-permute-done.3.refs_2_, bf16[32,64,128]{2,1,0:T(8,128)(2,1)} %collective-permute-done.8.refs_3_, ...), custom_call_target="tpu_custom_call" | custom-call | flops 134217728 | bytes 8388608 | tf_op jit(solution)/shard_map/panel_sums_1/pallas_call | solution.py:124
  95.2 3.0 %panel_sums_2.1 = bf16[2,4,27,16,128]{4,3,2,1,0:T(8,128)(2,1)S(1)} custom-call(s32[408]{0:T(512)S(1)} %broadcast_add_fusion.refs_0_, s32[8]{0:T(128)S(1)} %pad_add_fusion.info_ref.refs_1_, bf16[32,64,128]{2,1,0:T(8,128)(2,1)S(1)} %collective-permute-done.4.refs_2_, bf16[32,64,128]{2,1,0:T(8,128)(2,1)S(1)} %collective-permute-done.6.refs_3_, ...), custom_call_target="tpu_custom_call" | custom-call | flops 67108864 | bytes 8388608 | tf_op jit(solution)/shard_map/panel_sums_2/pallas_call | solution.py:124
  98.3 2.3 %collective-permute-start.10 = (bf16[4,27,16,128]{3,2,1,0:T(8,128)(2,1)S(1)}, bf16[4,27,16,128]{3,2,1,0:T(8,128)(2,1)S(1)}, u32[]{:S(2)}, u32[]{:S(2)}) collective-permute-start(bf16[4,27,16,128]{3,2,1,0:T(8,128)(2,1)S(1)} %slice_bitcast_fusion), channel_id=1, source_target_pairs={{0,1},{1,0},{2,3},{3,2},{4,5},{5,4},{6,7},{7,6},{8,9},{9,8},{10,11... | collective-permute-start | bytes 1327112 | tf_op jit(solution)/shard_map/ppermute | solution.py:25
  100.6 1.4 %collective-permute-done.10 = bf16[4,27,16,128]{3,2,1,0:T(8,128)(2,1)S(1)} collective-permute-done((bf16[4,27,16,128]{3,2,1,0:T(8,128)(2,1)S(1)}, bf16[4,27,16,128]{3,2,1,0:T(8,128)(2,1)S(1)}, u32[]{:S(2)}, u32[]{:S(2)}) %collective-permute-start.10) | collective-permute-done | bytes 442400 | tf_op jit(solution)/shard_map/ppermute | solution.py:25
  102.0 0.1 fusion.4
  102.1 18.0 %all_to_all.10 = bf16[4,27,16,128]{3,2,1,0:T(8,128)(2,1)S(1)} all-to-all(bf16[4,27,16,128]{3,2,1,0:T(8,128)(2,1)S(1)} %fusion.4), channel_id=1, replica_groups=mesh['z'=8,'yh'=2,'x'=4,'yl'=4,'core'=2] {'yl'}, dimensions={0} | all-to-all | bytes 884736 | tf_op jit(solution)/shard_map/all_to_all | solution.py:183
  120.1 0.1 convert_reduce_fusion
  120.2 1.9 %collective-permute-start.11 = (bf16[27,8,128]{2,1,0:T(8,128)(2,1)S(1)}, bf16[27,8,128]{2,1,0:T(8,128)(2,1)S(1)}, u32[]{:S(2)}, u32[]{:S(2)}) collective-permute-start(bf16[27,8,128]{2,1,0:T(8,128)(2,1)S(1)} %slice.61), channel_id=1, source_target_pairs={{0,8},{8,16},{16,24},{24,32},{32,40},{40,48},{48,56},{56,64},{64,7... | collective-permute-start | bytes 165896 | tf_op jit(solution)/shard_map/ppermute | solution.py:25
  122.1 11.2 %collective-permute-done.11 = bf16[27,8,128]{2,1,0:T(8,128)(2,1)S(1)} collective-permute-done((bf16[27,8,128]{2,1,0:T(8,128)(2,1)S(1)}, bf16[27,8,128]{2,1,0:T(8,128)(2,1)S(1)}, u32[]{:S(2)}, u32[]{:S(2)}) %collective-permute-start.11) | collective-permute-done | bytes 55328 | tf_op jit(solution)/shard_map/ppermute | solution.py:25
  133.3 0.1 slice_bitcast_fusion.3
  133.4 0.7 pad_maximum_fusion.2
  (15 shorter events, 0.1 us)
Async XLA Ops:
  2.2 44.3 %all-to-all-start = ((bf16[16,4,64,128]{3,2,1,0:T(8,128)(2,1)}), bf16[16,4,64,128]{3,2,1,0:T(8,128)(2,1)S(1)}, u32[]{:S(2)}, u32[]{:S(2)}) async-start(bf16[16,4,64,128]{3,2,1,0:T(8,128)(2,1)} %broadcast_in_dim.53), calls=%async_computation | async-start | bytes 2097152 | tf_op jit(solution)/shard_map/all_to_all | solution.py:31
  18.4 28.0 %collective-permute-start.2 = (bf16[4,64,128]{2,1,0:T(8,128)(2,1)S(1)}, bf16[4,64,128]{2,1,0:T(8,128)(2,1)S(1)}, u32[]{:S(2)}, u32[]{:S(2)}) collective-permute-start(bf16[4,64,128]{2,1,0:T(8,128)(2,1)S(1)} %pad_maximum_fusion.3), channel_id=1, source_target_pairs={{0,6},{2,0},{4,2},{6,4},{1,7},{3,1},{5,3},{7,5},{8,14},{10,8},{12,... | collective-permute-start | bytes 196616 | tf_op jit(solution)/shard_map/ppermute | solution.py:25
  21.0 25.5 %collective-permute-start = (bf16[4,64,128]{2,1,0:T(8,128)(2,1)S(1)}, bf16[4,64,128]{2,1,0:T(8,128)(2,1)S(1)}, u32[]{:S(2)}, u32[]{:S(2)}) collective-permute-start(bf16[4,64,128]{2,1,0:T(8,128)(2,1)S(1)} %pad_maximum_fusion.3), channel_id=1, source_target_pairs={{0,2},{2,4},{4,6},{6,0},{1,3},{3,5},{5,7},{7,1},{8,10},{10,12},{12... | collective-permute-start | bytes 196616 | tf_op jit(solution)/shard_map/ppermute | solution.py:25
  23.7 22.7 %collective-permute-start.1 = (bf16[4,64,128]{2,1,0:T(8,128)(2,1)S(1)}, bf16[4,64,128]{2,1,0:T(8,128)(2,1)S(1)}, u32[]{:S(2)}, u32[]{:S(2)}) collective-permute-start(bf16[4,64,128]{2,1,0:T(8,128)(2,1)S(1)} %pad_maximum_fusion.3), channel_id=1, source_target_pairs={{0,4},{2,6},{4,0},{6,2},{1,5},{3,7},{5,1},{7,3},{8,12},{10,14},{12... | collective-permute-start | bytes 196616 | tf_op jit(solution)/shard_map/ppermute | solution.py:25
  47.6 13.3 %collective-permute-start.3 = (bf16[32,64,128]{2,1,0:T(8,128)(2,1)}, bf16[32,64,128]{2,1,0:T(8,128)(2,1)S(1)}, u32[]{:S(2)}, u32[]{:S(2)}) collective-permute-start(bf16[32,64,128]{2,1,0:T(8,128)(2,1)} %bitcast.11), channel_id=1, source_target_pairs={{0,8},{8,16},{16,24},{24,0},{1,9},{9,17},{17,25},{25,1},{2,10},{10... | collective-permute-start | bytes 1572872 | tf_op jit(solution)/shard_map/ppermute | solution.py:25
  50.7 12.1 %collective-permute-start.5 = (bf16[32,64,128]{2,1,0:T(8,128)(2,1)}, bf16[32,64,128]{2,1,0:T(8,128)(2,1)S(1)}, u32[]{:S(2)}, u32[]{:S(2)}) collective-permute-start(bf16[32,64,128]{2,1,0:T(8,128)(2,1)} %bitcast.12), channel_id=1, source_target_pairs={{0,24},{8,0},{16,8},{24,16},{1,25},{9,1},{17,9},{25,17},{2,26},{10... | collective-permute-start | bytes 1572872 | tf_op jit(solution)/shard_map/ppermute | solution.py:25
  54.3 34.8 %collective-permute-start.8 = (bf16[32,64,128]{2,1,0:T(8,128)(2,1)}, bf16[32,64,128]{2,1,0:T(8,128)(2,1)}, u32[]{:S(2)}, u32[]{:S(2)}) collective-permute-start(bf16[32,64,128]{2,1,0:T(8,128)(2,1)} %bitcast.12), channel_id=1, source_target_pairs={{0,8},{8,16},{16,24},{24,0},{1,9},{9,17},{17,25},{25,1},{2,10},{10... | collective-permute-start | bytes 1572872 | tf_op jit(solution)/shard_map/ppermute | solution.py:25
  56.3 32.9 %collective-permute-start.9 = (bf16[32,64,128]{2,1,0:T(8,128)(2,1)}, bf16[32,64,128]{2,1,0:T(8,128)(2,1)}, u32[]{:S(2)}, u32[]{:S(2)}) collective-permute-start(bf16[32,64,128]{2,1,0:T(8,128)(2,1)} %bitcast.11), channel_id=1, source_target_pairs={{0,24},{8,0},{16,8},{24,16},{1,25},{9,1},{17,9},{25,17},{2,26},{10... | collective-permute-start | bytes 1572872 | tf_op jit(solution)/shard_map/ppermute | solution.py:25
  60.9 34.3 %collective-permute-start.4 = (bf16[32,64,128]{2,1,0:T(8,128)(2,1)S(1)}, bf16[32,64,128]{2,1,0:T(8,128)(2,1)S(1)}, u32[]{:S(2)}, u32[]{:S(2)}) collective-permute-start(bf16[32,64,128]{2,1,0:T(8,128)(2,1)S(1)} %collective-permute-done.3.refs_2_), channel_id=1, source_target_pairs={{0,8},{8,16},{16,24},{24,0},{1,9},{9,17},{17,25},{25,1},{2,10},{10... | collective-permute-start | bytes 1572872 | tf_op jit(solution)/shard_map/ppermute | solution.py:25
  62.9 32.3 %collective-permute-start.6 = (bf16[32,64,128]{2,1,0:T(8,128)(2,1)S(1)}, bf16[32,64,128]{2,1,0:T(8,128)(2,1)S(1)}, u32[]{:S(2)}, u32[]{:S(2)}) collective-permute-start(bf16[32,64,128]{2,1,0:T(8,128)(2,1)S(1)} %collective-permute-done.5.refs_5_), channel_id=1, source_target_pairs={{0,24},{8,0},{16,8},{24,16},{1,25},{9,1},{17,9},{25,17},{2,26},{10... | collective-permute-start | bytes 1572872 | tf_op jit(solution)/shard_map/ppermute | solution.py:25
  67.6 11.9 %collective-permute-start.7 = (bf16[4,4,64,128]{3,2,1,0:T(8,128)(2,1)S(1)}, bf16[4,4,64,128]{3,2,1,0:T(8,128)(2,1)S(1)}, u32[]{:S(2)}, u32[]{:S(2)}) collective-permute-start(bf16[4,4,64,128]{3,2,1,0:T(8,128)(2,1)S(1)} %pad_maximum_fusion.1), channel_id=1, source_target_pairs={{0,1},{1,0},{2,3},{3,2},{4,5},{5,4},{6,7},{7,6},{8,9},{9,8},{10,11... | collective-permute-start | bytes 786440 | tf_op jit(solution)/shard_map/ppermute | solution.py:25
  79.5 2.8 %copy-start = (bf16[64,6,64,64]{3,2,1,0:T(8,128)(2,1)S(1)}, bf16[64,6,64,64]{3,2,1,0:T(8,128)(2,1)}, u32[]{:S(2)}) copy-start(bf16[64,6,64,64]{3,2,1,0:T(8,128)(2,1)} %param.6) | copy-start | bytes 9437188
  98.3 3.7 %collective-permute-start.10 = (bf16[4,27,16,128]{3,2,1,0:T(8,128)(2,1)S(1)}, bf16[4,27,16,128]{3,2,1,0:T(8,128)(2,1)S(1)}, u32[]{:S(2)}, u32[]{:S(2)}) collective-permute-start(bf16[4,27,16,128]{3,2,1,0:T(8,128)(2,1)S(1)} %slice_bitcast_fusion), channel_id=1, source_target_pairs={{0,1},{1,0},{2,3},{3,2},{4,5},{5,4},{6,7},{7,6},{8,9},{9,8},{10,11... | collective-permute-start | bytes 1327112 | tf_op jit(solution)/shard_map/ppermute | solution.py:25
  120.2 13.1 %collective-permute-start.11 = (bf16[27,8,128]{2,1,0:T(8,128)(2,1)S(1)}, bf16[27,8,128]{2,1,0:T(8,128)(2,1)S(1)}, u32[]{:S(2)}, u32[]{:S(2)}) collective-permute-start(bf16[27,8,128]{2,1,0:T(8,128)(2,1)S(1)} %slice.61), channel_id=1, source_target_pairs={{0,8},{8,16},{16,24},{24,32},{32,40},{40,48},{48,56},{56,64},{64,7... | collective-permute-start | bytes 165896 | tf_op jit(solution)/shard_map/ppermute | solution.py:25

commit v4 on v3

--- a/solution.py
+++ b/solution.py
@@ -31,35 +31,45 @@
     return lax.all_to_all(copies, axis, 0, 0, tiled=True)
 
 
-def left_kernel(info_ref, own_ref, a_ref, b_ref):
+def left_kernel(info_ref, own_ref, a_ref, b_ref, done_ref, a_here, sems):
     core, yl = info_ref[6], info_ref[7]
-    for c in range(8):
-        far = jnp.bitwise_and(yl - c // 2 + NY, NY - 1)
-        both = own_ref[jnp.bitwise_xor(core, c % 2), far, 0].astype(F32).T.astype(BF16)
+    done_ref[...] = jnp.zeros(done_ref.shape, F32)
+
+    def fetch(v, h):
+        return pltpu.make_async_copy(a_ref.at[h, v], a_here.at[v, h], sems.at[v, h])
+
+    for v in range(4):
         for h in range(2):
-            left = both[h * T:(h + 1) * T]
-            for s in range(a_ref.shape[3]):
-                b_ref[h, 0, c, s] = jnp.dot(left, a_ref[h, 0, c, s], preferred_element_type=F32).astype(BF16)
+            fetch(v, h).start()
+
+    @pl.loop(0, 4)
+    def _(v):
+        for h in range(2):
+            fetch(v, h).wait()
+        for c in range(8):
+            far = jnp.bitwise_and(yl - c // 2 + NY, NY - 1)
+            both = own_ref[jnp.bitwise_xor(core, c % 2), far, v].astype(F32).T.astype(BF16)
+            for h in range(2):
+                left = both[h * T:(h + 1) * T]
+                for s in range(a_ref.shape[3]):
+                    b_ref[h, v, c, s] = jnp.dot(left, a_here[v, h, c, s], preferred_element_type=F32).astype(BF16)
 
 
 def left_products(info, own, a_tiles):
     rows, slots = a_tiles.shape[:2]
     a = a_tiles.reshape(2, 4, 8, slots, T, T)
-    b = pl.pallas_call(
+    vmem = pl.BlockSpec(memory_space=pltpu.VMEM)
+    b, done = pl.pallas_call(
         left_kernel,
-        grid=(4,),
-        in_specs=[
-            pl.BlockSpec(memory_space=pltpu.SMEM),
-            pl.BlockSpec((2, NY, 1, T, 2 * T), lambda v: (0, 0, v, 0, 0)),
-            pl.BlockSpec((2, 1, 8, slots, T, T), lambda v: (0, v, 0, 0, 0, 0)),
-        ],
-        out_specs=pl.BlockSpec((2, 1, 8, slots, T, T), lambda v: (0, v, 0, 0, 0, 0)),
-        out_shape=jax.ShapeDtypeStruct(a.shape, BF16),
-        compiler_params=pltpu.CompilerParams(vmem_limit_bytes=16 * MIB),
+        in_specs=[pl.BlockSpec(memory_space=pltpu.SMEM), vmem, pl.BlockSpec(memory_space=pltpu.HBM)],
+        out_specs=[vmem, vmem],
+        out_shape=[jax.ShapeDtypeStruct(a.shape, BF16), jax.ShapeDtypeStruct((8, 2 * T), F32)],
+        scratch_shapes=[pltpu.VMEM((4, 2, 8, slots, T, T), BF16), pltpu.SemaphoreType.DMA((4, 2))],
+        compiler_params=pltpu.CompilerParams(vmem_limit_bytes=46 * MIB),
         cost_estimate=pl.CostEstimate(flops=2 * rows * slots * T**3, bytes_accessed=16 * MIB, transcendentals=0),
         name="left_products",
     )(info, own, a)
-    return b.reshape(rows * slots, T, T)
+    return b.reshape(rows * slots, T, T), done
 
 
 def sum_kernel(group, n_chunks, n_before, *refs):
@@ -141,23 +151,23 @@
     rows, slots = a_tiles.shape[:2]
     total = rows * slots
     core, yl, me_x = lax.axis_index("core"), lax.axis_index("yl"), lax.axis_index("x")
+    me_yh = lax.axis_index("yh")
     packed = jnp.concatenate([p_tiles[0, :4], p_tiles[0, 4:]], axis=-1)
 
-    column = spread(packed, ("yh", "z"))
+    across = shifted(packed, "yh", 1)
     own = jnp.stack([packed] + [shifted(packed, "yl", k) for k in range(1, NY)])
-    column, own = lax.optimization_barrier((column, own))
-    column = column.reshape(2, -1, T, 2 * T)
-
-    left_a, right_b = shifted(column[0], "x", 1), shifted(column[1], "x", -1)
-    left_b, right_a = shifted(column[1], "x", 1), shifted(column[0], "x", -1)
-    left2, right2 = shifted(left_a, "x", 1), shifted(right_b, "x", -1)
+    near = spread(packed, "z").reshape(-1, T, 2 * T)
+    across, near = lax.optimization_barrier((across, near))
+    left_a, right_a = shifted(near, "x", 1), shifted(near, "x", -1)
     own = jnp.stack([own, shifted(own, "core", 1)])
+    other = spread(across, "z").reshape(-1, T, 2 * T)
 
     live = jnp.arange(slots, dtype=I32)[None, :] < a_count
     owner = a_cols // 8
     far = jnp.bitwise_and(owner - me_x + 4, 3)
-    pair = ((owner // 4) % 2 * 8 + owner // 8) * 4 + a_cols % 4 + jnp.where(far == 1, 64, 0)
-    group = jnp.where(far == 0, 0, jnp.where(far == 2, 2, 1))
+    away = jnp.bitwise_xor((owner // 4) % 2, me_yh)
+    group = jnp.where(far == 2, 1 + away, away)
+    pair = owner // 8 * 4 + a_cols % 4 + jnp.where(far == 3, 32, jnp.where(far == 1, 64, jnp.where(far == 2, 96 * (1 - away), 0)))
     to_high = jnp.broadcast_to(agg[:, None] % CR, a_cols.shape)
     target = agg[:, None] // CR * KC + a_slot
     swap = ((a_cols % 8) // 4 + to_high) % 2
@@ -174,10 +184,13 @@
     code = jnp.sum(jnp.where(here, code[None, :] - empty, 0), axis=1) + empty
     info = jnp.concatenate([first, steps, jnp.stack([core, yl])]).astype(I32)
 
-    b = left_products(info, own, a_tiles)
-    sums0 = panel_sums(0, code, info, [column.reshape(-1, T, 2 * T)], b)
-    sums1 = panel_sums(1, code, info, [left_a, left_b, right_a, right_b], b)
-    sums2 = panel_sums(2, code, info, [left2, right2], b, (sums0, sums1))
+    b, done = left_products(info, own, a_tiles)
+    other, _ = lax.optimization_barrier((other, done))
+    left_b, right_b = shifted(other, "x", 1), shifted(other, "x", -1)
+    left2, right2 = shifted(left_a, "x", 1), shifted(right_b, "x", -1)
+    sums0 = panel_sums(0, code, info, [near, left_a, right_a], b)
+    sums1 = panel_sums(1, code, info, [other, left_b, right_b, left2], b)
+    sums2 = panel_sums(2, code, info, [right2], b, (sums0, sums1))
 
     chip = (sums2[0].astype(F32) + shifted(sums2[1], "core", 1).astype(F32)).astype(BF16)
     shares = jnp.sum(lax.all_to_all(chip, "yl", 0, 0, tiled=True).astype(F32), axis=0)

time: 135 us -> 132 us (0.978)
  starting transfers between devices: 58.3 us -> 67.5 us
  waiting for transfers between devices: 31 us -> 24.3 us
  local copies, waits for them, and re-layouts: 6.7 us -> 3.45 us
  blocking collectives: 18 us -> 15.2 us
    ppermute x12 -> x13, waiting for transfers between devices: 31 us -> 13.7 us  [shifted(): lax.ppermute(value, axis, [(i, (i + by) % count) for i in range(count)])]
    all_to_all x1 -> x2, waiting for transfers between devices: 0.01 us -> 10.6 us  [spread(): return lax.all_to_all(copies, axis, 0, 0, tiled=True)]
    ppermute x12 -> x13, starting transfers between devices: 42.1 us -> 51.4 us  [shifted(): lax.ppermute(value, axis, [(i, (i + by) % count) for i in range(count)])]
    all_to_all x1, blocking collectives: 18 us -> 15.2 us  [body(): lax.all_to_all(chip, 'yl', 0, 0, tiled=True).astype(F32)]
    unnamed x2 -> x0, local copies, waits for them, and re-layouts: 2.78 us -> none
    all_to_all x1 -> x2, starting transfers between devices: 16.2 us -> 16.1 us  [spread(): return lax.all_to_all(copies, axis, 0, 0, tiled=True)]
  transfers between devices with their start and end apart: 13 -> 15, of which waited for: 5 -> 5; matrix products, arithmetic and copies ran while one was open for 3% -> 3% of each run, Pallas kernels for 10% -> 10%
where the time goes in v4:
time: 132 us; the launch traced here: 131 us
  starting transfers between devices  67.5 us (51%)
  waiting for transfers between devices  24.3 us (18%)
  Pallas kernels  16.2 us (12%)
  blocking collectives  15.2 us (12%)
  other arithmetic  3.79 us (3%)
  local copies, waits for them, and re-layouts  3.45 us (3%)
    ppermute x13, starting transfers between devices, shifted(): lax.ppermute(value, axis, [(i, (i + by) % count) for i in range(count)])  51.4 us
    all_to_all x2, starting transfers between devices, spread(): return lax.all_to_all(copies, axis, 0, 0, tiled=True)  16.1 us
    all_to_all x1, blocking collectives, body(): lax.all_to_all(chip, 'yl', 0, 0, tiled=True).astype(F32)  15.2 us
    ppermute x13, waiting for transfers between devices, shifted(): lax.ppermute(value, axis, [(i, (i + by) % count) for i in range(count)])  13.7 us
    pallas_call x3, Pallas kernels, panel_sums(): pl.pallas_call(functools.partial(sum_kernel, group, len(chunks), len(befo...  11.3 us
    all_to_all x2, waiting for transfers between devices, spread(): return lax.all_to_all(copies, axis, 0, 0, tiled=True)  10.6 us
    pallas_call x1, Pallas kernels, left_products(): pl.pallas_call(left_kernel, in_specs=[pl.BlockSpec(memory_space=pltpu.SME...  4.93 us
  transfers between devices with their start and end apart: 15, of which 5 were waited for; matrix products, arithmetic and copies ran while one was open for 3% of the time, Pallas kernels for 10%

profile of v4, /device:TPU:1, one launch (start us, length us, event | category | flops | bytes accessed | tf_op | source)
XLA Modules:
  0.0 130.9 jit_solution(10455213076408266610)
XLA Ops:
  0.0 0.9 slice_bitcast_fusion.5
  0.9 0.1 pad_maximum_fusion.3
  1.0 0.9 broadcast_in_dim.59
  1.9 10.9 %all-to-all-start = ((bf16[8,4,64,128]{3,2,1,0:T(8,128)(2,1)}), bf16[8,4,64,128]{3,2,1,0:T(8,128)(2,1)S(1)}, u32[]{:S(2)}, u32[]{:S(2)}) async-start(bf16[8,4,64,128]{3,2,1,0:T(8,128)(2,1)} %broadcast_in_dim.59), calls=%async_computation | async-start | bytes 1048576 | tf_op jit(solution)/shard_map/all_to_all | solution.py:31
  12.8 7.4 %collective-permute-start = (bf16[4,64,128]{2,1,0:T(8,128)(2,1)S(1)}, bf16[4,64,128]{2,1,0:T(8,128)(2,1)S(1)}, u32[]{:S(2)}, u32[]{:S(2)}) collective-permute-start(bf16[4,64,128]{2,1,0:T(8,128)(2,1)S(1)} %pad_maximum_fusion.3), channel_id=1, source_target_pairs={{0,32},{32,0},{1,33},{33,1},{2,34},{34,2},{3,35},{35,3},{4,36},{36... | collective-permute-start | bytes 196616 | tf_op jit(solution)/shard_map/ppermute | solution.py:25
  20.2 2.3 %collective-permute-start.3 = (bf16[4,64,128]{2,1,0:T(8,128)(2,1)S(1)}, bf16[4,64,128]{2,1,0:T(8,128)(2,1)S(1)}, u32[]{:S(2)}, u32[]{:S(2)}) collective-permute-start(bf16[4,64,128]{2,1,0:T(8,128)(2,1)S(1)} %pad_maximum_fusion.3), channel_id=1, source_target_pairs={{0,2},{2,4},{4,6},{6,0},{1,3},{3,5},{5,7},{7,1},{8,10},{10,12},{12... | collective-permute-start | bytes 196616 | tf_op jit(solution)/shard_map/ppermute | solution.py:25
  22.5 2.4 %collective-permute-start.4 = (bf16[4,64,128]{2,1,0:T(8,128)(2,1)S(1)}, bf16[4,64,128]{2,1,0:T(8,128)(2,1)S(1)}, u32[]{:S(2)}, u32[]{:S(2)}) collective-permute-start(bf16[4,64,128]{2,1,0:T(8,128)(2,1)S(1)} %pad_maximum_fusion.3), channel_id=1, source_target_pairs={{0,4},{2,6},{4,0},{6,2},{1,5},{3,7},{5,1},{7,3},{8,12},{10,14},{12... | collective-permute-start | bytes 196616 | tf_op jit(solution)/shard_map/ppermute | solution.py:25
  25.0 4.3 %collective-permute-start.5 = (bf16[4,64,128]{2,1,0:T(8,128)(2,1)S(1)}, bf16[4,64,128]{2,1,0:T(8,128)(2,1)S(1)}, u32[]{:S(2)}, u32[]{:S(2)}) collective-permute-start(bf16[4,64,128]{2,1,0:T(8,128)(2,1)S(1)} %pad_maximum_fusion.3), channel_id=1, source_target_pairs={{0,6},{2,0},{4,2},{6,4},{1,7},{3,1},{5,3},{7,5},{8,14},{10,8},{12,... | collective-permute-start | bytes 196616 | tf_op jit(solution)/shard_map/ppermute | solution.py:25
  29.2 0.0 collective-permute-done
  29.3 1.5 %all-to-all-done = bf16[8,4,64,128]{3,2,1,0:T(8,128)(2,1)S(1)} async-done(((bf16[8,4,64,128]{3,2,1,0:T(8,128)(2,1)}), bf16[8,4,64,128]{3,2,1,0:T(8,128)(2,1)S(1)}, u32[]{:S(2)}, u32[]{:S(2)}) %all-to-all-start) | async-done | bytes 524320 | tf_op jit(solution)/shard_map/all_to_all | solution.py:31
  30.7 0.9 broadcast_in_dim.60
  31.6 5.2 %all-to-all-start.1 = ((bf16[8,4,64,128]{3,2,1,0:T(8,128)(2,1)}), bf16[8,4,64,128]{3,2,1,0:T(8,128)(2,1)S(1)}, u32[]{:S(2)}, u32[]{:S(2)}) async-start(bf16[8,4,64,128]{3,2,1,0:T(8,128)(2,1)} %broadcast_in_dim.60), calls=%async_computation.1 | async-start | bytes 1048576 | tf_op jit(solution)/shard_map/all_to_all | solution.py:31
  36.8 0.7 fusion.32
  37.5 0.7 add_select_fusion.5
  38.2 0.1 copy.9
  38.3 0.1 eq.47
  38.5 0.7 iota_compare_fusion.3
  39.2 0.1 lt.51
  39.4 0.1 convert_reduce_fusion.1
  39.5 0.2 reduce-window.7
  39.7 3.1 %collective-permute-start.7 = (bf16[32,64,128]{2,1,0:T(8,128)(2,1)S(1)}, bf16[32,64,128]{2,1,0:T(8,128)(2,1)S(1)}, u32[]{:S(2)}, u32[]{:S(2)}) collective-permute-start(bf16[32,64,128]{2,1,0:T(8,128)(2,1)S(1)} %bitcast.44), channel_id=1, source_target_pairs={{0,8},{8,16},{16,24},{24,0},{1,9},{9,17},{17,25},{25,1},{2,10},{10... | collective-permute-start | bytes 1572872 | tf_op jit(solution)/shard_map/ppermute | solution.py:25
  42.8 9.2 %all-to-all-done.1 = bf16[8,4,64,128]{3,2,1,0:T(8,128)(2,1)S(1)} async-done(((bf16[8,4,64,128]{3,2,1,0:T(8,128)(2,1)}), bf16[8,4,64,128]{3,2,1,0:T(8,128)(2,1)S(1)}, u32[]{:S(2)}, u32[]{:S(2)}) %all-to-all-start.1) | async-done | bytes 524320 | tf_op jit(solution)/shard_map/all_to_all | solution.py:31
  52.0 4.4 %collective-permute-start.1 = (bf16[32,64,128]{2,1,0:T(8,128)(2,1)S(1)}, bf16[32,64,128]{2,1,0:T(8,128)(2,1)S(1)}, u32[]{:S(2)}, u32[]{:S(2)}) collective-permute-start(bf16[32,64,128]{2,1,0:T(8,128)(2,1)S(1)} %bitcast.47), channel_id=1, source_target_pairs={{0,24},{8,0},{16,8},{24,16},{1,25},{9,1},{17,9},{25,17},{2,26},{10... | collective-permute-start | bytes 1572872 | tf_op jit(solution)/shard_map/ppermute | solution.py:25
  56.4 0.1 copy.10
  56.5 0.1 sub.82
  56.6 0.2 fusion.3
  56.8 0.2 select_reduce_fusion
  57.0 2.5 %collective-permute-start.8 = (bf16[32,64,128]{2,1,0:T(8,128)(2,1)S(1)}, bf16[32,64,128]{2,1,0:T(8,128)(2,1)S(1)}, u32[]{:S(2)}, u32[]{:S(2)}) collective-permute-start(bf16[32,64,128]{2,1,0:T(8,128)(2,1)S(1)} %bitcast.45), channel_id=1, source_target_pairs={{0,24},{8,0},{16,8},{24,16},{1,25},{9,1},{17,9},{25,17},{2,26},{10... | collective-permute-start | bytes 1572872 | tf_op jit(solution)/shard_map/ppermute | solution.py:25
  59.5 2.8 %collective-permute-start.10 = (bf16[32,64,128]{2,1,0:T(8,128)(2,1)S(1)}, bf16[32,64,128]{2,1,0:T(8,128)(2,1)S(1)}, u32[]{:S(2)}, u32[]{:S(2)}) collective-permute-start(bf16[32,64,128]{2,1,0:T(8,128)(2,1)S(1)} %collective-permute-done.7.refs_3_), channel_id=1, source_target_pairs={{0,8},{8,16},{16,24},{24,0},{1,9},{9,17},{17,25},{25,1},{2,10},{10... | collective-permute-start | bytes 1572872 | tf_op jit(solution)/shard_map/ppermute | solution.py:25
  62.3 1.9 %collective-permute-start.9 = (bf16[32,64,128]{2,1,0:T(8,128)(2,1)S(1)}, bf16[32,64,128]{2,1,0:T(8,128)(2,1)S(1)}, u32[]{:S(2)}, u32[]{:S(2)}) collective-permute-start(bf16[32,64,128]{2,1,0:T(8,128)(2,1)S(1)} %bitcast.48), channel_id=1, source_target_pairs={{0,8},{8,16},{16,24},{24,0},{1,9},{9,17},{17,25},{25,1},{2,10},{10... | collective-permute-start | bytes 1572872 | tf_op jit(solution)/shard_map/ppermute | solution.py:25
  64.3 5.3 %collective-permute-start.2 = (bf16[32,64,128]{2,1,0:T(8,128)(2,1)S(1)}, bf16[32,64,128]{2,1,0:T(8,128)(2,1)S(1)}, u32[]{:S(2)}, u32[]{:S(2)}) collective-permute-start(bf16[32,64,128]{2,1,0:T(8,128)(2,1)S(1)} %collective-permute-done.1.refs_4_), channel_id=1, source_target_pairs={{0,24},{8,0},{16,8},{24,16},{1,25},{9,1},{17,9},{25,17},{2,26},{10... | collective-permute-start | bytes 1572872 | tf_op jit(solution)/shard_map/ppermute | solution.py:25
  69.6 10.3 %collective-permute-start.6 = (bf16[4,4,64,128]{3,2,1,0:T(8,128)(2,1)S(1)}, bf16[4,4,64,128]{3,2,1,0:T(8,128)(2,1)S(1)}, u32[]{:S(2)}, u32[]{:S(2)}) collective-permute-start(bf16[4,4,64,128]{3,2,1,0:T(8,128)(2,1)S(1)} %get-tuple-element.14), channel_id=1, source_target_pairs={{0,1},{1,0},{2,3},{3,2},{4,5},{5,4},{6,7},{7,6},{8,9},{9,8},{10,11... | collective-permute-start | bytes 786440 | tf_op jit(solution)/shard_map/ppermute | solution.py:25
  79.9 0.1 pad_add_fusion.info_ref.refs_1_
  80.0 1.1 collective-permute-done.6
  81.0 0.1 pad_maximum_fusion.own_ref
  81.1 4.9 %left_products.1 = (bf16[2,4,8,6,64,64]{5,4,3,2,1,0:T(8,128)(2,1)S(1)}, f32[8,128]{1,0:T(8,128)}) custom-call(s32[8]{0:T(128)S(1)} %pad_add_fusion.info_ref.refs_1_, bf16[2,4,4,64,128]{4,3,2,1,0:T(8,128)(2,1)S(1)} %pad_maximum_fusion.own_ref, bf16[2,4,8,6,64,64]{5,4,3,2,1,0:T(8,128)(2,1)} %bitcast.50), custom_call_target="tpu_custom_call" | custom-call | flops 201326592 | bytes 16777216 | tf_op jit(solution)/shard_map/left_products/pallas_call | solution.py:62
  86.0 3.9 %panel_sums_0.1.refs_4_ = bf16[2,4,27,16,128]{4,3,2,1,0:T(8,128)(2,1)S(1)} custom-call(s32[408]{0:T(512)S(1)} %broadcast_add_fusion.refs_0_, s32[8]{0:T(128)S(1)} %pad_add_fusion.info_ref.refs_1_, bf16[32,64,128]{2,1,0:T(8,128)(2,1)S(1)} %bitcast.46, bf16[32,64,128]{2,1,0:T(8,128)(2,1)S(1)} %collective-permute-done.7.refs_3_, ...), custom_call_target="tpu_custom_call" | custom-call | flops 100663296 | bytes 8388608 | tf_op jit(solution)/shard_map/panel_sums_0/pallas_call | solution.py:134
  89.9 4.9 %panel_sums_1.1.refs_5_ = bf16[2,4,27,16,128]{4,3,2,1,0:T(8,128)(2,1)S(1)} custom-call(s32[408]{0:T(512)S(1)} %broadcast_add_fusion.refs_0_, s32[8]{0:T(128)S(1)} %pad_add_fusion.info_ref.refs_1_, bf16[32,64,128]{2,1,0:T(8,128)(2,1)S(1)} %bitcast.49, bf16[32,64,128]{2,1,0:T(8,128)(2,1)S(1)} %collective-permute-done.9.refs_3_, ...), custom_call_target="tpu_custom_call" | custom-call | flops 134217728 | bytes 8388608 | tf_op jit(solution)/shard_map/panel_sums_1/pallas_call | solution.py:134
  94.9 2.5 %panel_sums_2.1 = bf16[2,4,27,16,128]{4,3,2,1,0:T(8,128)(2,1)S(1)} custom-call(s32[408]{0:T(512)S(1)} %broadcast_add_fusion.refs_0_, s32[8]{0:T(128)S(1)} %pad_add_fusion.info_ref.refs_1_, bf16[32,64,128]{2,1,0:T(8,128)(2,1)S(1)} %collective-permute-done.2.refs_2_, bf16[384,64,64]{2,1,0:T(8,128)(2,1)S(1)} %bitcast.43, ...), custom_call_target="tpu_custom_call" | custom-call | flops 33554432 | bytes 8388608 | tf_op jit(solution)/shard_map/panel_sums_2/pallas_call | solution.py:134
  97.4 2.8 %collective-permute-start.11 = (bf16[4,27,16,128]{3,2,1,0:T(8,128)(2,1)S(1)}, bf16[4,27,16,128]{3,2,1,0:T(8,128)(2,1)S(1)}, u32[]{:S(2)}, u32[]{:S(2)}) collective-permute-start(bf16[4,27,16,128]{3,2,1,0:T(8,128)(2,1)S(1)} %slice_bitcast_fusion), channel_id=1, source_target_pairs={{0,1},{1,0},{2,3},{3,2},{4,5},{5,4},{6,7},{7,6},{8,9},{9,8},{10,11... | collective-permute-start | bytes 1327112 | tf_op jit(solution)/shard_map/ppermute | solution.py:25
  100.2 1.4 %collective-permute-done.11 = bf16[4,27,16,128]{3,2,1,0:T(8,128)(2,1)S(1)} collective-permute-done((bf16[4,27,16,128]{3,2,1,0:T(8,128)(2,1)S(1)}, bf16[4,27,16,128]{3,2,1,0:T(8,128)(2,1)S(1)}, u32[]{:S(2)}, u32[]{:S(2)}) %collective-permute-start.11) | collective-permute-done | bytes 442400 | tf_op jit(solution)/shard_map/ppermute | solution.py:25
  101.6 0.1 fusion.4
  101.7 15.2 %all_to_all.15 = bf16[4,27,16,128]{3,2,1,0:T(8,128)(2,1)S(1)} all-to-all(bf16[4,27,16,128]{3,2,1,0:T(8,128)(2,1)S(1)} %fusion.4), channel_id=1, replica_groups=mesh['z'=8,'yh'=2,'x'=4,'yl'=4,'core'=2] {'yl'}, dimensions={0} | all-to-all | bytes 884736 | tf_op jit(solution)/shard_map/all_to_all | solution.py:196
  116.9 0.1 convert_reduce_fusion
  116.9 1.9 %collective-permute-start.12 = (bf16[27,8,128]{2,1,0:T(8,128)(2,1)S(1)}, bf16[27,8,128]{2,1,0:T(8,128)(2,1)S(1)}, u32[]{:S(2)}, u32[]{:S(2)}) collective-permute-start(bf16[27,8,128]{2,1,0:T(8,128)(2,1)S(1)} %slice.49), channel_id=1, source_target_pairs={{0,8},{8,16},{16,24},{24,32},{32,40},{40,48},{48,56},{56,64},{64,7... | collective-permute-start | bytes 165896 | tf_op jit(solution)/shard_map/ppermute | solution.py:25
  118.9 11.2 %collective-permute-done.12 = bf16[27,8,128]{2,1,0:T(8,128)(2,1)S(1)} collective-permute-done((bf16[27,8,128]{2,1,0:T(8,128)(2,1)S(1)}, bf16[27,8,128]{2,1,0:T(8,128)(2,1)S(1)}, u32[]{:S(2)}, u32[]{:S(2)}) %collective-permute-start.12) | collective-permute-done | bytes 55328 | tf_op jit(solution)/shard_map/ppermute | solution.py:25
  130.1 0.1 slice_bitcast_fusion.3
  130.2 0.7 pad_maximum_fusion.2
  (17 shorter events, 0.2 us)
Async XLA Ops:
  1.9 28.8 %all-to-all-start = ((bf16[8,4,64,128]{3,2,1,0:T(8,128)(2,1)}), bf16[8,4,64,128]{3,2,1,0:T(8,128)(2,1)S(1)}, u32[]{:S(2)}, u32[]{:S(2)}) async-start(bf16[8,4,64,128]{3,2,1,0:T(8,128)(2,1)} %broadcast_in_dim.59), calls=%async_computation | async-start | bytes 1048576 | tf_op jit(solution)/shard_map/all_to_all | solution.py:31
  12.8 16.5 %collective-permute-start = (bf16[4,64,128]{2,1,0:T(8,128)(2,1)S(1)}, bf16[4,64,128]{2,1,0:T(8,128)(2,1)S(1)}, u32[]{:S(2)}, u32[]{:S(2)}) collective-permute-start(bf16[4,64,128]{2,1,0:T(8,128)(2,1)S(1)} %pad_maximum_fusion.3), channel_id=1, source_target_pairs={{0,32},{32,0},{1,33},{33,1},{2,34},{34,2},{3,35},{35,3},{4,36},{36... | collective-permute-start | bytes 196616 | tf_op jit(solution)/shard_map/ppermute | solution.py:25
  20.2 36.8 %collective-permute-start.3 = (bf16[4,64,128]{2,1,0:T(8,128)(2,1)S(1)}, bf16[4,64,128]{2,1,0:T(8,128)(2,1)S(1)}, u32[]{:S(2)}, u32[]{:S(2)}) collective-permute-start(bf16[4,64,128]{2,1,0:T(8,128)(2,1)S(1)} %pad_maximum_fusion.3), channel_id=1, source_target_pairs={{0,2},{2,4},{4,6},{6,0},{1,3},{3,5},{5,7},{7,1},{8,10},{10,12},{12... | collective-permute-start | bytes 196616 | tf_op jit(solution)/shard_map/ppermute | solution.py:25
  22.5 39.8 %collective-permute-start.4 = (bf16[4,64,128]{2,1,0:T(8,128)(2,1)S(1)}, bf16[4,64,128]{2,1,0:T(8,128)(2,1)S(1)}, u32[]{:S(2)}, u32[]{:S(2)}) collective-permute-start(bf16[4,64,128]{2,1,0:T(8,128)(2,1)S(1)} %pad_maximum_fusion.3), channel_id=1, source_target_pairs={{0,4},{2,6},{4,0},{6,2},{1,5},{3,7},{5,1},{7,3},{8,12},{10,14},{12... | collective-permute-start | bytes 196616 | tf_op jit(solution)/shard_map/ppermute | solution.py:25
  25.0 44.6 %collective-permute-start.5 = (bf16[4,64,128]{2,1,0:T(8,128)(2,1)S(1)}, bf16[4,64,128]{2,1,0:T(8,128)(2,1)S(1)}, u32[]{:S(2)}, u32[]{:S(2)}) collective-permute-start(bf16[4,64,128]{2,1,0:T(8,128)(2,1)S(1)} %pad_maximum_fusion.3), channel_id=1, source_target_pairs={{0,6},{2,0},{4,2},{6,4},{1,7},{3,1},{5,3},{7,5},{8,14},{10,8},{12,... | collective-permute-start | bytes 196616 | tf_op jit(solution)/shard_map/ppermute | solution.py:25
  31.6 20.3 %all-to-all-start.1 = ((bf16[8,4,64,128]{3,2,1,0:T(8,128)(2,1)}), bf16[8,4,64,128]{3,2,1,0:T(8,128)(2,1)S(1)}, u32[]{:S(2)}, u32[]{:S(2)}) async-start(bf16[8,4,64,128]{3,2,1,0:T(8,128)(2,1)} %broadcast_in_dim.60), calls=%async_computation.1 | async-start | bytes 1048576 | tf_op jit(solution)/shard_map/all_to_all | solution.py:31
  39.7 19.8 %collective-permute-start.7 = (bf16[32,64,128]{2,1,0:T(8,128)(2,1)S(1)}, bf16[32,64,128]{2,1,0:T(8,128)(2,1)S(1)}, u32[]{:S(2)}, u32[]{:S(2)}) collective-permute-start(bf16[32,64,128]{2,1,0:T(8,128)(2,1)S(1)} %bitcast.44), channel_id=1, source_target_pairs={{0,8},{8,16},{16,24},{24,0},{1,9},{9,17},{17,25},{25,1},{2,10},{10... | collective-permute-start | bytes 1572872 | tf_op jit(solution)/shard_map/ppermute | solution.py:25
  52.0 12.3 %collective-permute-start.1 = (bf16[32,64,128]{2,1,0:T(8,128)(2,1)S(1)}, bf16[32,64,128]{2,1,0:T(8,128)(2,1)S(1)}, u32[]{:S(2)}, u32[]{:S(2)}) collective-permute-start(bf16[32,64,128]{2,1,0:T(8,128)(2,1)S(1)} %bitcast.47), channel_id=1, source_target_pairs={{0,24},{8,0},{16,8},{24,16},{1,25},{9,1},{17,9},{25,17},{2,26},{10... | collective-permute-start | bytes 1572872 | tf_op jit(solution)/shard_map/ppermute | solution.py:25
  57.0 29.0 %collective-permute-start.8 = (bf16[32,64,128]{2,1,0:T(8,128)(2,1)S(1)}, bf16[32,64,128]{2,1,0:T(8,128)(2,1)S(1)}, u32[]{:S(2)}, u32[]{:S(2)}) collective-permute-start(bf16[32,64,128]{2,1,0:T(8,128)(2,1)S(1)} %bitcast.45), channel_id=1, source_target_pairs={{0,24},{8,0},{16,8},{24,16},{1,25},{9,1},{17,9},{25,17},{2,26},{10... | collective-permute-start | bytes 1572872 | tf_op jit(solution)/shard_map/ppermute | solution.py:25
  59.5 30.4 %collective-permute-start.10 = (bf16[32,64,128]{2,1,0:T(8,128)(2,1)S(1)}, bf16[32,64,128]{2,1,0:T(8,128)(2,1)S(1)}, u32[]{:S(2)}, u32[]{:S(2)}) collective-permute-start(bf16[32,64,128]{2,1,0:T(8,128)(2,1)S(1)} %collective-permute-done.7.refs_3_), channel_id=1, source_target_pairs={{0,8},{8,16},{16,24},{24,0},{1,9},{9,17},{17,25},{25,1},{2,10},{10... | collective-permute-start | bytes 1572872 | tf_op jit(solution)/shard_map/ppermute | solution.py:25
  62.3 27.6 %collective-permute-start.9 = (bf16[32,64,128]{2,1,0:T(8,128)(2,1)S(1)}, bf16[32,64,128]{2,1,0:T(8,128)(2,1)S(1)}, u32[]{:S(2)}, u32[]{:S(2)}) collective-permute-start(bf16[32,64,128]{2,1,0:T(8,128)(2,1)S(1)} %bitcast.48), channel_id=1, source_target_pairs={{0,8},{8,16},{16,24},{24,0},{1,9},{9,17},{17,25},{25,1},{2,10},{10... | collective-permute-start | bytes 1572872 | tf_op jit(solution)/shard_map/ppermute | solution.py:25
  64.3 30.6 %collective-permute-start.2 = (bf16[32,64,128]{2,1,0:T(8,128)(2,1)S(1)}, bf16[32,64,128]{2,1,0:T(8,128)(2,1)S(1)}, u32[]{:S(2)}, u32[]{:S(2)}) collective-permute-start(bf16[32,64,128]{2,1,0:T(8,128)(2,1)S(1)} %collective-permute-done.1.refs_4_), channel_id=1, source_target_pairs={{0,24},{8,0},{16,8},{24,16},{1,25},{9,1},{17,9},{25,17},{2,26},{10... | collective-permute-start | bytes 1572872 | tf_op jit(solution)/shard_map/ppermute | solution.py:25
  69.6 11.4 %collective-permute-start.6 = (bf16[4,4,64,128]{3,2,1,0:T(8,128)(2,1)S(1)}, bf16[4,4,64,128]{3,2,1,0:T(8,128)(2,1)S(1)}, u32[]{:S(2)}, u32[]{:S(2)}) collective-permute-start(bf16[4,4,64,128]{3,2,1,0:T(8,128)(2,1)S(1)} %get-tuple-element.14), channel_id=1, source_target_pairs={{0,1},{1,0},{2,3},{3,2},{4,5},{5,4},{6,7},{7,6},{8,9},{9,8},{10,11... | collective-permute-start | bytes 786440 | tf_op jit(solution)/shard_map/ppermute | solution.py:25
  97.4 4.2 %collective-permute-start.11 = (bf16[4,27,16,128]{3,2,1,0:T(8,128)(2,1)S(1)}, bf16[4,27,16,128]{3,2,1,0:T(8,128)(2,1)S(1)}, u32[]{:S(2)}, u32[]{:S(2)}) collective-permute-start(bf16[4,27,16,128]{3,2,1,0:T(8,128)(2,1)S(1)} %slice_bitcast_fusion), channel_id=1, source_target_pairs={{0,1},{1,0},{2,3},{3,2},{4,5},{5,4},{6,7},{7,6},{8,9},{9,8},{10,11... | collective-permute-start | bytes 1327112 | tf_op jit(solution)/shard_map/ppermute | solution.py:25
  116.9 13.1 %collective-permute-start.12 = (bf16[27,8,128]{2,1,0:T(8,128)(2,1)S(1)}, bf16[27,8,128]{2,1,0:T(8,128)(2,1)S(1)}, u32[]{:S(2)}, u32[]{:S(2)}) collective-permute-start(bf16[27,8,128]{2,1,0:T(8,128)(2,1)S(1)} %slice.49), channel_id=1, source_target_pairs={{0,8},{8,16},{16,24},{24,32},{32,40},{40,48},{48,56},{56,64},{64,7... | collective-permute-start | bytes 165896 | tf_op jit(solution)/shard_map/ppermute | solution.py:25

commit v5 on v4

--- a/solution.py
+++ b/solution.py
@@ -33,7 +33,7 @@
 
 def left_kernel(info_ref, own_ref, a_ref, b_ref, done_ref, a_here, sems):
     core, yl = info_ref[6], info_ref[7]
-    done_ref[...] = jnp.zeros(done_ref.shape, F32)
+    done_ref[...] = jnp.zeros(done_ref.shape, I32)
 
     def fetch(v, h):
         return pltpu.make_async_copy(a_ref.at[h, v], a_here.at[v, h], sems.at[v, h])
@@ -63,9 +63,9 @@
         left_kernel,
         in_specs=[pl.BlockSpec(memory_space=pltpu.SMEM), vmem, pl.BlockSpec(memory_space=pltpu.HBM)],
         out_specs=[vmem, vmem],
-        out_shape=[jax.ShapeDtypeStruct(a.shape, BF16), jax.ShapeDtypeStruct((8, 2 * T), F32)],
+        out_shape=[jax.ShapeDtypeStruct(a.shape, BF16), jax.ShapeDtypeStruct((8, 2 * T), I32)],
         scratch_shapes=[pltpu.VMEM((4, 2, 8, slots, T, T), BF16), pltpu.SemaphoreType.DMA((4, 2))],
-        compiler_params=pltpu.CompilerParams(vmem_limit_bytes=46 * MIB),
+        compiler_params=pltpu.CompilerParams(vmem_limit_bytes=48 * MIB),
         cost_estimate=pl.CostEstimate(flops=2 * rows * slots * T**3, bytes_accessed=16 * MIB, transcendentals=0),
         name="left_products",
     )(info, own, a)
@@ -141,7 +141,7 @@
             pltpu.VMEM((2 * KC + 1, T, 2 * T), F32),
             pltpu.SemaphoreType.DMA((len(chunks),)),
         ],
-        compiler_params=pltpu.CompilerParams(vmem_limit_bytes=24 * MIB),
+        compiler_params=pltpu.CompilerParams(vmem_limit_bytes=14 * MIB),
         cost_estimate=pl.CostEstimate(flops=pairs * 2**20, bytes_accessed=8 * MIB, transcendentals=0),
         name=f"panel_sums_{group}",
     )(code, info, *chunks, b, *before)
@@ -185,7 +185,8 @@
     info = jnp.concatenate([first, steps, jnp.stack([core, yl])]).astype(I32)
 
     b, done = left_products(info, own, a_tiles)
-    other, _ = lax.optimization_barrier((other, done))
+    other, left_a, right_a, done = lax.optimization_barrier((other, left_a, right_a, done))
+    info = info + done[0, :info.shape[0]]
     left_b, right_b = shifted(other, "x", 1), shifted(other, "x", -1)
     left2, right2 = shifted(left_a, "x", 1), shifted(right_b, "x", -1)
     sums0 = panel_sums(0, code, info, [near, left_a, right_a], b)

time: 132 us -> 136 us (1.030)
  starting transfers between devices: 67.5 us -> 63 us
  Pallas kernels: 16.2 us -> 19.4 us
  local copies, waits for them, and re-layouts: 3.45 us -> 6.25 us
    ppermute x13, waiting for transfers between devices: 13.7 us -> 25.4 us  [shifted(): lax.ppermute(value, axis, [(i, (i + by) % count) for i in range(count)])]
    all_to_all x2, waiting for transfers between devices: 10.6 us -> 0.01 us  [spread(): return lax.all_to_all(copies, axis, 0, 0, tiled=True)]
    ppermute x13, starting transfers between devices: 51.4 us -> 45.5 us  [shifted(): lax.ppermute(value, axis, [(i, (i + by) % count) for i in range(count)])]
    unnamed x0 -> x2, local copies, waits for them, and re-layouts: none -> 2.78 us
    pallas_call x1, Pallas kernels: 4.93 us -> 7.13 us  [left_products(): pl.pallas_call(left_kernel, in_specs=[pl.BlockSpec(memory_space=pltpu.SME...]
    all_to_all x2, starting transfers between devices: 16.1 us -> 17.5 us  [spread(): return lax.all_to_all(copies, axis, 0, 0, tiled=True)]
  transfers between devices with their start and end apart: 15 -> 15, of which waited for: 5 -> 6; matrix products, arithmetic and copies ran while one was open for 3% -> 3% of each run, Pallas kernels for 10% -> 12%
where the time goes in v5:
time: 136 us; the launch traced here: 135 us
  starting transfers between devices  63 us (46%)
  waiting for transfers between devices  25.4 us (19%)
  Pallas kernels  19.4 us (14%)
  blocking collectives  16.5 us (12%)
  local copies, waits for them, and re-layouts  6.25 us (5%)
  other arithmetic  3.79 us (3%)
    ppermute x13, starting transfers between devices, shifted(): lax.ppermute(value, axis, [(i, (i + by) % count) for i in range(count)])  45.5 us
    ppermute x13, waiting for transfers between devices, shifted(): lax.ppermute(value, axis, [(i, (i + by) % count) for i in range(count)])  25.4 us
    all_to_all x2, starting transfers between devices, spread(): return lax.all_to_all(copies, axis, 0, 0, tiled=True)  17.5 us
    all_to_all x1, blocking collectives, body(): lax.all_to_all(chip, 'yl', 0, 0, tiled=True).astype(F32)  16.5 us
    pallas_call x3, Pallas kernels, panel_sums(): pl.pallas_call(functools.partial(sum_kernel, group, len(chunks), len(befo...  12.2 us
    pallas_call x1, Pallas kernels, left_products(): pl.pallas_call(left_kernel, in_specs=[pl.BlockSpec(memory_space=pltpu.SME...  7.13 us
    unnamed x2, local copies, waits for them, and re-layouts  2.78 us
  transfers between devices with their start and end apart: 15, of which 6 were waited for; matrix products, arithmetic and copies ran while one was open for 3% of the time, Pallas kernels for 12%

profile of v5, /device:TPU:1, one launch (start us, length us, event | category | flops | bytes accessed | tf_op | source)
XLA Modules:
  0.0 134.7 jit_solution(3275498659253018675)
XLA Ops:
  0.0 0.9 slice_bitcast_fusion.5
  0.9 0.1 pad_maximum_fusion.3
  1.0 0.9 broadcast_in_dim.59
  1.9 10.9 %all-to-all-start = ((bf16[8,4,64,128]{3,2,1,0:T(8,128)(2,1)}), bf16[8,4,64,128]{3,2,1,0:T(8,128)(2,1)S(1)}, u32[]{:S(2)}, u32[]{:S(2)}) async-start(bf16[8,4,64,128]{3,2,1,0:T(8,128)(2,1)} %broadcast_in_dim.59), calls=%async_computation | async-start | bytes 1048576 | tf_op jit(solution)/shard_map/all_to_all | solution.py:31
  12.8 5.2 %collective-permute-start.5 = (bf16[4,64,128]{2,1,0:T(8,128)(2,1)S(1)}, bf16[4,64,128]{2,1,0:T(8,128)(2,1)S(1)}, u32[]{:S(2)}, u32[]{:S(2)}) collective-permute-start(bf16[4,64,128]{2,1,0:T(8,128)(2,1)S(1)} %pad_maximum_fusion.3), channel_id=1, source_target_pairs={{0,6},{2,0},{4,2},{6,4},{1,7},{3,1},{5,3},{7,5},{8,14},{10,8},{12,... | collective-permute-start | bytes 196616 | tf_op jit(solution)/shard_map/ppermute | solution.py:25
  18.0 1.9 %collective-permute-start.4 = (bf16[4,64,128]{2,1,0:T(8,128)(2,1)S(1)}, bf16[4,64,128]{2,1,0:T(8,128)(2,1)S(1)}, u32[]{:S(2)}, u32[]{:S(2)}) collective-permute-start(bf16[4,64,128]{2,1,0:T(8,128)(2,1)S(1)} %pad_maximum_fusion.3), channel_id=1, source_target_pairs={{0,4},{2,6},{4,0},{6,2},{1,5},{3,7},{5,1},{7,3},{8,12},{10,14},{12... | collective-permute-start | bytes 196616 | tf_op jit(solution)/shard_map/ppermute | solution.py:25
  19.9 2.3 %collective-permute-start.3 = (bf16[4,64,128]{2,1,0:T(8,128)(2,1)S(1)}, bf16[4,64,128]{2,1,0:T(8,128)(2,1)S(1)}, u32[]{:S(2)}, u32[]{:S(2)}) collective-permute-start(bf16[4,64,128]{2,1,0:T(8,128)(2,1)S(1)} %pad_maximum_fusion.3), channel_id=1, source_target_pairs={{0,2},{2,4},{4,6},{6,0},{1,3},{3,5},{5,7},{7,1},{8,10},{10,12},{12... | collective-permute-start | bytes 196616 | tf_op jit(solution)/shard_map/ppermute | solution.py:25
  22.3 5.7 %collective-permute-start = (bf16[4,64,128]{2,1,0:T(8,128)(2,1)S(1)}, bf16[4,64,128]{2,1,0:T(8,128)(2,1)S(1)}, u32[]{:S(2)}, u32[]{:S(2)}) collective-permute-start(bf16[4,64,128]{2,1,0:T(8,128)(2,1)S(1)} %pad_maximum_fusion.3), channel_id=1, source_target_pairs={{0,32},{32,0},{1,33},{33,1},{2,34},{34,2},{3,35},{35,3},{4,36},{36... | collective-permute-start | bytes 196616 | tf_op jit(solution)/shard_map/ppermute | solution.py:25
  27.9 0.7 fusion.32
  28.6 0.7 add_select_fusion.5
  29.3 0.7 iota_compare_fusion.3
  30.1 0.1 lt.51
  30.2 0.1 copy.9
  30.3 0.1 eq.47
  30.5 0.8 collective-permute-done
  31.3 0.9 broadcast_in_dim.60
  32.2 6.6 %all-to-all-start.1 = ((bf16[8,4,64,128]{3,2,1,0:T(8,128)(2,1)}), bf16[8,4,64,128]{3,2,1,0:T(8,128)(2,1)S(1)}, u32[]{:S(2)}, u32[]{:S(2)}) async-start(bf16[8,4,64,128]{3,2,1,0:T(8,128)(2,1)} %broadcast_in_dim.60), calls=%async_computation.1 | async-start | bytes 1048576 | tf_op jit(solution)/shard_map/all_to_all | solution.py:31
  38.9 0.1 convert_reduce_fusion.1
  39.0 0.2 reduce-window.7
  39.2 4.4 %collective-permute-start.2 = (bf16[32,64,128]{2,1,0:T(8,128)(2,1)S(1)}, bf16[32,64,128]{2,1,0:T(8,128)(2,1)S(1)}, u32[]{:S(2)}, u32[]{:S(2)}) collective-permute-start(bf16[32,64,128]{2,1,0:T(8,128)(2,1)S(1)} %bitcast.46), channel_id=1, source_target_pairs={{0,24},{8,0},{16,8},{24,16},{1,25},{9,1},{17,9},{25,17},{2,26},{10... | collective-permute-start | bytes 1572872 | tf_op jit(solution)/shard_map/ppermute | solution.py:25
  43.6 1.9 %collective-permute-start.1 = (bf16[32,64,128]{2,1,0:T(8,128)(2,1)S(1)}, bf16[32,64,128]{2,1,0:T(8,128)(2,1)S(1)}, u32[]{:S(2)}, u32[]{:S(2)}) collective-permute-start(bf16[32,64,128]{2,1,0:T(8,128)(2,1)S(1)} %bitcast.47), channel_id=1, source_target_pairs={{0,8},{8,16},{16,24},{24,0},{1,9},{9,17},{17,25},{25,1},{2,10},{10... | collective-permute-start | bytes 1572872 | tf_op jit(solution)/shard_map/ppermute | solution.py:25
  45.6 5.7 %collective-permute-start.6 = (bf16[4,4,64,128]{3,2,1,0:T(8,128)(2,1)S(1)}, bf16[4,4,64,128]{3,2,1,0:T(8,128)(2,1)S(1)}, u32[]{:S(2)}, u32[]{:S(2)}) collective-permute-start(bf16[4,4,64,128]{3,2,1,0:T(8,128)(2,1)S(1)} %get-tuple-element.24), channel_id=1, source_target_pairs={{0,1},{1,0},{2,3},{3,2},{4,5},{5,4},{6,7},{7,6},{8,9},{9,8},{10,11... | collective-permute-start | bytes 786440 | tf_op jit(solution)/shard_map/ppermute | solution.py:25
  51.3 0.1 pad_add_fusion.info_ref
  51.4 1.0 collective-permute-done.6
  52.5 7.1 %left_products.1 = (bf16[2,4,8,6,64,64]{5,4,3,2,1,0:T(8,128)(2,1)}, s32[8,128]{1,0:T(8,128)S(1)}) custom-call(s32[8]{0:T(128)S(1)} %pad_add_fusion.info_ref, bf16[2,4,4,64,128]{4,3,2,1,0:T(8,128)(2,1)S(1)} %pad_maximum_fusion.own_ref, bf16[2,4,8,6,64,64]{5,4,3,2,1,0:T(8,128)(2,1)} %bitcast.52), custom_call_target="tpu_custom_call" | custom-call | flops 201326592 | bytes 16777216 | tf_op jit(solution)/shard_map/left_products/pallas_call | solution.py:62
  59.7 4.9 %collective-permute-start.7 = (bf16[32,64,128]{2,1,0:T(8,128)(2,1)S(1)}, bf16[32,64,128]{2,1,0:T(8,128)(2,1)S(1)}, u32[]{:S(2)}, u32[]{:S(2)}) collective-permute-start(bf16[32,64,128]{2,1,0:T(8,128)(2,1)S(1)} %bitcast.49), channel_id=1, source_target_pairs={{0,24},{8,0},{16,8},{24,16},{1,25},{9,1},{17,9},{25,17},{2,26},{10... | collective-permute-start | bytes 1572872 | tf_op jit(solution)/shard_map/ppermute | solution.py:25
  64.5 0.1 copy.10
  64.6 0.1 sub.82
  64.8 0.2 fusion.3
  65.0 1.9 %collective-permute-start.9 = (bf16[32,64,128]{2,1,0:T(8,128)(2,1)S(1)}, bf16[32,64,128]{2,1,0:T(8,128)(2,1)S(1)}, u32[]{:S(2)}, u32[]{:S(2)}) collective-permute-start(bf16[32,64,128]{2,1,0:T(8,128)(2,1)S(1)} %bitcast.50), channel_id=1, source_target_pairs={{0,8},{8,16},{16,24},{24,0},{1,9},{9,17},{17,25},{25,1},{2,10},{10... | collective-permute-start | bytes 1572872 | tf_op jit(solution)/shard_map/ppermute | solution.py:25
  66.9 1.9 %collective-permute-start.10 = (bf16[32,64,128]{2,1,0:T(8,128)(2,1)S(1)}, bf16[32,64,128]{2,1,0:T(8,128)(2,1)S(1)}, u32[]{:S(2)}, u32[]{:S(2)}) collective-permute-start(bf16[32,64,128]{2,1,0:T(8,128)(2,1)S(1)} %collective-permute-done.1.refs_3_), channel_id=1, source_target_pairs={{0,8},{8,16},{16,24},{24,0},{1,9},{9,17},{17,25},{25,1},{2,10},{10... | collective-permute-start | bytes 1572872 | tf_op jit(solution)/shard_map/ppermute | solution.py:25
  68.8 6.6 %collective-permute-done.7.refs_4_ = bf16[32,64,128]{2,1,0:T(8,128)(2,1)S(1)} collective-permute-done((bf16[32,64,128]{2,1,0:T(8,128)(2,1)S(1)}, bf16[32,64,128]{2,1,0:T(8,128)(2,1)S(1)}, u32[]{:S(2)}, u32[]{:S(2)}) %collective-permute-start.7) | collective-permute-done | bytes 524320 | tf_op jit(solution)/shard_map/ppermute | solution.py:25
  75.4 5.3 %collective-permute-start.8 = (bf16[32,64,128]{2,1,0:T(8,128)(2,1)S(1)}, bf16[32,64,128]{2,1,0:T(8,128)(2,1)S(1)}, u32[]{:S(2)}, u32[]{:S(2)}) collective-permute-start(bf16[32,64,128]{2,1,0:T(8,128)(2,1)S(1)} %collective-permute-done.7.refs_4_), channel_id=1, source_target_pairs={{0,24},{8,0},{16,8},{24,16},{1,25},{9,1},{17,9},{25,17},{2,26},{10... | collective-permute-start | bytes 1572872 | tf_op jit(solution)/shard_map/ppermute | solution.py:25
  80.7 0.2 select_reduce_fusion
  80.9 2.8 %copy-done = bf16[2,4,8,6,64,64]{5,4,3,2,1,0:T(8,128)(2,1)S(1)} copy-done((bf16[2,4,8,6,64,64]{5,4,3,2,1,0:T(8,128)(2,1)S(1)}, bf16[2,4,8,6,64,64]{5,4,3,2,1,0:T(8,128)(2,1)}, u32[]{:S(2)}) %copy-start) | copy-done | bytes 3145752
  83.7 4.1 %panel_sums_0.1.refs_4_ = bf16[2,4,27,16,128]{4,3,2,1,0:T(8,128)(2,1)S(1)} custom-call(s32[408]{0:T(512)S(1)} %broadcast_add_fusion.refs_0_, s32[8]{0:T(128)S(1)} %bitcast_add_fusion.refs_1_, bf16[32,64,128]{2,1,0:T(8,128)(2,1)S(1)} %bitcast.48, bf16[32,64,128]{2,1,0:T(8,128)(2,1)S(1)} %collective-permute-done.1.refs_3_, ...), custom_call_target="tpu_custom_call" | custom-call | flops 100663296 | bytes 8388608 | tf_op jit(solution)/shard_map/panel_sums_0/pallas_call | solution.py:134
  87.8 4.3 %collective-permute-done.10.refs_5_ = bf16[32,64,128]{2,1,0:T(8,128)(2,1)S(1)} collective-permute-done((bf16[32,64,128]{2,1,0:T(8,128)(2,1)S(1)}, bf16[32,64,128]{2,1,0:T(8,128)(2,1)S(1)}, u32[]{:S(2)}, u32[]{:S(2)}) %collective-permute-start.10) | collective-permute-done | bytes 524320 | tf_op jit(solution)/shard_map/ppermute | solution.py:25
  92.1 5.2 %panel_sums_1.1.refs_5_ = bf16[2,4,27,16,128]{4,3,2,1,0:T(8,128)(2,1)S(1)} custom-call(s32[408]{0:T(512)S(1)} %broadcast_add_fusion.refs_0_, s32[8]{0:T(128)S(1)} %bitcast_add_fusion.refs_1_, bf16[32,64,128]{2,1,0:T(8,128)(2,1)S(1)} %bitcast.51, bf16[32,64,128]{2,1,0:T(8,128)(2,1)S(1)} %collective-permute-done.9.refs_3_, ...), custom_call_target="tpu_custom_call" | custom-call | flops 134217728 | bytes 8388608 | tf_op jit(solution)/shard_map/panel_sums_1/pallas_call | solution.py:134
  97.3 3.0 %panel_sums_2.1 = bf16[2,4,27,16,128]{4,3,2,1,0:T(8,128)(2,1)S(1)} custom-call(s32[408]{0:T(512)S(1)} %broadcast_add_fusion.refs_0_, s32[8]{0:T(128)S(1)} %bitcast_add_fusion.refs_1_, bf16[32,64,128]{2,1,0:T(8,128)(2,1)S(1)} %collective-permute-done.8.refs_2_, bf16[384,64,64]{2,1,0:T(8,128)(2,1)S(1)} %bitcast.45, ...), custom_call_target="tpu_custom_call" | custom-call | flops 33554432 | bytes 8388608 | tf_op jit(solution)/shard_map/panel_sums_2/pallas_call | solution.py:134
  100.3 2.4 %collective-permute-start.11 = (bf16[4,27,16,128]{3,2,1,0:T(8,128)(2,1)S(1)}, bf16[4,27,16,128]{3,2,1,0:T(8,128)(2,1)S(1)}, u32[]{:S(2)}, u32[]{:S(2)}) collective-permute-start(bf16[4,27,16,128]{3,2,1,0:T(8,128)(2,1)S(1)} %slice_bitcast_fusion), channel_id=1, source_target_pairs={{0,1},{1,0},{2,3},{3,2},{4,5},{5,4},{6,7},{7,6},{8,9},{9,8},{10,11... | collective-permute-start | bytes 1327112 | tf_op jit(solution)/shard_map/ppermute | solution.py:25
  102.7 1.4 %collective-permute-done.11 = bf16[4,27,16,128]{3,2,1,0:T(8,128)(2,1)S(1)} collective-permute-done((bf16[4,27,16,128]{3,2,1,0:T(8,128)(2,1)S(1)}, bf16[4,27,16,128]{3,2,1,0:T(8,128)(2,1)S(1)}, u32[]{:S(2)}, u32[]{:S(2)}) %collective-permute-start.11) | collective-permute-done | bytes 442400 | tf_op jit(solution)/shard_map/ppermute | solution.py:25
  104.1 0.1 fusion.4
  104.3 16.5 %all_to_all.15 = bf16[4,27,16,128]{3,2,1,0:T(8,128)(2,1)S(1)} all-to-all(bf16[4,27,16,128]{3,2,1,0:T(8,128)(2,1)S(1)} %fusion.4), channel_id=1, replica_groups=mesh['z'=8,'yh'=2,'x'=4,'yl'=4,'core'=2] {'yl'}, dimensions={0} | all-to-all | bytes 884736 | tf_op jit(solution)/shard_map/all_to_all | solution.py:197
  120.7 0.1 convert_reduce_fusion
  120.8 1.9 %collective-permute-start.12 = (bf16[27,8,128]{2,1,0:T(8,128)(2,1)S(1)}, bf16[27,8,128]{2,1,0:T(8,128)(2,1)S(1)}, u32[]{:S(2)}, u32[]{:S(2)}) collective-permute-start(bf16[27,8,128]{2,1,0:T(8,128)(2,1)S(1)} %slice.54), channel_id=1, source_target_pairs={{0,8},{8,16},{16,24},{24,32},{32,40},{40,48},{48,56},{56,64},{64,7... | collective-permute-start | bytes 165896 | tf_op jit(solution)/shard_map/ppermute | solution.py:25
  122.7 11.2 %collective-permute-done.12 = bf16[27,8,128]{2,1,0:T(8,128)(2,1)S(1)} collective-permute-done((bf16[27,8,128]{2,1,0:T(8,128)(2,1)S(1)}, bf16[27,8,128]{2,1,0:T(8,128)(2,1)S(1)}, u32[]{:S(2)}, u32[]{:S(2)}) %collective-permute-start.12) | collective-permute-done | bytes 55328 | tf_op jit(solution)/shard_map/ppermute | solution.py:25
  133.9 0.1 slice_bitcast_fusion.3
  134.0 0.7 pad_maximum_fusion.2
  (20 shorter events, 0.2 us)
Async XLA Ops:
  1.9 29.4 %all-to-all-start = ((bf16[8,4,64,128]{3,2,1,0:T(8,128)(2,1)}), bf16[8,4,64,128]{3,2,1,0:T(8,128)(2,1)S(1)}, u32[]{:S(2)}, u32[]{:S(2)}) async-start(bf16[8,4,64,128]{3,2,1,0:T(8,128)(2,1)} %broadcast_in_dim.59), calls=%async_computation | async-start | bytes 1048576 | tf_op jit(solution)/shard_map/all_to_all | solution.py:31
  12.8 32.7 %collective-permute-start.5 = (bf16[4,64,128]{2,1,0:T(8,128)(2,1)S(1)}, bf16[4,64,128]{2,1,0:T(8,128)(2,1)S(1)}, u32[]{:S(2)}, u32[]{:S(2)}) collective-permute-start(bf16[4,64,128]{2,1,0:T(8,128)(2,1)S(1)} %pad_maximum_fusion.3), channel_id=1, source_target_pairs={{0,6},{2,0},{4,2},{6,4},{1,7},{3,1},{5,3},{7,5},{8,14},{10,8},{12,... | collective-permute-start | bytes 196616 | tf_op jit(solution)/shard_map/ppermute | solution.py:25
  18.0 27.5 %collective-permute-start.4 = (bf16[4,64,128]{2,1,0:T(8,128)(2,1)S(1)}, bf16[4,64,128]{2,1,0:T(8,128)(2,1)S(1)}, u32[]{:S(2)}, u32[]{:S(2)}) collective-permute-start(bf16[4,64,128]{2,1,0:T(8,128)(2,1)S(1)} %pad_maximum_fusion.3), channel_id=1, source_target_pairs={{0,4},{2,6},{4,0},{6,2},{1,5},{3,7},{5,1},{7,3},{8,12},{10,14},{12... | collective-permute-start | bytes 196616 | tf_op jit(solution)/shard_map/ppermute | solution.py:25
  19.9 25.6 %collective-permute-start.3 = (bf16[4,64,128]{2,1,0:T(8,128)(2,1)S(1)}, bf16[4,64,128]{2,1,0:T(8,128)(2,1)S(1)}, u32[]{:S(2)}, u32[]{:S(2)}) collective-permute-start(bf16[4,64,128]{2,1,0:T(8,128)(2,1)S(1)} %pad_maximum_fusion.3), channel_id=1, source_target_pairs={{0,2},{2,4},{4,6},{6,0},{1,3},{3,5},{5,7},{7,1},{8,10},{10,12},{12... | collective-permute-start | bytes 196616 | tf_op jit(solution)/shard_map/ppermute | solution.py:25
  22.3 9.0 %collective-permute-start = (bf16[4,64,128]{2,1,0:T(8,128)(2,1)S(1)}, bf16[4,64,128]{2,1,0:T(8,128)(2,1)S(1)}, u32[]{:S(2)}, u32[]{:S(2)}) collective-permute-start(bf16[4,64,128]{2,1,0:T(8,128)(2,1)S(1)} %pad_maximum_fusion.3), channel_id=1, source_target_pairs={{0,32},{32,0},{1,33},{33,1},{2,34},{34,2},{3,35},{35,3},{4,36},{36... | collective-permute-start | bytes 196616 | tf_op jit(solution)/shard_map/ppermute | solution.py:25
  32.2 27.4 %all-to-all-start.1 = ((bf16[8,4,64,128]{3,2,1,0:T(8,128)(2,1)}), bf16[8,4,64,128]{3,2,1,0:T(8,128)(2,1)S(1)}, u32[]{:S(2)}, u32[]{:S(2)}) async-start(bf16[8,4,64,128]{3,2,1,0:T(8,128)(2,1)} %broadcast_in_dim.60), calls=%async_computation.1 | async-start | bytes 1048576 | tf_op jit(solution)/shard_map/all_to_all | solution.py:31
  39.2 20.4 %collective-permute-start.2 = (bf16[32,64,128]{2,1,0:T(8,128)(2,1)S(1)}, bf16[32,64,128]{2,1,0:T(8,128)(2,1)S(1)}, u32[]{:S(2)}, u32[]{:S(2)}) collective-permute-start(bf16[32,64,128]{2,1,0:T(8,128)(2,1)S(1)} %bitcast.46), channel_id=1, source_target_pairs={{0,24},{8,0},{16,8},{24,16},{1,25},{9,1},{17,9},{25,17},{2,26},{10... | collective-permute-start | bytes 1572872 | tf_op jit(solution)/shard_map/ppermute | solution.py:25
  43.6 16.1 %collective-permute-start.1 = (bf16[32,64,128]{2,1,0:T(8,128)(2,1)S(1)}, bf16[32,64,128]{2,1,0:T(8,128)(2,1)S(1)}, u32[]{:S(2)}, u32[]{:S(2)}) collective-permute-start(bf16[32,64,128]{2,1,0:T(8,128)(2,1)S(1)} %bitcast.47), channel_id=1, source_target_pairs={{0,8},{8,16},{16,24},{24,0},{1,9},{9,17},{17,25},{25,1},{2,10},{10... | collective-permute-start | bytes 1572872 | tf_op jit(solution)/shard_map/ppermute | solution.py:25
  45.6 6.8 %collective-permute-start.6 = (bf16[4,4,64,128]{3,2,1,0:T(8,128)(2,1)S(1)}, bf16[4,4,64,128]{3,2,1,0:T(8,128)(2,1)S(1)}, u32[]{:S(2)}, u32[]{:S(2)}) collective-permute-start(bf16[4,4,64,128]{3,2,1,0:T(8,128)(2,1)S(1)} %get-tuple-element.24), channel_id=1, source_target_pairs={{0,1},{1,0},{2,3},{3,2},{4,5},{5,4},{6,7},{7,6},{8,9},{9,8},{10,11... | collective-permute-start | bytes 786440 | tf_op jit(solution)/shard_map/ppermute | solution.py:25
  59.7 15.8 %collective-permute-start.7 = (bf16[32,64,128]{2,1,0:T(8,128)(2,1)S(1)}, bf16[32,64,128]{2,1,0:T(8,128)(2,1)S(1)}, u32[]{:S(2)}, u32[]{:S(2)}) collective-permute-start(bf16[32,64,128]{2,1,0:T(8,128)(2,1)S(1)} %bitcast.49), channel_id=1, source_target_pairs={{0,24},{8,0},{16,8},{24,16},{1,25},{9,1},{17,9},{25,17},{2,26},{10... | collective-permute-start | bytes 1572872 | tf_op jit(solution)/shard_map/ppermute | solution.py:25
  65.0 27.2 %collective-permute-start.9 = (bf16[32,64,128]{2,1,0:T(8,128)(2,1)S(1)}, bf16[32,64,128]{2,1,0:T(8,128)(2,1)S(1)}, u32[]{:S(2)}, u32[]{:S(2)}) collective-permute-start(bf16[32,64,128]{2,1,0:T(8,128)(2,1)S(1)} %bitcast.50), channel_id=1, source_target_pairs={{0,8},{8,16},{16,24},{24,0},{1,9},{9,17},{17,25},{25,1},{2,10},{10... | collective-permute-start | bytes 1572872 | tf_op jit(solution)/shard_map/ppermute | solution.py:25
  66.9 25.2 %collective-permute-start.10 = (bf16[32,64,128]{2,1,0:T(8,128)(2,1)S(1)}, bf16[32,64,128]{2,1,0:T(8,128)(2,1)S(1)}, u32[]{:S(2)}, u32[]{:S(2)}) collective-permute-start(bf16[32,64,128]{2,1,0:T(8,128)(2,1)S(1)} %collective-permute-done.1.refs_3_), channel_id=1, source_target_pairs={{0,8},{8,16},{16,24},{24,0},{1,9},{9,17},{17,25},{25,1},{2,10},{10... | collective-permute-start | bytes 1572872 | tf_op jit(solution)/shard_map/ppermute | solution.py:25
  75.4 21.9 %collective-permute-start.8 = (bf16[32,64,128]{2,1,0:T(8,128)(2,1)S(1)}, bf16[32,64,128]{2,1,0:T(8,128)(2,1)S(1)}, u32[]{:S(2)}, u32[]{:S(2)}) collective-permute-start(bf16[32,64,128]{2,1,0:T(8,128)(2,1)S(1)} %collective-permute-done.7.refs_4_), channel_id=1, source_target_pairs={{0,24},{8,0},{16,8},{24,16},{1,25},{9,1},{17,9},{25,17},{2,26},{10... | collective-permute-start | bytes 1572872 | tf_op jit(solution)/shard_map/ppermute | solution.py:25
  80.9 2.8 %copy-start = (bf16[2,4,8,6,64,64]{5,4,3,2,1,0:T(8,128)(2,1)S(1)}, bf16[2,4,8,6,64,64]{5,4,3,2,1,0:T(8,128)(2,1)}, u32[]{:S(2)}) copy-start(bf16[2,4,8,6,64,64]{5,4,3,2,1,0:T(8,128)(2,1)} %get-tuple-element.18) | copy-start | bytes 9437188
  100.3 3.8 %collective-permute-start.11 = (bf16[4,27,16,128]{3,2,1,0:T(8,128)(2,1)S(1)}, bf16[4,27,16,128]{3,2,1,0:T(8,128)(2,1)S(1)}, u32[]{:S(2)}, u32[]{:S(2)}) collective-permute-start(bf16[4,27,16,128]{3,2,1,0:T(8,128)(2,1)S(1)} %slice_bitcast_fusion), channel_id=1, source_target_pairs={{0,1},{1,0},{2,3},{3,2},{4,5},{5,4},{6,7},{7,6},{8,9},{9,8},{10,11... | collective-permute-start | bytes 1327112 | tf_op jit(solution)/shard_map/ppermute | solution.py:25
  120.8 13.1 %collective-permute-start.12 = (bf16[27,8,128]{2,1,0:T(8,128)(2,1)S(1)}, bf16[27,8,128]{2,1,0:T(8,128)(2,1)S(1)}, u32[]{:S(2)}, u32[]{:S(2)}) collective-permute-start(bf16[27,8,128]{2,1,0:T(8,128)(2,1)S(1)} %slice.54), channel_id=1, source_target_pairs={{0,8},{8,16},{16,24},{24,32},{32,40},{40,48},{48,56},{56,64},{64,7... | collective-permute-start | bytes 165896 | tf_op jit(solution)/shard_map/ppermute | solution.py:25

commit v6 on v4

--- a/solution.py
+++ b/solution.py
@@ -25,15 +25,18 @@
     return lax.ppermute(value, axis, [(i, (i + by) % count) for i in range(count)])
 
 
+def swapped(value, axis, by):
+    return lax.ppermute(value, axis, [(i, i ^ by) for i in range(lax.axis_size(axis))])
+
+
 def spread(value, axis):
     count = lax.axis_size(axis)
     copies = jnp.broadcast_to(value[None], (count,) + value.shape)
     return lax.all_to_all(copies, axis, 0, 0, tiled=True)
 
 
-def left_kernel(info_ref, own_ref, a_ref, b_ref, done_ref, a_here, sems):
+def left_kernel(info_ref, own_ref, a_ref, b_ref, a_here, sems):
     core, yl = info_ref[6], info_ref[7]
-    done_ref[...] = jnp.zeros(done_ref.shape, F32)
 
     def fetch(v, h):
         return pltpu.make_async_copy(a_ref.at[h, v], a_here.at[v, h], sems.at[v, h])
@@ -47,7 +50,7 @@
         for h in range(2):
             fetch(v, h).wait()
         for c in range(8):
-            far = jnp.bitwise_and(yl - c // 2 + NY, NY - 1)
+            far = jnp.bitwise_xor(yl, c // 2)
             both = own_ref[jnp.bitwise_xor(core, c % 2), far, v].astype(F32).T.astype(BF16)
             for h in range(2):
                 left = both[h * T:(h + 1) * T]
@@ -59,17 +62,17 @@
     rows, slots = a_tiles.shape[:2]
     a = a_tiles.reshape(2, 4, 8, slots, T, T)
     vmem = pl.BlockSpec(memory_space=pltpu.VMEM)
-    b, done = pl.pallas_call(
+    b = pl.pallas_call(
         left_kernel,
         in_specs=[pl.BlockSpec(memory_space=pltpu.SMEM), vmem, pl.BlockSpec(memory_space=pltpu.HBM)],
-        out_specs=[vmem, vmem],
-        out_shape=[jax.ShapeDtypeStruct(a.shape, BF16), jax.ShapeDtypeStruct((8, 2 * T), F32)],
+        out_specs=vmem,
+        out_shape=jax.ShapeDtypeStruct(a.shape, BF16),
         scratch_shapes=[pltpu.VMEM((4, 2, 8, slots, T, T), BF16), pltpu.SemaphoreType.DMA((4, 2))],
         compiler_params=pltpu.CompilerParams(vmem_limit_bytes=46 * MIB),
         cost_estimate=pl.CostEstimate(flops=2 * rows * slots * T**3, bytes_accessed=16 * MIB, transcendentals=0),
         name="left_products",
     )(info, own, a)
-    return b.reshape(rows * slots, T, T), done
+    return b.reshape(rows * slots, T, T)
 
 
 def sum_kernel(group, n_chunks, n_before, *refs):
@@ -78,7 +81,7 @@
     b_ref = refs[2 + n_chunks]
     before = refs[3 + n_chunks:3 + n_chunks + n_before]
     out_ref, panel, acc, sems = refs[-4:]
-    core = info_ref[6]
+    core, yl = info_ref[6], info_ref[7]
     copies, at = [], 0
     for n, chunk in enumerate(chunks):
         size = chunk.shape[0]
@@ -120,7 +123,8 @@
     def _(k):
         for o in range(8):
             tile = jnp.concatenate([acc[k, o * 8:(o + 1) * 8], acc[KC + k, o * 8:(o + 1) * 8]], axis=0)
-            place = (jnp.bitwise_xor(core, o % 2), o // 2, k)
+            far = jnp.bitwise_xor(yl, o // 2)
+            place = (jnp.bitwise_xor(core, o % 2), jnp.bitwise_and(far, 1), jnp.right_shift(far, 1), k)
             for earlier in before:
                 tile = tile + earlier[place].astype(F32)
             out_ref[place] = tile.astype(BF16)
@@ -135,7 +139,7 @@
         functools.partial(sum_kernel, group, len(chunks), len(before)),
         in_specs=[smem, smem] + [anyw] * len(chunks) + [vmem] * (1 + len(before)),
         out_specs=vmem,
-        out_shape=jax.ShapeDtypeStruct((2, NY, KC, 16, 2 * T), BF16),
+        out_shape=jax.ShapeDtypeStruct((2, 2, 2, KC, 16, 2 * T), BF16),
         scratch_shapes=[
             pltpu.VMEM((pairs, T, 2 * T), BF16),
             pltpu.VMEM((2 * KC + 1, T, 2 * T), F32),
@@ -155,12 +159,13 @@
     packed = jnp.concatenate([p_tiles[0, :4], p_tiles[0, 4:]], axis=-1)
 
     across = shifted(packed, "yh", 1)
-    own = jnp.stack([packed] + [shifted(packed, "yl", k) for k in range(1, NY)])
     near = spread(packed, "z").reshape(-1, T, 2 * T)
-    across, near = lax.optimization_barrier((across, near))
+    across, near, packed = lax.optimization_barrier((across, near, packed))
     left_a, right_a = shifted(near, "x", 1), shifted(near, "x", -1)
-    own = jnp.stack([own, shifted(own, "core", 1)])
     other = spread(across, "z").reshape(-1, T, 2 * T)
+    own = jnp.stack([packed, swapped(packed, "yl", 1)])
+    own = jnp.concatenate([own, swapped(own, "yl", 2)])
+    own = jnp.stack([own, swapped(own, "core", 1)])
 
     live = jnp.arange(slots, dtype=I32)[None, :] < a_count
     owner = a_cols // 8
@@ -184,18 +189,25 @@
     code = jnp.sum(jnp.where(here, code[None, :] - empty, 0), axis=1) + empty
     info = jnp.concatenate([first, steps, jnp.stack([core, yl])]).astype(I32)
 
-    b, done = left_products(info, own, a_tiles)
-    other, _ = lax.optimization_barrier((other, done))
+    other, left_a, right_a, own, info, code = lax.optimization_barrier((other, left_a, right_a, own, info, code))
     left_b, right_b = shifted(other, "x", 1), shifted(other, "x", -1)
     left2, right2 = shifted(left_a, "x", 1), shifted(right_b, "x", -1)
+    b = left_products(info, own, a_tiles)
     sums0 = panel_sums(0, code, info, [near, left_a, right_a], b)
     sums1 = panel_sums(1, code, info, [other, left_b, right_b, left2], b)
     sums2 = panel_sums(2, code, info, [right2], b, (sums0, sums1))
 
-    chip = (sums2[0].astype(F32) + shifted(sums2[1], "core", 1).astype(F32)).astype(BF16)
-    shares = jnp.sum(lax.all_to_all(chip, "yl", 0, 0, tiled=True).astype(F32), axis=0)
-    moved = shifted(shares[:, 8:].astype(BF16), ROW, 1)
-    result = shares[:, :8] + moved.astype(F32)
+    chip = (sums2[0].astype(F32) + swapped(sums2[1], "core", 1).astype(F32)).astype(BF16)
+    two = chip[0].astype(F32) + swapped(chip[1], "yl", 1).astype(F32)
+    mine, theirs = two[0], two[1].astype(BF16)
+    count = lax.axis_size(ROW)
+    ahead = [[(r * NY + y, (r + 1) % count * NY + (y ^ by)) for r in range(count) for y in range(NY)] for by in (0, 2)]
+    last = [
+        lax.ppermute(theirs[:, 8:], ROW + ("yl",), ahead[1]),
+        lax.ppermute(mine[:, 8:].astype(BF16), ROW + ("yl",), ahead[0]),
+        swapped(theirs[:, :8], "yl", 2),
+    ]
+    result = mine[:, :8] + sum(part.astype(F32) for part in last)
     return jnp.stack([result[..., :T], result[..., T:]])
 
 

time: 132 us -> 138 us (1.045)
  waiting for transfers between devices: 24.3 us -> 44 us
  blocking collectives: 15.2 us -> 0 us
    ppermute x0 -> x8, starting transfers between devices: none -> 26 us  [the longest x6 22.2 us: swapped(): lax.ppermute(value, axis, [(i, i ^ by) for i in range(lax.axis_size(axis))])]
    ppermute x13 -> x7, starting transfers between devices: 51.4 us -> 28.5 us  [shifted(): lax.ppermute(value, axis, [(i, (i + by) % count) for i in range(count)])]
    ppermute x0 -> x8, waiting for transfers between devices: none -> 19.2 us  [the longest x1 9.91 us: body(): lax.ppermute(mine[:, 8:].astype(BF16), ROW + ('yl',), ahead[0])]
    all_to_all x1 -> x0, blocking collectives: 15.2 us -> none  [body(): lax.all_to_all(chip, 'yl', 0, 0, tiled=True).astype(F32)]
    all_to_all x2, waiting for transfers between devices: 10.6 us -> 14.2 us  [spread(): return lax.all_to_all(copies, axis, 0, 0, tiled=True)]
    ppermute x13 -> x7, waiting for transfers between devices: 13.7 us -> 10.7 us  [shifted(): lax.ppermute(value, axis, [(i, (i + by) % count) for i in range(count)])]
    all_to_all x2, starting transfers between devices: 16.1 us -> 13.5 us  [spread(): return lax.all_to_all(copies, axis, 0, 0, tiled=True)]
  transfers between devices with their start and end apart: 15 -> 17, of which waited for: 5 -> 11; matrix products, arithmetic and copies ran while one was open for 3% -> 4% of each run, Pallas kernels for 10% -> 10%
where the time goes in v6:
time: 138 us; the launch traced here: 136 us
  starting transfers between devices  68 us (49%)
  waiting for transfers between devices  44 us (32%)
  Pallas kernels  16 us (12%)
  other arithmetic  3.82 us (3%)
  local copies, waits for them, and re-layouts  3.5 us (3%)
    ppermute x7, starting transfers between devices, shifted(): lax.ppermute(value, axis, [(i, (i + by) % count) for i in range(count)])  28.5 us
    ppermute x6, starting transfers between devices, swapped(): lax.ppermute(value, axis, [(i, i ^ by) for i in range(lax.axis_size(axis))])  22.2 us
    all_to_all x2, waiting for transfers between devices, spread(): return lax.all_to_all(copies, axis, 0, 0, tiled=True)  14.2 us
    all_to_all x2, starting transfers between devices, spread(): return lax.all_to_all(copies, axis, 0, 0, tiled=True)  13.5 us
    pallas_call x3, Pallas kernels, panel_sums(): pl.pallas_call(functools.partial(sum_kernel, group, len(chunks), len(befo...  11.6 us
    ppermute x7, waiting for transfers between devices, shifted(): lax.ppermute(value, axis, [(i, (i + by) % count) for i in range(count)])  10.7 us
    ppermute x1, waiting for transfers between devices, body(): lax.ppermute(mine[:, 8:].astype(BF16), ROW + ('yl',), ahead[0])  9.91 us
    ppermute x6, waiting for transfers between devices, swapped(): lax.ppermute(value, axis, [(i, i ^ by) for i in range(lax.axis_size(axis))])  8.56 us
  transfers between devices with their start and end apart: 17, of which 11 were waited for; matrix products, arithmetic and copies ran while one was open for 4% of the time, Pallas kernels for 10%

profile of v6, /device:TPU:1, one launch (start us, length us, event | category | flops | bytes accessed | tf_op | source)
XLA Modules:
  0.0 136.0 jit_solution(16752845482555277040)
XLA Ops:
  0.0 0.9 slice_bitcast_fusion.8
  1.0 8.3 %collective-permute-start = (bf16[4,64,128]{2,1,0:T(8,128)(2,1)S(1)}, bf16[4,64,128]{2,1,0:T(8,128)(2,1)S(1)}, u32[]{:S(2)}, u32[]{:S(2)}) collective-permute-start(bf16[4,64,128]{2,1,0:T(8,128)(2,1)S(1)} %pad_maximum_fusion.4), channel_id=1, source_target_pairs={{0,32},{32,0},{1,33},{33,1},{2,34},{34,2},{3,35},{35,3},{4,36},{36... | collective-permute-start | bytes 196616 | tf_op jit(solution)/shard_map/ppermute | solution.py:25
  9.3 0.9 broadcast_in_dim.27
  10.2 10.0 %all-to-all-start = ((bf16[8,4,64,128]{3,2,1,0:T(8,128)(2,1)}), bf16[8,4,64,128]{3,2,1,0:T(8,128)(2,1)S(1)}, u32[]{:S(2)}, u32[]{:S(2)}) async-start(bf16[8,4,64,128]{3,2,1,0:T(8,128)(2,1)} %broadcast_in_dim.27), calls=%async_computation | async-start | bytes 1048576 | tf_op jit(solution)/shard_map/all_to_all | solution.py:35
  20.2 0.7 fusion.33
  20.9 0.7 fusion.17
  21.7 0.1 eq.46
  21.9 0.7 iota_compare_fusion.3
  22.6 0.1 lt.51
  22.7 0.1 convert_reduce_fusion
  22.9 0.2 reduce-window.7
  23.1 14.2 %all-to-all-done = bf16[8,4,64,128]{3,2,1,0:T(8,128)(2,1)S(1)} async-done(((bf16[8,4,64,128]{3,2,1,0:T(8,128)(2,1)}), bf16[8,4,64,128]{3,2,1,0:T(8,128)(2,1)S(1)}, u32[]{:S(2)}, u32[]{:S(2)}) %all-to-all-start) | async-done | bytes 524320 | tf_op jit(solution)/shard_map/all_to_all | solution.py:35
  37.3 2.3 %collective-permute-start.3 = (bf16[4,64,128]{2,1,0:T(8,128)(2,1)S(1)}, bf16[4,64,128]{2,1,0:T(8,128)(2,1)S(1)}, u32[]{:S(2)}, u32[]{:S(2)}) collective-permute-start(bf16[4,64,128]{2,1,0:T(8,128)(2,1)S(1)} %pad_maximum_fusion.4), channel_id=1, source_target_pairs={{0,2},{2,0},{4,6},{6,4},{1,3},{3,1},{5,7},{7,5},{8,10},{10,8},{12,... | collective-permute-start | bytes 196616 | tf_op jit(solution)/shard_map/ppermute | solution.py:29
  39.6 0.2 fusion.3
  39.8 0.9 broadcast_in_dim.28
  40.7 3.5 %all-to-all-start.1 = ((bf16[8,4,64,128]{3,2,1,0:T(8,128)(2,1)}), bf16[8,4,64,128]{3,2,1,0:T(8,128)(2,1)S(1)}, u32[]{:S(2)}, u32[]{:S(2)}) async-start(bf16[8,4,64,128]{3,2,1,0:T(8,128)(2,1)} %broadcast_in_dim.28), calls=%async_computation.1 | async-start | bytes 1048576 | tf_op jit(solution)/shard_map/all_to_all | solution.py:35
  44.2 2.4 %collective-permute-start.4 = (bf16[2,4,64,128]{3,2,1,0:T(8,128)(2,1)S(1)}, bf16[2,4,64,128]{3,2,1,0:T(8,128)(2,1)S(1)}, u32[]{:S(2)}, u32[]{:S(2)}) collective-permute-start(bf16[2,4,64,128]{3,2,1,0:T(8,128)(2,1)S(1)} %pad_maximum_fusion.3), channel_id=1, source_target_pairs={{0,4},{2,6},{4,0},{6,2},{1,5},{3,7},{5,1},{7,3},{8,12},{10,14},{12... | collective-permute-start | bytes 393224 | tf_op jit(solution)/shard_map/ppermute | solution.py:29
  46.7 0.1 copy.10
  46.7 0.1 sub.82
  46.9 0.2 select_reduce_fusion
  47.1 3.1 %collective-permute-start.1 = (bf16[32,64,128]{2,1,0:T(8,128)(2,1)S(1)}, bf16[32,64,128]{2,1,0:T(8,128)(2,1)S(1)}, u32[]{:S(2)}, u32[]{:S(2)}) collective-permute-start(bf16[32,64,128]{2,1,0:T(8,128)(2,1)S(1)} %bitcast.53), channel_id=1, source_target_pairs={{0,8},{8,16},{16,24},{24,0},{1,9},{9,17},{17,25},{25,1},{2,10},{10... | collective-permute-start | bytes 1572872 | tf_op jit(solution)/shard_map/ppermute | solution.py:25
  50.2 3.4 %collective-permute-start.2 = (bf16[32,64,128]{2,1,0:T(8,128)(2,1)S(1)}, bf16[32,64,128]{2,1,0:T(8,128)(2,1)S(1)}, u32[]{:S(2)}, u32[]{:S(2)}) collective-permute-start(bf16[32,64,128]{2,1,0:T(8,128)(2,1)S(1)} %bitcast.54), channel_id=1, source_target_pairs={{0,24},{8,0},{16,8},{24,16},{1,25},{9,1},{17,9},{25,17},{2,26},{10... | collective-permute-start | bytes 1572872 | tf_op jit(solution)/shard_map/ppermute | solution.py:25
  53.6 0.8 collective-permute-done.4
  54.4 3.6 %collective-permute-start.5 = (bf16[4,4,64,128]{3,2,1,0:T(8,128)(2,1)S(1)}, bf16[4,4,64,128]{3,2,1,0:T(8,128)(2,1)S(1)}, u32[]{:S(2)}, u32[]{:S(2)}) collective-permute-start(bf16[4,4,64,128]{3,2,1,0:T(8,128)(2,1)S(1)} %get-tuple-element.26), channel_id=1, source_target_pairs={{0,1},{1,0},{2,3},{3,2},{4,5},{5,4},{6,7},{7,6},{8,9},{9,8},{10,11... | collective-permute-start | bytes 786440 | tf_op jit(solution)/shard_map/ppermute | solution.py:29
  58.2 1.1 collective-permute-done.5
  59.3 2.3 %collective-permute-done.1.refs_3_ = bf16[32,64,128]{2,1,0:T(8,128)(2,1)S(1)} collective-permute-done((bf16[32,64,128]{2,1,0:T(8,128)(2,1)S(1)}, bf16[32,64,128]{2,1,0:T(8,128)(2,1)S(1)}, u32[]{:S(2)}, u32[]{:S(2)}) %collective-permute-start.1) | collective-permute-done | bytes 524320 | tf_op jit(solution)/shard_map/ppermute | solution.py:25
  61.6 1.6 %collective-permute-done.2.refs_4_ = bf16[32,64,128]{2,1,0:T(8,128)(2,1)S(1)} collective-permute-done((bf16[32,64,128]{2,1,0:T(8,128)(2,1)S(1)}, bf16[32,64,128]{2,1,0:T(8,128)(2,1)S(1)}, u32[]{:S(2)}, u32[]{:S(2)}) %collective-permute-start.2) | collective-permute-done | bytes 524320 | tf_op jit(solution)/shard_map/ppermute | solution.py:25
  63.2 4.6 %collective-permute-start.6 = (bf16[32,64,128]{2,1,0:T(8,128)(2,1)S(1)}, bf16[32,64,128]{2,1,0:T(8,128)(2,1)S(1)}, u32[]{:S(2)}, u32[]{:S(2)}) collective-permute-start(bf16[32,64,128]{2,1,0:T(8,128)(2,1)S(1)} %bitcast.56), channel_id=1, source_target_pairs={{0,24},{8,0},{16,8},{24,16},{1,25},{9,1},{17,9},{25,17},{2,26},{10... | collective-permute-start | bytes 1572872 | tf_op jit(solution)/shard_map/ppermute | solution.py:25
  67.8 1.9 %collective-permute-start.8 = (bf16[32,64,128]{2,1,0:T(8,128)(2,1)S(1)}, bf16[32,64,128]{2,1,0:T(8,128)(2,1)S(1)}, u32[]{:S(2)}, u32[]{:S(2)}) collective-permute-start(bf16[32,64,128]{2,1,0:T(8,128)(2,1)S(1)} %bitcast.57), channel_id=1, source_target_pairs={{0,8},{8,16},{16,24},{24,0},{1,9},{9,17},{17,25},{25,1},{2,10},{10... | collective-permute-start | bytes 1572872 | tf_op jit(solution)/shard_map/ppermute | solution.py:25
  69.8 1.9 %collective-permute-start.9 = (bf16[32,64,128]{2,1,0:T(8,128)(2,1)S(1)}, bf16[32,64,128]{2,1,0:T(8,128)(2,1)S(1)}, u32[]{:S(2)}, u32[]{:S(2)}) collective-permute-start(bf16[32,64,128]{2,1,0:T(8,128)(2,1)S(1)} %collective-permute-done.1.refs_3_), channel_id=1, source_target_pairs={{0,8},{8,16},{16,24},{24,0},{1,9},{9,17},{17,25},{25,1},{2,10},{10... | collective-permute-start | bytes 1572872 | tf_op jit(solution)/shard_map/ppermute | solution.py:25
  71.7 4.2 %collective-permute-done.6.refs_4_ = bf16[32,64,128]{2,1,0:T(8,128)(2,1)S(1)} collective-permute-done((bf16[32,64,128]{2,1,0:T(8,128)(2,1)S(1)}, bf16[32,64,128]{2,1,0:T(8,128)(2,1)S(1)}, u32[]{:S(2)}, u32[]{:S(2)}) %collective-permute-start.6) | collective-permute-done | bytes 524320 | tf_op jit(solution)/shard_map/ppermute | solution.py:25
  75.8 5.3 %collective-permute-start.7 = (bf16[32,64,128]{2,1,0:T(8,128)(2,1)S(1)}, bf16[32,64,128]{2,1,0:T(8,128)(2,1)S(1)}, u32[]{:S(2)}, u32[]{:S(2)}) collective-permute-start(bf16[32,64,128]{2,1,0:T(8,128)(2,1)S(1)} %collective-permute-done.6.refs_4_), channel_id=1, source_target_pairs={{0,24},{8,0},{16,8},{24,16},{1,25},{9,1},{17,9},{25,17},{2,26},{10... | collective-permute-start | bytes 1572872 | tf_op jit(solution)/shard_map/ppermute | solution.py:25
  81.2 4.5 %left_products.1 = bf16[2,4,8,6,64,64]{5,4,3,2,1,0:T(8,128)(2,1)S(1)} custom-call(s32[8]{0:T(128)S(1)} %pad_add_fusion.info_ref.refs_1_, bf16[2,4,4,64,128]{4,3,2,1,0:T(8,128)(2,1)S(1)} %pad_maximum_fusion.own_ref, bf16[2,4,8,6,64,64]{5,4,3,2,1,0:T(8,128)(2,1)} %bitcast.59), custom_call_target="tpu_custom_call" | custom-call | flops 201326592 | bytes 16777216 | tf_op jit(solution)/shard_map/left_products/pallas_call | solution.py:65
  85.6 3.9 %panel_sums_0.1.refs_4_ = bf16[2,2,2,27,16,128]{5,4,3,2,1,0:T(8,128)(2,1)S(1)} custom-call(s32[408]{0:T(512)S(1)} %broadcast_add_fusion.refs_0_, s32[8]{0:T(128)S(1)} %pad_add_fusion.info_ref.refs_1_, bf16[32,64,128]{2,1,0:T(8,128)(2,1)S(1)} %bitcast.55, bf16[32,64,128]{2,1,0:T(8,128)(2,1)S(1)} %collective-permute-done.1.refs_3_, ...), custom_call_target="tpu_custom_call" | custom-call | flops 100663296 | bytes 8388608 | tf_op jit(solution)/shard_map/panel_sums_0/pallas_call | solution.py:138
  89.6 2.6 %collective-permute-done.9.refs_5_ = bf16[32,64,128]{2,1,0:T(8,128)(2,1)S(1)} collective-permute-done((bf16[32,64,128]{2,1,0:T(8,128)(2,1)S(1)}, bf16[32,64,128]{2,1,0:T(8,128)(2,1)S(1)}, u32[]{:S(2)}, u32[]{:S(2)}) %collective-permute-start.9) | collective-permute-done | bytes 524320 | tf_op jit(solution)/shard_map/ppermute | solution.py:25
  92.1 5.0 %panel_sums_1.1.refs_5_ = bf16[2,2,2,27,16,128]{5,4,3,2,1,0:T(8,128)(2,1)S(1)} custom-call(s32[408]{0:T(512)S(1)} %broadcast_add_fusion.refs_0_, s32[8]{0:T(128)S(1)} %pad_add_fusion.info_ref.refs_1_, bf16[32,64,128]{2,1,0:T(8,128)(2,1)S(1)} %bitcast.58, bf16[32,64,128]{2,1,0:T(8,128)(2,1)S(1)} %collective-permute-done.8.refs_3_, ...), custom_call_target="tpu_custom_call" | custom-call | flops 134217728 | bytes 8388608 | tf_op jit(solution)/shard_map/panel_sums_1/pallas_call | solution.py:138
  97.1 2.7 %panel_sums_2.1 = bf16[2,2,2,27,16,128]{5,4,3,2,1,0:T(8,128)(2,1)S(1)} custom-call(s32[408]{0:T(512)S(1)} %broadcast_add_fusion.refs_0_, s32[8]{0:T(128)S(1)} %pad_add_fusion.info_ref.refs_1_, bf16[32,64,128]{2,1,0:T(8,128)(2,1)S(1)} %collective-permute-done.7.refs_2_, bf16[384,64,64]{2,1,0:T(8,128)(2,1)S(1)} %bitcast.52, ...), custom_call_target="tpu_custom_call" | custom-call | flops 33554432 | bytes 8388608 | tf_op jit(solution)/shard_map/panel_sums_2/pallas_call | solution.py:138
  99.9 7.1 %collective-permute-start.10 = (bf16[2,2,27,16,128]{4,3,2,1,0:T(8,128)(2,1)S(1)}, bf16[2,2,27,16,128]{4,3,2,1,0:T(8,128)(2,1)S(1)}, u32[]{:S(2)}, u32[]{:S(2)}) collective-permute-start(bf16[2,2,27,16,128]{4,3,2,1,0:T(8,128)(2,1)S(1)} %slice_bitcast_fusion), channel_id=1, source_target_pairs={{0,1},{1,0},{2,3},{3,2},{4,5},{5,4},{6,7},{7,6},{8,9},{9,8},{10,11... | collective-permute-start | bytes 1327112 | tf_op jit(solution)/shard_map/ppermute | solution.py:29
  106.9 1.4 %collective-permute-done.10 = bf16[2,2,27,16,128]{4,3,2,1,0:T(8,128)(2,1)S(1)} collective-permute-done((bf16[2,2,27,16,128]{4,3,2,1,0:T(8,128)(2,1)S(1)}, bf16[2,2,27,16,128]{4,3,2,1,0:T(8,128)(2,1)S(1)}, u32[]{:S(2)}, u32[]{:S(2)}) %collective-permute-start.10) | collective-permute-done | bytes 442400 | tf_op jit(solution)/shard_map/ppermute | solution.py:29
  108.3 0.1 fusion.4
  108.5 3.2 %collective-permute-start.11 = (bf16[2,27,16,128]{3,2,1,0:T(8,128)(2,1)S(1)}, bf16[2,27,16,128]{3,2,1,0:T(8,128)(2,1)S(1)}, u32[]{:S(2)}, u32[]{:S(2)}) collective-permute-start(bf16[2,27,16,128]{3,2,1,0:T(8,128)(2,1)S(1)} %slice_bitcast_fusion.3), channel_id=1, source_target_pairs={{0,2},{2,0},{4,6},{6,4},{1,3},{3,1},{5,7},{7,5},{8,10},{10,8},{12,... | collective-permute-start | bytes 663560 | tf_op jit(solution)/shard_map/ppermute | solution.py:29
  111.7 5.3 %collective-permute-done.11 = bf16[2,27,16,128]{3,2,1,0:T(8,128)(2,1)S(1)} collective-permute-done((bf16[2,27,16,128]{3,2,1,0:T(8,128)(2,1)S(1)}, bf16[2,27,16,128]{3,2,1,0:T(8,128)(2,1)S(1)}, u32[]{:S(2)}, u32[]{:S(2)}) %collective-permute-start.11) | collective-permute-done | bytes 221216 | tf_op jit(solution)/shard_map/ppermute | solution.py:29
  117.1 3.5 %collective-permute-start.14 = (bf16[27,8,128]{2,1,0:T(8,128)(2,1)S(1)}, bf16[27,8,128]{2,1,0:T(8,128)(2,1)S(1)}, u32[]{:S(2)}, u32[]{:S(2)}) collective-permute-start(bf16[27,8,128]{2,1,0:T(8,128)(2,1)S(1)} %get-tuple-element.32), channel_id=1, source_target_pairs={{0,4},{2,6},{4,0},{6,2},{1,5},{3,7},{5,1},{7,3},{8,12},{10,14},{12... | collective-permute-start | bytes 165896 | tf_op jit(solution)/shard_map/ppermute | solution.py:29
  120.7 1.9 %collective-permute-start.13 = (bf16[27,8,128]{2,1,0:T(8,128)(2,1)S(1)}, bf16[27,8,128]{2,1,0:T(8,128)(2,1)S(1)}, u32[]{:S(2)}, u32[]{:S(2)}) collective-permute-start(bf16[27,8,128]{2,1,0:T(8,128)(2,1)S(1)} %slice.88), channel_id=1, source_target_pairs={{0,8},{2,10},{4,12},{6,14},{8,16},{10,18},{12,20},{14,22},{16,24},... | collective-permute-start | bytes 165896 | tf_op jit(solution)/shard_map/ppermute | solution.py:207
  122.6 1.9 %collective-permute-start.12 = (bf16[27,8,128]{2,1,0:T(8,128)(2,1)S(1)}, bf16[27,8,128]{2,1,0:T(8,128)(2,1)S(1)}, u32[]{:S(2)}, u32[]{:S(2)}) collective-permute-start(bf16[27,8,128]{2,1,0:T(8,128)(2,1)S(1)} %get-tuple-element.31), channel_id=1, source_target_pairs={{0,12},{2,14},{4,8},{6,10},{8,20},{10,22},{12,16},{14,18},{16,28},... | collective-permute-start | bytes 165896 | tf_op jit(solution)/shard_map/ppermute | solution.py:206
  124.5 9.9 %collective-permute-done.13 = bf16[27,8,128]{2,1,0:T(8,128)(2,1)S(1)} collective-permute-done((bf16[27,8,128]{2,1,0:T(8,128)(2,1)S(1)}, bf16[27,8,128]{2,1,0:T(8,128)(2,1)S(1)}, u32[]{:S(2)}, u32[]{:S(2)}) %collective-permute-start.13) | collective-permute-done | bytes 55328 | tf_op jit(solution)/shard_map/ppermute | solution.py:207
  134.4 0.7 collective-permute-done.12
  135.3 0.7 pad_maximum_fusion.2
  (25 shorter events, 0.7 us)
Async XLA Ops:
  1.0 22.1 %collective-permute-start = (bf16[4,64,128]{2,1,0:T(8,128)(2,1)S(1)}, bf16[4,64,128]{2,1,0:T(8,128)(2,1)S(1)}, u32[]{:S(2)}, u32[]{:S(2)}) collective-permute-start(bf16[4,64,128]{2,1,0:T(8,128)(2,1)S(1)} %pad_maximum_fusion.4), channel_id=1, source_target_pairs={{0,32},{32,0},{1,33},{33,1},{2,34},{34,2},{3,35},{35,3},{4,36},{36... | collective-permute-start | bytes 196616 | tf_op jit(solution)/shard_map/ppermute | solution.py:25
  10.2 27.1 %all-to-all-start = ((bf16[8,4,64,128]{3,2,1,0:T(8,128)(2,1)}), bf16[8,4,64,128]{3,2,1,0:T(8,128)(2,1)S(1)}, u32[]{:S(2)}, u32[]{:S(2)}) async-start(bf16[8,4,64,128]{3,2,1,0:T(8,128)(2,1)} %broadcast_in_dim.27), calls=%async_computation | async-start | bytes 1048576 | tf_op jit(solution)/shard_map/all_to_all | solution.py:35
  37.3 6.9 %collective-permute-start.3 = (bf16[4,64,128]{2,1,0:T(8,128)(2,1)S(1)}, bf16[4,64,128]{2,1,0:T(8,128)(2,1)S(1)}, u32[]{:S(2)}, u32[]{:S(2)}) collective-permute-start(bf16[4,64,128]{2,1,0:T(8,128)(2,1)S(1)} %pad_maximum_fusion.4), channel_id=1, source_target_pairs={{0,2},{2,0},{4,6},{6,4},{1,3},{3,1},{5,7},{7,5},{8,10},{10,8},{12,... | collective-permute-start | bytes 196616 | tf_op jit(solution)/shard_map/ppermute | solution.py:29
  40.7 22.6 %all-to-all-start.1 = ((bf16[8,4,64,128]{3,2,1,0:T(8,128)(2,1)}), bf16[8,4,64,128]{3,2,1,0:T(8,128)(2,1)S(1)}, u32[]{:S(2)}, u32[]{:S(2)}) async-start(bf16[8,4,64,128]{3,2,1,0:T(8,128)(2,1)} %broadcast_in_dim.28), calls=%async_computation.1 | async-start | bytes 1048576 | tf_op jit(solution)/shard_map/all_to_all | solution.py:35
  44.2 10.2 %collective-permute-start.4 = (bf16[2,4,64,128]{3,2,1,0:T(8,128)(2,1)S(1)}, bf16[2,4,64,128]{3,2,1,0:T(8,128)(2,1)S(1)}, u32[]{:S(2)}, u32[]{:S(2)}) collective-permute-start(bf16[2,4,64,128]{3,2,1,0:T(8,128)(2,1)S(1)} %pad_maximum_fusion.3), channel_id=1, source_target_pairs={{0,4},{2,6},{4,0},{6,2},{1,5},{3,7},{5,1},{7,3},{8,12},{10,14},{12... | collective-permute-start | bytes 393224 | tf_op jit(solution)/shard_map/ppermute | solution.py:29
  47.1 14.5 %collective-permute-start.1 = (bf16[32,64,128]{2,1,0:T(8,128)(2,1)S(1)}, bf16[32,64,128]{2,1,0:T(8,128)(2,1)S(1)}, u32[]{:S(2)}, u32[]{:S(2)}) collective-permute-start(bf16[32,64,128]{2,1,0:T(8,128)(2,1)S(1)} %bitcast.53), channel_id=1, source_target_pairs={{0,8},{8,16},{16,24},{24,0},{1,9},{9,17},{17,25},{25,1},{2,10},{10... | collective-permute-start | bytes 1572872 | tf_op jit(solution)/shard_map/ppermute | solution.py:25
  50.2 13.1 %collective-permute-start.2 = (bf16[32,64,128]{2,1,0:T(8,128)(2,1)S(1)}, bf16[32,64,128]{2,1,0:T(8,128)(2,1)S(1)}, u32[]{:S(2)}, u32[]{:S(2)}) collective-permute-start(bf16[32,64,128]{2,1,0:T(8,128)(2,1)S(1)} %bitcast.54), channel_id=1, source_target_pairs={{0,24},{8,0},{16,8},{24,16},{1,25},{9,1},{17,9},{25,17},{2,26},{10... | collective-permute-start | bytes 1572872 | tf_op jit(solution)/shard_map/ppermute | solution.py:25
  54.4 4.8 %collective-permute-start.5 = (bf16[4,4,64,128]{3,2,1,0:T(8,128)(2,1)S(1)}, bf16[4,4,64,128]{3,2,1,0:T(8,128)(2,1)S(1)}, u32[]{:S(2)}, u32[]{:S(2)}) collective-permute-start(bf16[4,4,64,128]{3,2,1,0:T(8,128)(2,1)S(1)} %get-tuple-element.26), channel_id=1, source_target_pairs={{0,1},{1,0},{2,3},{3,2},{4,5},{5,4},{6,7},{7,6},{8,9},{9,8},{10,11... | collective-permute-start | bytes 786440 | tf_op jit(solution)/shard_map/ppermute | solution.py:29
  63.2 12.6 %collective-permute-start.6 = (bf16[32,64,128]{2,1,0:T(8,128)(2,1)S(1)}, bf16[32,64,128]{2,1,0:T(8,128)(2,1)S(1)}, u32[]{:S(2)}, u32[]{:S(2)}) collective-permute-start(bf16[32,64,128]{2,1,0:T(8,128)(2,1)S(1)} %bitcast.56), channel_id=1, source_target_pairs={{0,24},{8,0},{16,8},{24,16},{1,25},{9,1},{17,9},{25,17},{2,26},{10... | collective-permute-start | bytes 1572872 | tf_op jit(solution)/shard_map/ppermute | solution.py:25
  67.8 21.7 %collective-permute-start.8 = (bf16[32,64,128]{2,1,0:T(8,128)(2,1)S(1)}, bf16[32,64,128]{2,1,0:T(8,128)(2,1)S(1)}, u32[]{:S(2)}, u32[]{:S(2)}) collective-permute-start(bf16[32,64,128]{2,1,0:T(8,128)(2,1)S(1)} %bitcast.57), channel_id=1, source_target_pairs={{0,8},{8,16},{16,24},{24,0},{1,9},{9,17},{17,25},{25,1},{2,10},{10... | collective-permute-start | bytes 1572872 | tf_op jit(solution)/shard_map/ppermute | solution.py:25
  69.8 22.4 %collective-permute-start.9 = (bf16[32,64,128]{2,1,0:T(8,128)(2,1)S(1)}, bf16[32,64,128]{2,1,0:T(8,128)(2,1)S(1)}, u32[]{:S(2)}, u32[]{:S(2)}) collective-permute-start(bf16[32,64,128]{2,1,0:T(8,128)(2,1)S(1)} %collective-permute-done.1.refs_3_), channel_id=1, source_target_pairs={{0,8},{8,16},{16,24},{24,0},{1,9},{9,17},{17,25},{25,1},{2,10},{10... | collective-permute-start | bytes 1572872 | tf_op jit(solution)/shard_map/ppermute | solution.py:25
  75.8 21.3 %collective-permute-start.7 = (bf16[32,64,128]{2,1,0:T(8,128)(2,1)S(1)}, bf16[32,64,128]{2,1,0:T(8,128)(2,1)S(1)}, u32[]{:S(2)}, u32[]{:S(2)}) collective-permute-start(bf16[32,64,128]{2,1,0:T(8,128)(2,1)S(1)} %collective-permute-done.6.refs_4_), channel_id=1, source_target_pairs={{0,24},{8,0},{16,8},{24,16},{1,25},{9,1},{17,9},{25,17},{2,26},{10... | collective-permute-start | bytes 1572872 | tf_op jit(solution)/shard_map/ppermute | solution.py:25
  99.9 8.5 %collective-permute-start.10 = (bf16[2,2,27,16,128]{4,3,2,1,0:T(8,128)(2,1)S(1)}, bf16[2,2,27,16,128]{4,3,2,1,0:T(8,128)(2,1)S(1)}, u32[]{:S(2)}, u32[]{:S(2)}) collective-permute-start(bf16[2,2,27,16,128]{4,3,2,1,0:T(8,128)(2,1)S(1)} %slice_bitcast_fusion), channel_id=1, source_target_pairs={{0,1},{1,0},{2,3},{3,2},{4,5},{5,4},{6,7},{7,6},{8,9},{9,8},{10,11... | collective-permute-start | bytes 1327112 | tf_op jit(solution)/shard_map/ppermute | solution.py:29
  108.5 8.5 %collective-permute-start.11 = (bf16[2,27,16,128]{3,2,1,0:T(8,128)(2,1)S(1)}, bf16[2,27,16,128]{3,2,1,0:T(8,128)(2,1)S(1)}, u32[]{:S(2)}, u32[]{:S(2)}) collective-permute-start(bf16[2,27,16,128]{3,2,1,0:T(8,128)(2,1)S(1)} %slice_bitcast_fusion.3), channel_id=1, source_target_pairs={{0,2},{2,0},{4,6},{6,4},{1,3},{3,1},{5,7},{7,5},{8,10},{10,8},{12,... | collective-permute-start | bytes 663560 | tf_op jit(solution)/shard_map/ppermute | solution.py:29
  117.1 7.4 %collective-permute-start.14 = (bf16[27,8,128]{2,1,0:T(8,128)(2,1)S(1)}, bf16[27,8,128]{2,1,0:T(8,128)(2,1)S(1)}, u32[]{:S(2)}, u32[]{:S(2)}) collective-permute-start(bf16[27,8,128]{2,1,0:T(8,128)(2,1)S(1)} %get-tuple-element.32), channel_id=1, source_target_pairs={{0,4},{2,6},{4,0},{6,2},{1,5},{3,7},{5,1},{7,3},{8,12},{10,14},{12... | collective-permute-start | bytes 165896 | tf_op jit(solution)/shard_map/ppermute | solution.py:29
  120.7 13.8 %collective-permute-start.13 = (bf16[27,8,128]{2,1,0:T(8,128)(2,1)S(1)}, bf16[27,8,128]{2,1,0:T(8,128)(2,1)S(1)}, u32[]{:S(2)}, u32[]{:S(2)}) collective-permute-start(bf16[27,8,128]{2,1,0:T(8,128)(2,1)S(1)} %slice.88), channel_id=1, source_target_pairs={{0,8},{2,10},{4,12},{6,14},{8,16},{10,18},{12,20},{14,22},{16,24},... | collective-permute-start | bytes 165896 | tf_op jit(solution)/shard_map/ppermute | solution.py:207
  122.6 12.5 %collective-permute-start.12 = (bf16[27,8,128]{2,1,0:T(8,128)(2,1)S(1)}, bf16[27,8,128]{2,1,0:T(8,128)(2,1)S(1)}, u32[]{:S(2)}, u32[]{:S(2)}) collective-permute-start(bf16[27,8,128]{2,1,0:T(8,128)(2,1)S(1)} %get-tuple-element.31), channel_id=1, source_target_pairs={{0,12},{2,14},{4,8},{6,10},{8,20},{10,22},{12,16},{14,18},{16,28},... | collective-permute-start | bytes 165896 | tf_op jit(solution)/shard_map/ppermute | solution.py:206

commit v7 on v6

--- a/solution.py
+++ b/solution.py
@@ -35,9 +35,7 @@
     return lax.all_to_all(copies, axis, 0, 0, tiled=True)
 
 
-def left_kernel(info_ref, own_ref, a_ref, b_ref, a_here, sems):
-    core, yl = info_ref[6], info_ref[7]
-
+def left_kernel(own_ref, a_ref, b_ref, a_here, sems):
     def fetch(v, h):
         return pltpu.make_async_copy(a_ref.at[h, v], a_here.at[v, h], sems.at[v, h])
 
@@ -50,28 +48,27 @@
         for h in range(2):
             fetch(v, h).wait()
         for c in range(8):
-            far = jnp.bitwise_xor(yl, c // 2)
-            both = own_ref[jnp.bitwise_xor(core, c % 2), far, v].astype(F32).T.astype(BF16)
+            both = own_ref[c, v].astype(F32).T.astype(BF16)
             for h in range(2):
                 left = both[h * T:(h + 1) * T]
                 for s in range(a_ref.shape[3]):
                     b_ref[h, v, c, s] = jnp.dot(left, a_here[v, h, c, s], preferred_element_type=F32).astype(BF16)
 
 
-def left_products(info, own, a_tiles):
+def left_products(own, a_tiles):
     rows, slots = a_tiles.shape[:2]
     a = a_tiles.reshape(2, 4, 8, slots, T, T)
     vmem = pl.BlockSpec(memory_space=pltpu.VMEM)
     b = pl.pallas_call(
         left_kernel,
-        in_specs=[pl.BlockSpec(memory_space=pltpu.SMEM), vmem, pl.BlockSpec(memory_space=pltpu.HBM)],
+        in_specs=[vmem, pl.BlockSpec(memory_space=pltpu.HBM)],
         out_specs=vmem,
         out_shape=jax.ShapeDtypeStruct(a.shape, BF16),
         scratch_shapes=[pltpu.VMEM((4, 2, 8, slots, T, T), BF16), pltpu.SemaphoreType.DMA((4, 2))],
         compiler_params=pltpu.CompilerParams(vmem_limit_bytes=46 * MIB),
         cost_estimate=pl.CostEstimate(flops=2 * rows * slots * T**3, bytes_accessed=16 * MIB, transcendentals=0),
         name="left_products",
-    )(info, own, a)
+    )(own, a)
     return b.reshape(rows * slots, T, T)
 
 
@@ -155,24 +152,15 @@
     rows, slots = a_tiles.shape[:2]
     total = rows * slots
     core, yl, me_x = lax.axis_index("core"), lax.axis_index("yl"), lax.axis_index("x")
-    me_yh = lax.axis_index("yh")
     packed = jnp.concatenate([p_tiles[0, :4], p_tiles[0, 4:]], axis=-1)
-
-    across = shifted(packed, "yh", 1)
-    near = spread(packed, "z").reshape(-1, T, 2 * T)
-    across, near, packed = lax.optimization_barrier((across, near, packed))
-    left_a, right_a = shifted(near, "x", 1), shifted(near, "x", -1)
-    other = spread(across, "z").reshape(-1, T, 2 * T)
-    own = jnp.stack([packed, swapped(packed, "yl", 1)])
-    own = jnp.concatenate([own, swapped(own, "yl", 2)])
-    own = jnp.stack([own, swapped(own, "core", 1)])
 
     live = jnp.arange(slots, dtype=I32)[None, :] < a_count
     owner = a_cols // 8
     far = jnp.bitwise_and(owner - me_x + 4, 3)
-    away = jnp.bitwise_xor((owner // 4) % 2, me_yh)
-    group = jnp.where(far == 2, 1 + away, away)
-    pair = owner // 8 * 4 + a_cols % 4 + jnp.where(far == 3, 32, jnp.where(far == 1, 64, jnp.where(far == 2, 96 * (1 - away), 0)))
+    high = (owner // 4) % 2
+    group = jnp.where(far == 0, 0, jnp.where(far == 2, 2, jnp.where((far == 3) == (high == 0), 0, 1)))
+    seat = jnp.where(far == 1, 3 - 2 * (1 - high), jnp.where(far == 3, 2 * (1 - high), high))
+    pair = seat * 32 + owner // 8 * 4 + a_cols % 4
     to_high = jnp.broadcast_to(agg[:, None] % CR, a_cols.shape)
     target = agg[:, None] // CR * KC + a_slot
     swap = ((a_cols % 8) // 4 + to_high) % 2
@@ -189,13 +177,17 @@
     code = jnp.sum(jnp.where(here, code[None, :] - empty, 0), axis=1) + empty
     info = jnp.concatenate([first, steps, jnp.stack([core, yl])]).astype(I32)
 
-    other, left_a, right_a, own, info, code = lax.optimization_barrier((other, left_a, right_a, own, info, code))
-    left_b, right_b = shifted(other, "x", 1), shifted(other, "x", -1)
+    column = spread(packed, ("yh", "z")).reshape(-1, T, 2 * T)
+    column, packed, info, code = lax.optimization_barrier((column, packed, info, code))
+    low, high = column[:column.shape[0] // 2], column[column.shape[0] // 2:]
+    left_a, right_b = shifted(low, "x", 1), shifted(high, "x", -1)
+    left_b, right_a = shifted(high, "x", 1), shifted(low, "x", -1)
     left2, right2 = shifted(left_a, "x", 1), shifted(right_b, "x", -1)
-    b = left_products(info, own, a_tiles)
-    sums0 = panel_sums(0, code, info, [near, left_a, right_a], b)
-    sums1 = panel_sums(1, code, info, [other, left_b, right_b, left2], b)
-    sums2 = panel_sums(2, code, info, [right2], b, (sums0, sums1))
+
+    b = left_products(spread(packed, COL), a_tiles)
+    sums0 = panel_sums(0, code, info, [column, left_a, right_b], b)
+    sums1 = panel_sums(1, code, info, [left_b, right_a], b)
+    sums2 = panel_sums(2, code, info, [left2, right2], b, (sums0, sums1))
 
     chip = (sums2[0].astype(F32) + swapped(sums2[1], "core", 1).astype(F32)).astype(BF16)
     two = chip[0].astype(F32) + swapped(chip[1], "yl", 1).astype(F32)
@@ -203,9 +195,9 @@
     count = lax.axis_size(ROW)
     ahead = [[(r * NY + y, (r + 1) % count * NY + (y ^ by)) for r in range(count) for y in range(NY)] for by in (0, 2)]
     last = [
+        swapped(theirs[:, :8], "yl", 2),
+        lax.ppermute(mine[:, 8:].astype(BF16), ROW + ("yl",), ahead[0]),
         lax.ppermute(theirs[:, 8:], ROW + ("yl",), ahead[1]),
-        lax.ppermute(mine[:, 8:].astype(BF16), ROW + ("yl",), ahead[0]),
-        swapped(theirs[:, :8], "yl", 2),
     ]
     result = mine[:, :8] + sum(part.astype(F32) for part in last)
     return jnp.stack([result[..., :T], result[..., T:]])

time: 138 us -> 128 us (0.928)
  waiting for transfers between devices: 44 us -> 34.7 us
  starting transfers between devices: 68 us -> 65.6 us
  Pallas kernels: 16 us -> 17.5 us
  local copies, waits for them, and re-layouts: 3.5 us -> 4.92 us
    all_to_all x2, starting transfers between devices: 13.5 us -> 29.7 us  [spread(): return lax.all_to_all(copies, axis, 0, 0, tiled=True)]
    ppermute x6 -> x3, starting transfers between devices: 22.2 us -> 9.45 us  [swapped(): lax.ppermute(value, axis, [(i, i ^ by) for i in range(lax.axis_size(axis))])]
    ppermute x7 -> x6, waiting for transfers between devices: 10.7 us -> 0.27 us  [shifted(): lax.ppermute(value, axis, [(i, (i + by) % count) for i in range(count)])]
    ppermute x7 -> x6, starting transfers between devices: 28.5 us -> 19.5 us  [shifted(): lax.ppermute(value, axis, [(i, (i + by) % count) for i in range(count)])]
    all_to_all x2, waiting for transfers between devices: 14.2 us -> 21.3 us  [spread(): return lax.all_to_all(copies, axis, 0, 0, tiled=True)]
    ppermute x1, waiting for transfers between devices: 9.91 us -> 3.88 us  [body(): lax.ppermute(mine[:, 8:].astype(BF16), ROW + ('yl',), ahead[0])]
    ppermute x1, starting transfers between devices: 1.92 us -> 4.34 us  [body(): lax.ppermute(theirs[:, 8:], ROW + ('yl',), ahead[1])]
    pallas_call x3, Pallas kernels: 11.6 us -> 13.6 us  [panel_sums(): pl.pallas_call(functools.partial(sum_kernel, group, len(chunks), len(befo...]
  transfers between devices with their start and end apart: 17 -> 13, of which waited for: 11 -> 7; matrix products, arithmetic and copies ran while one was open for 4% -> 4% of each run, Pallas kernels for 10% -> 11%
where the time goes in v7:
time: 128 us; the launch traced here: 127 us
  starting transfers between devices  65.6 us (51%)
  waiting for transfers between devices  34.7 us (27%)
  Pallas kernels  17.5 us (14%)
  local copies, waits for them, and re-layouts  4.92 us (4%)
  other arithmetic  3.71 us (3%)
    all_to_all x2, starting transfers between devices, spread(): return lax.all_to_all(copies, axis, 0, 0, tiled=True)  29.7 us
    all_to_all x2, waiting for transfers between devices, spread(): return lax.all_to_all(copies, axis, 0, 0, tiled=True)  21.3 us
    ppermute x6, starting transfers between devices, shifted(): lax.ppermute(value, axis, [(i, (i + by) % count) for i in range(count)])  19.5 us
    pallas_call x3, Pallas kernels, panel_sums(): pl.pallas_call(functools.partial(sum_kernel, group, len(chunks), len(befo...  13.6 us
    ppermute x3, starting transfers between devices, swapped(): lax.ppermute(value, axis, [(i, i ^ by) for i in range(lax.axis_size(axis))])  9.45 us
    ppermute x3, waiting for transfers between devices, swapped(): lax.ppermute(value, axis, [(i, i ^ by) for i in range(lax.axis_size(axis))])  6.88 us
    ppermute x1, starting transfers between devices, body(): lax.ppermute(theirs[:, 8:], ROW + ('yl',), ahead[1])  4.34 us
    pallas_call x1, Pallas kernels, left_products(): pl.pallas_call(left_kernel, in_specs=[vmem, pl.BlockSpec(memory_space=plt...  3.94 us
  transfers between devices with their start and end apart: 13, of which 7 were waited for; matrix products, arithmetic and copies ran while one was open for 4% of the time, Pallas kernels for 11%

profile of v7, /device:TPU:1, one launch (start us, length us, event | category | flops | bytes accessed | tf_op | source)
XLA Modules:
  0.0 126.9 jit_solution(9669288263925611864)
XLA Ops:
  0.0 0.9 slice_bitcast_fusion.8
  0.9 0.1 pad_maximum_fusion.1
  1.0 1.2 broadcast_in_dim.29
  2.2 16.2 %all-to-all-start = ((bf16[16,4,64,128]{3,2,1,0:T(8,128)(2,1)}), bf16[16,4,64,128]{3,2,1,0:T(8,128)(2,1)S(1)}, u32[]{:S(2)}, u32[]{:S(2)}) async-start(bf16[16,4,64,128]{3,2,1,0:T(8,128)(2,1)} %broadcast_in_dim.29), calls=%async_computation | async-start | bytes 2097152 | tf_op jit(solution)/shard_map/all_to_all | solution.py:35
  18.5 0.7 fusion.32
  19.1 0.7 fusion.16
  19.9 0.1 copy.9
  20.0 0.1 eq.59
  20.1 0.7 iota_compare_fusion.3
  20.8 0.1 lt.51
  21.0 0.1 copy.10
  21.1 0.1 sub.87
  21.2 0.1 convert_reduce_fusion
  21.4 0.2 reduce-window.7
  21.6 0.1 pad_add_fusion.refs_1_
  21.6 0.2 fusion.3
  21.9 0.2 select_reduce_fusion
  22.0 19.8 %all-to-all-done = bf16[16,4,64,128]{3,2,1,0:T(8,128)(2,1)S(1)} async-done(((bf16[16,4,64,128]{3,2,1,0:T(8,128)(2,1)}), bf16[16,4,64,128]{3,2,1,0:T(8,128)(2,1)S(1)}, u32[]{:S(2)}, u32[]{:S(2)}) %all-to-all-start) | async-done | bytes 1048608 | tf_op jit(solution)/shard_map/all_to_all | solution.py:35
  41.8 1.1 fusion.33
  42.9 3.1 %collective-permute-start = (bf16[32,64,128]{2,1,0:T(8,128)(2,1)}, bf16[32,64,128]{2,1,0:T(8,128)(2,1)}, u32[]{:S(2)}, u32[]{:S(2)}) collective-permute-start(bf16[32,64,128]{2,1,0:T(8,128)(2,1)} %get-tuple-element.16), channel_id=1, source_target_pairs={{0,8},{8,16},{16,24},{24,0},{1,9},{9,17},{17,25},{25,1},{2,10},{10... | collective-permute-start | bytes 1572872 | tf_op jit(solution)/shard_map/ppermute | solution.py:25
  46.0 3.4 %collective-permute-start.2 = (bf16[32,64,128]{2,1,0:T(8,128)(2,1)}, bf16[32,64,128]{2,1,0:T(8,128)(2,1)}, u32[]{:S(2)}, u32[]{:S(2)}) collective-permute-start(bf16[32,64,128]{2,1,0:T(8,128)(2,1)} %get-tuple-element.15), channel_id=1, source_target_pairs={{0,24},{8,0},{16,8},{24,16},{1,25},{9,1},{17,9},{25,17},{2,26},{10... | collective-permute-start | bytes 1572872 | tf_op jit(solution)/shard_map/ppermute | solution.py:25
  49.4 0.9 broadcast_in_dim.34
  50.4 13.4 %all-to-all-start.1 = ((bf16[8,4,64,128]{3,2,1,0:T(8,128)(2,1)}), bf16[8,4,64,128]{3,2,1,0:T(8,128)(2,1)S(1)}, u32[]{:S(2)}, u32[]{:S(2)}) async-start(bf16[8,4,64,128]{3,2,1,0:T(8,128)(2,1)} %broadcast_in_dim.34), calls=%async_computation.1 | async-start | bytes 1048576 | tf_op jit(solution)/shard_map/all_to_all | solution.py:35
  63.8 1.9 %collective-permute-start.4 = (bf16[32,64,128]{2,1,0:T(8,128)(2,1)}, bf16[32,64,128]{2,1,0:T(8,128)(2,1)S(1)}, u32[]{:S(2)}, u32[]{:S(2)}) collective-permute-start(bf16[32,64,128]{2,1,0:T(8,128)(2,1)} %get-tuple-element.15), channel_id=1, source_target_pairs={{0,8},{8,16},{16,24},{24,0},{1,9},{9,17},{17,25},{25,1},{2,10},{10... | collective-permute-start | bytes 1572872 | tf_op jit(solution)/shard_map/ppermute | solution.py:25
  65.7 4.6 %collective-permute-start.5 = (bf16[32,64,128]{2,1,0:T(8,128)(2,1)}, bf16[32,64,128]{2,1,0:T(8,128)(2,1)}, u32[]{:S(2)}, u32[]{:S(2)}) collective-permute-start(bf16[32,64,128]{2,1,0:T(8,128)(2,1)} %get-tuple-element.16), channel_id=1, source_target_pairs={{0,24},{8,0},{16,8},{24,16},{1,25},{9,1},{17,9},{25,17},{2,26},{10... | collective-permute-start | bytes 1572872 | tf_op jit(solution)/shard_map/ppermute | solution.py:25
  70.3 0.0 collective-permute-done.refs_3_
  70.3 1.9 %collective-permute-start.1 = (bf16[32,64,128]{2,1,0:T(8,128)(2,1)}, bf16[32,64,128]{2,1,0:T(8,128)(2,1)S(1)}, u32[]{:S(2)}, u32[]{:S(2)}) collective-permute-start(bf16[32,64,128]{2,1,0:T(8,128)(2,1)} %collective-permute-done.refs_3_), channel_id=1, source_target_pairs={{0,8},{8,16},{16,24},{24,0},{1,9},{9,17},{17,25},{25,1},{2,10},{10... | collective-permute-start | bytes 1572872 | tf_op jit(solution)/shard_map/ppermute | solution.py:25
  72.2 0.0 collective-permute-done.2.refs_4_
  72.2 4.6 %collective-permute-start.3 = (bf16[32,64,128]{2,1,0:T(8,128)(2,1)}, bf16[32,64,128]{2,1,0:T(8,128)(2,1)S(1)}, u32[]{:S(2)}, u32[]{:S(2)}) collective-permute-start(bf16[32,64,128]{2,1,0:T(8,128)(2,1)} %collective-permute-done.2.refs_4_), channel_id=1, source_target_pairs={{0,24},{8,0},{16,8},{24,16},{1,25},{9,1},{17,9},{25,17},{2,26},{10... | collective-permute-start | bytes 1572872 | tf_op jit(solution)/shard_map/ppermute | solution.py:25
  76.8 1.5 %all-to-all-done.1.own_ref = bf16[8,4,64,128]{3,2,1,0:T(8,128)(2,1)S(1)} async-done(((bf16[8,4,64,128]{3,2,1,0:T(8,128)(2,1)}), bf16[8,4,64,128]{3,2,1,0:T(8,128)(2,1)S(1)}, u32[]{:S(2)}, u32[]{:S(2)}) %all-to-all-start.1) | async-done | bytes 524320 | tf_op jit(solution)/shard_map/all_to_all | solution.py:35
  78.3 3.9 %left_products.1 = bf16[2,4,8,6,64,64]{5,4,3,2,1,0:T(8,128)(2,1)S(1)} custom-call(bf16[8,4,64,128]{3,2,1,0:T(8,128)(2,1)S(1)} %all-to-all-done.1.own_ref, bf16[2,4,8,6,64,64]{5,4,3,2,1,0:T(8,128)(2,1)} %bitcast.49), custom_call_target="tpu_custom_call" | custom-call | flops 201326592 | bytes 16777216 | tf_op jit(solution)/shard_map/left_products/pallas_call | solution.py:62
  82.3 4.3 %panel_sums_1.1.refs_6_ = bf16[2,2,2,27,16,128]{5,4,3,2,1,0:T(8,128)(2,1)S(1)} custom-call(s32[408]{0:T(512)S(1)} %broadcast_add_fusion.refs_0_, s32[8]{0:T(128)S(1)} %pad_add_fusion.refs_1_, bf16[32,64,128]{2,1,0:T(8,128)(2,1)S(1)} %collective-permute-done.4.refs_2_, bf16[32,64,128]{2,1,0:T(8,128)(2,1)} %collective-permute-done.5.refs_3_, ...), custom_call_target="tpu_custom_call" | custom-call | flops 67108864 | bytes 8388608 | tf_op jit(solution)/shard_map/panel_sums_1/pallas_call | solution.py:135
  86.5 6.0 %panel_sums_0.1.refs_5_ = bf16[2,2,2,27,16,128]{5,4,3,2,1,0:T(8,128)(2,1)S(1)} custom-call(s32[408]{0:T(512)S(1)} %broadcast_add_fusion.refs_0_, s32[8]{0:T(128)S(1)} %pad_add_fusion.refs_1_, bf16[64,64,128]{2,1,0:T(8,128)(2,1)S(1)} %bitcast.48, bf16[32,64,128]{2,1,0:T(8,128)(2,1)} %collective-permute-done.refs_3_, ...), custom_call_target="tpu_custom_call" | custom-call | flops 134217728 | bytes 8388608 | tf_op jit(solution)/shard_map/panel_sums_0/pallas_call | solution.py:135
  92.6 0.3 collective-permute-done.3.refs_3_
  92.8 3.2 %panel_sums_2.1 = bf16[2,2,2,27,16,128]{5,4,3,2,1,0:T(8,128)(2,1)S(1)} custom-call(s32[408]{0:T(512)S(1)} %broadcast_add_fusion.refs_0_, s32[8]{0:T(128)S(1)} %pad_add_fusion.refs_1_, bf16[32,64,128]{2,1,0:T(8,128)(2,1)S(1)} %collective-permute-done.1.refs_2_, bf16[32,64,128]{2,1,0:T(8,128)(2,1)S(1)} %collective-permute-done.3.refs_3_, ...), custom_call_target="tpu_custom_call" | custom-call | flops 67108864 | bytes 8388608 | tf_op jit(solution)/shard_map/panel_sums_2/pallas_call | solution.py:135
  96.1 3.5 %collective-permute-start.6 = (bf16[2,2,27,16,128]{4,3,2,1,0:T(8,128)(2,1)S(1)}, bf16[2,2,27,16,128]{4,3,2,1,0:T(8,128)(2,1)S(1)}, u32[]{:S(2)}, u32[]{:S(2)}) collective-permute-start(bf16[2,2,27,16,128]{4,3,2,1,0:T(8,128)(2,1)S(1)} %slice_bitcast_fusion), channel_id=1, source_target_pairs={{0,1},{1,0},{2,3},{3,2},{4,5},{5,4},{6,7},{7,6},{8,9},{9,8},{10,11... | collective-permute-start | bytes 1327112 | tf_op jit(solution)/shard_map/ppermute | solution.py:29
  99.7 1.4 %collective-permute-done.6 = bf16[2,2,27,16,128]{4,3,2,1,0:T(8,128)(2,1)S(1)} collective-permute-done((bf16[2,2,27,16,128]{4,3,2,1,0:T(8,128)(2,1)S(1)}, bf16[2,2,27,16,128]{4,3,2,1,0:T(8,128)(2,1)S(1)}, u32[]{:S(2)}, u32[]{:S(2)}) %collective-permute-start.6) | collective-permute-done | bytes 442400 | tf_op jit(solution)/shard_map/ppermute | solution.py:29
  101.1 0.1 fusion.4
  101.2 3.7 %collective-permute-start.7 = (bf16[2,27,16,128]{3,2,1,0:T(8,128)(2,1)S(1)}, bf16[2,27,16,128]{3,2,1,0:T(8,128)(2,1)S(1)}, u32[]{:S(2)}, u32[]{:S(2)}) collective-permute-start(bf16[2,27,16,128]{3,2,1,0:T(8,128)(2,1)S(1)} %slice_bitcast_fusion.3), channel_id=1, source_target_pairs={{0,2},{2,0},{4,6},{6,4},{1,3},{3,1},{5,7},{7,5},{8,10},{10,8},{12,... | collective-permute-start | bytes 663560 | tf_op jit(solution)/shard_map/ppermute | solution.py:29
  104.9 5.5 %collective-permute-done.7 = bf16[2,27,16,128]{3,2,1,0:T(8,128)(2,1)S(1)} collective-permute-done((bf16[2,27,16,128]{3,2,1,0:T(8,128)(2,1)S(1)}, bf16[2,27,16,128]{3,2,1,0:T(8,128)(2,1)S(1)}, u32[]{:S(2)}, u32[]{:S(2)}) %collective-permute-start.7) | collective-permute-done | bytes 221216 | tf_op jit(solution)/shard_map/ppermute | solution.py:29
  110.4 0.1 convert_add_fusion.1
  110.5 2.6 %collective-permute-start.9 = (bf16[27,8,128]{2,1,0:T(8,128)(2,1)S(1)}, bf16[27,8,128]{2,1,0:T(8,128)(2,1)S(1)}, u32[]{:S(2)}, u32[]{:S(2)}) collective-permute-start(bf16[27,8,128]{2,1,0:T(8,128)(2,1)S(1)} %slice.96), channel_id=1, source_target_pairs={{0,8},{2,10},{4,12},{6,14},{8,16},{10,18},{12,20},{14,22},{16,24},... | collective-permute-start | bytes 165896 | tf_op jit(solution)/shard_map/ppermute | solution.py:199
  113.2 4.3 %collective-permute-start.10 = (bf16[27,8,128]{2,1,0:T(8,128)(2,1)S(1)}, bf16[27,8,128]{2,1,0:T(8,128)(2,1)S(1)}, u32[]{:S(2)}, u32[]{:S(2)}) collective-permute-start(bf16[27,8,128]{2,1,0:T(8,128)(2,1)S(1)} %get-tuple-element.22), channel_id=1, source_target_pairs={{0,12},{2,14},{4,8},{6,10},{8,20},{10,22},{12,16},{14,18},{16,28},... | collective-permute-start | bytes 165896 | tf_op jit(solution)/shard_map/ppermute | solution.py:200
  117.5 2.2 %collective-permute-start.8 = (bf16[27,8,128]{2,1,0:T(8,128)(2,1)S(1)}, bf16[27,8,128]{2,1,0:T(8,128)(2,1)S(1)}, u32[]{:S(2)}, u32[]{:S(2)}) collective-permute-start(bf16[27,8,128]{2,1,0:T(8,128)(2,1)S(1)} %get-tuple-element.21), channel_id=1, source_target_pairs={{0,4},{2,6},{4,0},{6,2},{1,5},{3,7},{5,1},{7,3},{8,12},{10,14},{12... | collective-permute-start | bytes 165896 | tf_op jit(solution)/shard_map/ppermute | solution.py:29
  119.8 3.9 %collective-permute-done.9 = bf16[27,8,128]{2,1,0:T(8,128)(2,1)S(1)} collective-permute-done((bf16[27,8,128]{2,1,0:T(8,128)(2,1)S(1)}, bf16[27,8,128]{2,1,0:T(8,128)(2,1)S(1)}, u32[]{:S(2)}, u32[]{:S(2)}) %collective-permute-start.9) | collective-permute-done | bytes 55328 | tf_op jit(solution)/shard_map/ppermute | solution.py:199
  123.7 2.4 %collective-permute-done.10 = bf16[27,8,128]{2,1,0:T(8,128)(2,1)S(1)} collective-permute-done((bf16[27,8,128]{2,1,0:T(8,128)(2,1)S(1)}, bf16[27,8,128]{2,1,0:T(8,128)(2,1)S(1)}, u32[]{:S(2)}, u32[]{:S(2)}) %collective-permute-start.10) | collective-permute-done | bytes 55328 | tf_op jit(solution)/shard_map/ppermute | solution.py:200
  126.1 0.1 slice_bitcast_fusion.6
  126.2 0.7 pad_maximum_fusion
  (15 shorter events, 0.2 us)
Async XLA Ops:
  2.2 39.6 %all-to-all-start = ((bf16[16,4,64,128]{3,2,1,0:T(8,128)(2,1)}), bf16[16,4,64,128]{3,2,1,0:T(8,128)(2,1)S(1)}, u32[]{:S(2)}, u32[]{:S(2)}) async-start(bf16[16,4,64,128]{3,2,1,0:T(8,128)(2,1)} %broadcast_in_dim.29), calls=%async_computation | async-start | bytes 2097152 | tf_op jit(solution)/shard_map/all_to_all | solution.py:35
  42.9 27.4 %collective-permute-start = (bf16[32,64,128]{2,1,0:T(8,128)(2,1)}, bf16[32,64,128]{2,1,0:T(8,128)(2,1)}, u32[]{:S(2)}, u32[]{:S(2)}) collective-permute-start(bf16[32,64,128]{2,1,0:T(8,128)(2,1)} %get-tuple-element.16), channel_id=1, source_target_pairs={{0,8},{8,16},{16,24},{24,0},{1,9},{9,17},{17,25},{25,1},{2,10},{10... | collective-permute-start | bytes 1572872 | tf_op jit(solution)/shard_map/ppermute | solution.py:25
  46.0 26.2 %collective-permute-start.2 = (bf16[32,64,128]{2,1,0:T(8,128)(2,1)}, bf16[32,64,128]{2,1,0:T(8,128)(2,1)}, u32[]{:S(2)}, u32[]{:S(2)}) collective-permute-start(bf16[32,64,128]{2,1,0:T(8,128)(2,1)} %get-tuple-element.15), channel_id=1, source_target_pairs={{0,24},{8,0},{16,8},{24,16},{1,25},{9,1},{17,9},{25,17},{2,26},{10... | collective-permute-start | bytes 1572872 | tf_op jit(solution)/shard_map/ppermute | solution.py:25
  50.4 27.9 %all-to-all-start.1 = ((bf16[8,4,64,128]{3,2,1,0:T(8,128)(2,1)}), bf16[8,4,64,128]{3,2,1,0:T(8,128)(2,1)S(1)}, u32[]{:S(2)}, u32[]{:S(2)}) async-start(bf16[8,4,64,128]{3,2,1,0:T(8,128)(2,1)} %broadcast_in_dim.34), calls=%async_computation.1 | async-start | bytes 1048576 | tf_op jit(solution)/shard_map/all_to_all | solution.py:35
  63.8 18.4 %collective-permute-start.4 = (bf16[32,64,128]{2,1,0:T(8,128)(2,1)}, bf16[32,64,128]{2,1,0:T(8,128)(2,1)S(1)}, u32[]{:S(2)}, u32[]{:S(2)}) collective-permute-start(bf16[32,64,128]{2,1,0:T(8,128)(2,1)} %get-tuple-element.15), channel_id=1, source_target_pairs={{0,8},{8,16},{16,24},{24,0},{1,9},{9,17},{17,25},{25,1},{2,10},{10... | collective-permute-start | bytes 1572872 | tf_op jit(solution)/shard_map/ppermute | solution.py:25
  65.7 16.5 %collective-permute-start.5 = (bf16[32,64,128]{2,1,0:T(8,128)(2,1)}, bf16[32,64,128]{2,1,0:T(8,128)(2,1)}, u32[]{:S(2)}, u32[]{:S(2)}) collective-permute-start(bf16[32,64,128]{2,1,0:T(8,128)(2,1)} %get-tuple-element.16), channel_id=1, source_target_pairs={{0,24},{8,0},{16,8},{24,16},{1,25},{9,1},{17,9},{25,17},{2,26},{10... | collective-permute-start | bytes 1572872 | tf_op jit(solution)/shard_map/ppermute | solution.py:25
  70.3 22.3 %collective-permute-start.1 = (bf16[32,64,128]{2,1,0:T(8,128)(2,1)}, bf16[32,64,128]{2,1,0:T(8,128)(2,1)S(1)}, u32[]{:S(2)}, u32[]{:S(2)}) collective-permute-start(bf16[32,64,128]{2,1,0:T(8,128)(2,1)} %collective-permute-done.refs_3_), channel_id=1, source_target_pairs={{0,8},{8,16},{16,24},{24,0},{1,9},{9,17},{17,25},{25,1},{2,10},{10... | collective-permute-start | bytes 1572872 | tf_op jit(solution)/shard_map/ppermute | solution.py:25
  72.2 20.6 %collective-permute-start.3 = (bf16[32,64,128]{2,1,0:T(8,128)(2,1)}, bf16[32,64,128]{2,1,0:T(8,128)(2,1)S(1)}, u32[]{:S(2)}, u32[]{:S(2)}) collective-permute-start(bf16[32,64,128]{2,1,0:T(8,128)(2,1)} %collective-permute-done.2.refs_4_), channel_id=1, source_target_pairs={{0,24},{8,0},{16,8},{24,16},{1,25},{9,1},{17,9},{25,17},{2,26},{10... | collective-permute-start | bytes 1572872 | tf_op jit(solution)/shard_map/ppermute | solution.py:25
  96.1 4.9 %collective-permute-start.6 = (bf16[2,2,27,16,128]{4,3,2,1,0:T(8,128)(2,1)S(1)}, bf16[2,2,27,16,128]{4,3,2,1,0:T(8,128)(2,1)S(1)}, u32[]{:S(2)}, u32[]{:S(2)}) collective-permute-start(bf16[2,2,27,16,128]{4,3,2,1,0:T(8,128)(2,1)S(1)} %slice_bitcast_fusion), channel_id=1, source_target_pairs={{0,1},{1,0},{2,3},{3,2},{4,5},{5,4},{6,7},{7,6},{8,9},{9,8},{10,11... | collective-permute-start | bytes 1327112 | tf_op jit(solution)/shard_map/ppermute | solution.py:29
  101.2 9.2 %collective-permute-start.7 = (bf16[2,27,16,128]{3,2,1,0:T(8,128)(2,1)S(1)}, bf16[2,27,16,128]{3,2,1,0:T(8,128)(2,1)S(1)}, u32[]{:S(2)}, u32[]{:S(2)}) collective-permute-start(bf16[2,27,16,128]{3,2,1,0:T(8,128)(2,1)S(1)} %slice_bitcast_fusion.3), channel_id=1, source_target_pairs={{0,2},{2,0},{4,6},{6,4},{1,3},{3,1},{5,7},{7,5},{8,10},{10,8},{12,... | collective-permute-start | bytes 663560 | tf_op jit(solution)/shard_map/ppermute | solution.py:29
  110.5 13.1 %collective-permute-start.9 = (bf16[27,8,128]{2,1,0:T(8,128)(2,1)S(1)}, bf16[27,8,128]{2,1,0:T(8,128)(2,1)S(1)}, u32[]{:S(2)}, u32[]{:S(2)}) collective-permute-start(bf16[27,8,128]{2,1,0:T(8,128)(2,1)S(1)} %slice.96), channel_id=1, source_target_pairs={{0,8},{2,10},{4,12},{6,14},{8,16},{10,18},{12,20},{14,22},{16,24},... | collective-permute-start | bytes 165896 | tf_op jit(solution)/shard_map/ppermute | solution.py:199
  113.2 12.9 %collective-permute-start.10 = (bf16[27,8,128]{2,1,0:T(8,128)(2,1)S(1)}, bf16[27,8,128]{2,1,0:T(8,128)(2,1)S(1)}, u32[]{:S(2)}, u32[]{:S(2)}) collective-permute-start(bf16[27,8,128]{2,1,0:T(8,128)(2,1)S(1)} %get-tuple-element.22), channel_id=1, source_target_pairs={{0,12},{2,14},{4,8},{6,10},{8,20},{10,22},{12,16},{14,18},{16,28},... | collective-permute-start | bytes 165896 | tf_op jit(solution)/shard_map/ppermute | solution.py:200
  117.5 8.5 %collective-permute-start.8 = (bf16[27,8,128]{2,1,0:T(8,128)(2,1)S(1)}, bf16[27,8,128]{2,1,0:T(8,128)(2,1)S(1)}, u32[]{:S(2)}, u32[]{:S(2)}) collective-permute-start(bf16[27,8,128]{2,1,0:T(8,128)(2,1)S(1)} %get-tuple-element.21), channel_id=1, source_target_pairs={{0,4},{2,6},{4,0},{6,2},{1,5},{3,7},{5,1},{7,3},{8,12},{10,14},{12... | collective-permute-start | bytes 165896 | tf_op jit(solution)/shard_map/ppermute | solution.py:29

commit v8 on v7

--- a/solution.py
+++ b/solution.py
@@ -78,7 +78,7 @@
     b_ref = refs[2 + n_chunks]
     before = refs[3 + n_chunks:3 + n_chunks + n_before]
     out_ref, panel, acc, sems = refs[-4:]
-    core, yl = info_ref[6], info_ref[7]
+    core = info_ref[6]
     copies, at = [], 0
     for n, chunk in enumerate(chunks):
         size = chunk.shape[0]
@@ -120,8 +120,7 @@
     def _(k):
         for o in range(8):
             tile = jnp.concatenate([acc[k, o * 8:(o + 1) * 8], acc[KC + k, o * 8:(o + 1) * 8]], axis=0)
-            far = jnp.bitwise_xor(yl, o // 2)
-            place = (jnp.bitwise_xor(core, o % 2), jnp.bitwise_and(far, 1), jnp.right_shift(far, 1), k)
+            place = (jnp.bitwise_xor(core, o % 2), o // 4, o // 2 % 2, k)
             for earlier in before:
                 tile = tile + earlier[place].astype(F32)
             out_ref[place] = tile.astype(BF16)
@@ -189,17 +188,20 @@
     sums1 = panel_sums(1, code, info, [left_b, right_a], b)
     sums2 = panel_sums(2, code, info, [left2, right2], b, (sums0, sums1))
 
-    chip = (sums2[0].astype(F32) + swapped(sums2[1], "core", 1).astype(F32)).astype(BF16)
-    two = chip[0].astype(F32) + swapped(chip[1], "yl", 1).astype(F32)
-    mine, theirs = two[0], two[1].astype(BF16)
+    chip = sums2[0].astype(F32) + swapped(sums2[1], "core", 1).astype(F32)
+    staying = chip[..., :8, :].astype(BF16).reshape(NY, KC, 8, 2 * T)
+    staying = lax.all_to_all(staying, "yl", 0, 0, tiled=True)
+    coming = chip[..., 8:, :].astype(BF16)
+    bit0, bit1 = yl % 2, yl // 2
+    pick = functools.partial(lax.dynamic_index_in_dim, keepdims=False)
+    two = pick(coming, bit0, 1).astype(F32) + swapped(pick(coming, 1 - bit0, 1), "yl", 1).astype(F32)
     count = lax.axis_size(ROW)
     ahead = [[(r * NY + y, (r + 1) % count * NY + (y ^ by)) for r in range(count) for y in range(NY)] for by in (0, 2)]
     last = [
-        swapped(theirs[:, :8], "yl", 2),
-        lax.ppermute(mine[:, 8:].astype(BF16), ROW + ("yl",), ahead[0]),
-        lax.ppermute(theirs[:, 8:], ROW + ("yl",), ahead[1]),
+        lax.ppermute(pick(two, bit1, 0).astype(BF16), ROW + ("yl",), ahead[0]),
+        lax.ppermute(pick(two, 1 - bit1, 0).astype(BF16), ROW + ("yl",), ahead[1]),
     ]
-    result = mine[:, :8] + sum(part.astype(F32) for part in last)
+    result = jnp.sum(staying.astype(F32), axis=0) + sum(part.astype(F32) for part in last)
     return jnp.stack([result[..., :T], result[..., T:]])
 
 

time: 128 us -> 127 us (level)
  waiting for transfers between devices: 34.7 us -> 31.4 us
    ppermute x3 -> x2, waiting for transfers between devices: 6.88 us -> 1.38 us  [swapped(): lax.ppermute(value, axis, [(i, i ^ by) for i in range(lax.axis_size(axis))])]
    all_to_all x0 -> x1, starting transfers between devices: none -> 3.39 us  [body(): staying = lax.all_to_all(staying, 'yl', 0, 0, tiled=True)]
    ppermute x3 -> x2, starting transfers between devices: 9.45 us -> 6.14 us  [swapped(): lax.ppermute(value, axis, [(i, i ^ by) for i in range(lax.axis_size(axis))])]
    ppermute x2, waiting for transfers between devices: 6.27 us -> 8.11 us  [the longest x1 5.55 us: body(): lax.ppermute(pick(two, bit1, 0).astype(BF16), ROW + ('yl',), ahead[0])]
  transfers between devices with their start and end apart: 13 -> 13, of which waited for: 7 -> 6; matrix products, arithmetic and copies ran while one was open for 4% -> 4% of each run, Pallas kernels for 11% -> 11%
where the time goes in v8:
time: 127 us; the launch traced here: 125 us
  starting transfers between devices  66.2 us (52%)
  waiting for transfers between devices  31.4 us (25%)
  Pallas kernels  17.7 us (14%)
  local copies, waits for them, and re-layouts  5.63 us (4%)
  other arithmetic  3.71 us (3%)
    all_to_all x2, starting transfers between devices, spread(): return lax.all_to_all(copies, axis, 0, 0, tiled=True)  29.7 us
    all_to_all x2, waiting for transfers between devices, spread(): return lax.all_to_all(copies, axis, 0, 0, tiled=True)  21.3 us
    ppermute x6, starting transfers between devices, shifted(): lax.ppermute(value, axis, [(i, (i + by) % count) for i in range(count)])  19.5 us
    pallas_call x3, Pallas kernels, panel_sums(): pl.pallas_call(functools.partial(sum_kernel, group, len(chunks), len(befo...  13.8 us
    ppermute x2, starting transfers between devices, swapped(): lax.ppermute(value, axis, [(i, i ^ by) for i in range(lax.axis_size(axis))])  6.14 us
    ppermute x1, waiting for transfers between devices, body(): lax.ppermute(pick(two, bit1, 0).astype(BF16), ROW + ('yl',), ahead[0])  5.55 us
    ppermute x1, starting transfers between devices, body(): lax.ppermute(pick(two, 1 - bit1, 0).astype(BF16), ROW + ('yl',), ahead[1])  4.34 us
    pallas_call x1, Pallas kernels, left_products(): pl.pallas_call(left_kernel, in_specs=[vmem, pl.BlockSpec(memory_space=plt...  3.94 us
  transfers between devices with their start and end apart: 13, of which 6 were waited for; matrix products, arithmetic and copies ran while one was open for 4% of the time, Pallas kernels for 11%

profile of v8, /device:TPU:1, one launch (start us, length us, event | category | flops | bytes accessed | tf_op | source)
XLA Modules:
  0.0 125.2 jit_solution(9260798722866347709)
XLA Ops:
  0.0 0.9 slice_bitcast_fusion.5
  0.9 0.1 pad_maximum_fusion.1
  1.0 1.2 broadcast_in_dim.29
  2.2 16.2 %all-to-all-start = ((bf16[16,4,64,128]{3,2,1,0:T(8,128)(2,1)}), bf16[16,4,64,128]{3,2,1,0:T(8,128)(2,1)S(1)}, u32[]{:S(2)}, u32[]{:S(2)}) async-start(bf16[16,4,64,128]{3,2,1,0:T(8,128)(2,1)} %broadcast_in_dim.29), calls=%async_computation | async-start | bytes 2097152 | tf_op jit(solution)/shard_map/all_to_all | solution.py:35
  18.4 0.7 fusion.33
  19.1 0.7 fusion.17
  19.9 0.1 copy.9
  19.9 0.1 eq.61
  20.1 0.7 iota_compare_fusion.3
  20.8 0.1 lt.71
  21.0 0.1 copy.10
  21.1 0.1 sub.97
  21.2 0.1 convert_reduce_fusion.1
  21.3 0.2 reduce-window.7
  21.5 0.1 pad_add_fusion.refs_1_
  21.6 0.2 fusion.3
  21.8 0.2 select_reduce_fusion
  22.0 19.8 %all-to-all-done = bf16[16,4,64,128]{3,2,1,0:T(8,128)(2,1)S(1)} async-done(((bf16[16,4,64,128]{3,2,1,0:T(8,128)(2,1)}), bf16[16,4,64,128]{3,2,1,0:T(8,128)(2,1)S(1)}, u32[]{:S(2)}, u32[]{:S(2)}) %all-to-all-start) | async-done | bytes 1048608 | tf_op jit(solution)/shard_map/all_to_all | solution.py:35
  41.8 1.1 fusion.34
  42.9 3.1 %collective-permute-start = (bf16[32,64,128]{2,1,0:T(8,128)(2,1)}, bf16[32,64,128]{2,1,0:T(8,128)(2,1)}, u32[]{:S(2)}, u32[]{:S(2)}) collective-permute-start(bf16[32,64,128]{2,1,0:T(8,128)(2,1)} %get-tuple-element.16), channel_id=1, source_target_pairs={{0,8},{8,16},{16,24},{24,0},{1,9},{9,17},{17,25},{25,1},{2,10},{10... | collective-permute-start | bytes 1572872 | tf_op jit(solution)/shard_map/ppermute | solution.py:25
  46.0 3.4 %collective-permute-start.2 = (bf16[32,64,128]{2,1,0:T(8,128)(2,1)}, bf16[32,64,128]{2,1,0:T(8,128)(2,1)}, u32[]{:S(2)}, u32[]{:S(2)}) collective-permute-start(bf16[32,64,128]{2,1,0:T(8,128)(2,1)} %get-tuple-element.15), channel_id=1, source_target_pairs={{0,24},{8,0},{16,8},{24,16},{1,25},{9,1},{17,9},{25,17},{2,26},{10... | collective-permute-start | bytes 1572872 | tf_op jit(solution)/shard_map/ppermute | solution.py:25
  49.4 0.9 broadcast_in_dim.34
  50.3 13.4 %all-to-all-start.1 = ((bf16[8,4,64,128]{3,2,1,0:T(8,128)(2,1)}), bf16[8,4,64,128]{3,2,1,0:T(8,128)(2,1)S(1)}, u32[]{:S(2)}, u32[]{:S(2)}) async-start(bf16[8,4,64,128]{3,2,1,0:T(8,128)(2,1)} %broadcast_in_dim.34), calls=%async_computation.1 | async-start | bytes 1048576 | tf_op jit(solution)/shard_map/all_to_all | solution.py:35
  63.8 1.9 %collective-permute-start.4 = (bf16[32,64,128]{2,1,0:T(8,128)(2,1)}, bf16[32,64,128]{2,1,0:T(8,128)(2,1)S(1)}, u32[]{:S(2)}, u32[]{:S(2)}) collective-permute-start(bf16[32,64,128]{2,1,0:T(8,128)(2,1)} %get-tuple-element.15), channel_id=1, source_target_pairs={{0,8},{8,16},{16,24},{24,0},{1,9},{9,17},{17,25},{25,1},{2,10},{10... | collective-permute-start | bytes 1572872 | tf_op jit(solution)/shard_map/ppermute | solution.py:25
  65.7 4.6 %collective-permute-start.5 = (bf16[32,64,128]{2,1,0:T(8,128)(2,1)}, bf16[32,64,128]{2,1,0:T(8,128)(2,1)}, u32[]{:S(2)}, u32[]{:S(2)}) collective-permute-start(bf16[32,64,128]{2,1,0:T(8,128)(2,1)} %get-tuple-element.16), channel_id=1, source_target_pairs={{0,24},{8,0},{16,8},{24,16},{1,25},{9,1},{17,9},{25,17},{2,26},{10... | collective-permute-start | bytes 1572872 | tf_op jit(solution)/shard_map/ppermute | solution.py:25
  70.3 0.0 collective-permute-done.refs_3_
  70.3 1.9 %collective-permute-start.1 = (bf16[32,64,128]{2,1,0:T(8,128)(2,1)}, bf16[32,64,128]{2,1,0:T(8,128)(2,1)S(1)}, u32[]{:S(2)}, u32[]{:S(2)}) collective-permute-start(bf16[32,64,128]{2,1,0:T(8,128)(2,1)} %collective-permute-done.refs_3_), channel_id=1, source_target_pairs={{0,8},{8,16},{16,24},{24,0},{1,9},{9,17},{17,25},{25,1},{2,10},{10... | collective-permute-start | bytes 1572872 | tf_op jit(solution)/shard_map/ppermute | solution.py:25
  72.2 0.0 collective-permute-done.2.refs_4_
  72.2 4.6 %collective-permute-start.3 = (bf16[32,64,128]{2,1,0:T(8,128)(2,1)}, bf16[32,64,128]{2,1,0:T(8,128)(2,1)S(1)}, u32[]{:S(2)}, u32[]{:S(2)}) collective-permute-start(bf16[32,64,128]{2,1,0:T(8,128)(2,1)} %collective-permute-done.2.refs_4_), channel_id=1, source_target_pairs={{0,24},{8,0},{16,8},{24,16},{1,25},{9,1},{17,9},{25,17},{2,26},{10... | collective-permute-start | bytes 1572872 | tf_op jit(solution)/shard_map/ppermute | solution.py:25
  76.8 1.5 %all-to-all-done.1.own_ref = bf16[8,4,64,128]{3,2,1,0:T(8,128)(2,1)S(1)} async-done(((bf16[8,4,64,128]{3,2,1,0:T(8,128)(2,1)}), bf16[8,4,64,128]{3,2,1,0:T(8,128)(2,1)S(1)}, u32[]{:S(2)}, u32[]{:S(2)}) %all-to-all-start.1) | async-done | bytes 524320 | tf_op jit(solution)/shard_map/all_to_all | solution.py:35
  78.3 3.9 %left_products.1 = bf16[2,4,8,6,64,64]{5,4,3,2,1,0:T(8,128)(2,1)S(1)} custom-call(bf16[8,4,64,128]{3,2,1,0:T(8,128)(2,1)S(1)} %all-to-all-done.1.own_ref, bf16[2,4,8,6,64,64]{5,4,3,2,1,0:T(8,128)(2,1)} %bitcast.48), custom_call_target="tpu_custom_call" | custom-call | flops 201326592 | bytes 16777216 | tf_op jit(solution)/shard_map/left_products/pallas_call | solution.py:62
  82.2 0.0 collective-permute-done.4.refs_2_
  82.2 4.0 %panel_sums_1.1.refs_6_ = bf16[2,2,2,27,16,128]{5,4,3,2,1,0:T(8,128)(2,1)S(1)} custom-call(s32[408]{0:T(512)S(1)} %broadcast_add_fusion.refs_0_, s32[8]{0:T(128)S(1)} %pad_add_fusion.refs_1_, bf16[32,64,128]{2,1,0:T(8,128)(2,1)S(1)} %collective-permute-done.4.refs_2_, bf16[32,64,128]{2,1,0:T(8,128)(2,1)} %collective-permute-done.5.refs_3_, ...), custom_call_target="tpu_custom_call" | custom-call | flops 67108864 | bytes 8388608 | tf_op jit(solution)/shard_map/panel_sums_1/pallas_call | solution.py:134
  86.2 6.0 %panel_sums_0.1.refs_5_ = bf16[2,2,2,27,16,128]{5,4,3,2,1,0:T(8,128)(2,1)S(1)} custom-call(s32[408]{0:T(512)S(1)} %broadcast_add_fusion.refs_0_, s32[8]{0:T(128)S(1)} %pad_add_fusion.refs_1_, bf16[64,64,128]{2,1,0:T(8,128)(2,1)S(1)} %bitcast.47, bf16[32,64,128]{2,1,0:T(8,128)(2,1)} %collective-permute-done.refs_3_, ...), custom_call_target="tpu_custom_call" | custom-call | flops 134217728 | bytes 8388608 | tf_op jit(solution)/shard_map/panel_sums_0/pallas_call | solution.py:134
  92.2 0.6 collective-permute-done.3.refs_3_
  92.8 3.8 %panel_sums_2.1 = bf16[2,2,2,27,16,128]{5,4,3,2,1,0:T(8,128)(2,1)S(1)} custom-call(s32[408]{0:T(512)S(1)} %broadcast_add_fusion.refs_0_, s32[8]{0:T(128)S(1)} %pad_add_fusion.refs_1_, bf16[32,64,128]{2,1,0:T(8,128)(2,1)S(1)} %collective-permute-done.1.refs_2_, bf16[32,64,128]{2,1,0:T(8,128)(2,1)S(1)} %collective-permute-done.3.refs_3_, ...), custom_call_target="tpu_custom_call" | custom-call | flops 67108864 | bytes 8388608 | tf_op jit(solution)/shard_map/panel_sums_2/pallas_call | solution.py:134
  96.7 2.8 %collective-permute-start.6 = (bf16[2,2,27,16,128]{4,3,2,1,0:T(8,128)(2,1)S(1)}, bf16[2,2,27,16,128]{4,3,2,1,0:T(8,128)(2,1)S(1)}, u32[]{:S(2)}, u32[]{:S(2)}) collective-permute-start(bf16[2,2,27,16,128]{4,3,2,1,0:T(8,128)(2,1)S(1)} %slice_bitcast_fusion), channel_id=1, source_target_pairs={{0,1},{1,0},{2,3},{3,2},{4,5},{5,4},{6,7},{7,6},{8,9},{9,8},{10,11... | collective-permute-start | bytes 1327112 | tf_op jit(solution)/shard_map/ppermute | solution.py:29
  99.5 1.4 %collective-permute-done.6 = bf16[2,2,27,16,128]{4,3,2,1,0:T(8,128)(2,1)S(1)} collective-permute-done((bf16[2,2,27,16,128]{4,3,2,1,0:T(8,128)(2,1)S(1)}, bf16[2,2,27,16,128]{4,3,2,1,0:T(8,128)(2,1)S(1)}, u32[]{:S(2)}, u32[]{:S(2)}) %collective-permute-start.6) | collective-permute-done | bytes 442400 | tf_op jit(solution)/shard_map/ppermute | solution.py:29
  100.8 0.1 fusion.4
  101.0 0.8 fusion.35
  101.7 3.4 %collective-permute-start.7 = (bf16[2,27,8,128]{3,2,1,0:T(8,128)(2,1)S(1)}, bf16[2,27,8,128]{3,2,1,0:T(8,128)(2,1)S(1)}, u32[]{:S(2)}, u32[]{:S(2)}) collective-permute-start(bf16[2,27,8,128]{3,2,1,0:T(8,128)(2,1)S(1)} %dynamic-slice_bitcast_fusion), channel_id=1, source_target_pairs={{0,2},{2,0},{4,6},{6,4},{1,3},{3,1},{5,7},{7,5},{8,10},{10,8},{12,... | collective-permute-start | bytes 331784 | tf_op jit(solution)/shard_map/ppermute | solution.py:29
  105.2 3.4 %all-to-all-start.2 = ((bf16[4,27,8,128]{3,2,1,0:T(8,128)(2,1)}), bf16[4,27,8,128]{3,2,1,0:T(8,128)(2,1)S(1)}, u32[]{:S(2)}, u32[]{:S(2)}) async-start(bf16[4,27,8,128]{3,2,1,0:T(8,128)(2,1)} %bitcast.12), calls=%async_computation.2 | async-start | bytes 442368 | tf_op jit(solution)/shard_map/all_to_all | solution.py:193
  108.6 3.2 %collective-permute-start.8 = (bf16[27,8,128]{2,1,0:T(8,128)(2,1)S(1)}, bf16[27,8,128]{2,1,0:T(8,128)(2,1)S(1)}, u32[]{:S(2)}, u32[]{:S(2)}) collective-permute-start(bf16[27,8,128]{2,1,0:T(8,128)(2,1)S(1)} %get-tuple-element.23), channel_id=1, source_target_pairs={{0,8},{2,10},{4,12},{6,14},{8,16},{10,18},{12,20},{14,22},{16,24},... | collective-permute-start | bytes 165896 | tf_op jit(solution)/shard_map/ppermute | solution.py:201
  111.9 4.3 %collective-permute-start.9 = (bf16[27,8,128]{2,1,0:T(8,128)(2,1)S(1)}, bf16[27,8,128]{2,1,0:T(8,128)(2,1)S(1)}, u32[]{:S(2)}, u32[]{:S(2)}) collective-permute-start(bf16[27,8,128]{2,1,0:T(8,128)(2,1)S(1)} %get-tuple-element.24), channel_id=1, source_target_pairs={{0,12},{2,14},{4,8},{6,10},{8,20},{10,22},{12,16},{14,18},{16,28},... | collective-permute-start | bytes 165896 | tf_op jit(solution)/shard_map/ppermute | solution.py:202
  116.3 5.6 %collective-permute-done.8 = bf16[27,8,128]{2,1,0:T(8,128)(2,1)S(1)} collective-permute-done((bf16[27,8,128]{2,1,0:T(8,128)(2,1)S(1)}, bf16[27,8,128]{2,1,0:T(8,128)(2,1)S(1)}, u32[]{:S(2)}, u32[]{:S(2)}) %collective-permute-start.8) | collective-permute-done | bytes 55328 | tf_op jit(solution)/shard_map/ppermute | solution.py:201
  121.8 2.6 %collective-permute-done.9 = bf16[27,8,128]{2,1,0:T(8,128)(2,1)S(1)} collective-permute-done((bf16[27,8,128]{2,1,0:T(8,128)(2,1)S(1)}, bf16[27,8,128]{2,1,0:T(8,128)(2,1)S(1)}, u32[]{:S(2)}, u32[]{:S(2)}) %collective-permute-start.9) | collective-permute-done | bytes 55328 | tf_op jit(solution)/shard_map/ppermute | solution.py:202
  124.4 0.1 slice_bitcast_fusion.3
  124.5 0.7 pad_maximum_fusion
  (14 shorter events, 0.2 us)
Async XLA Ops:
  2.2 39.6 %all-to-all-start = ((bf16[16,4,64,128]{3,2,1,0:T(8,128)(2,1)}), bf16[16,4,64,128]{3,2,1,0:T(8,128)(2,1)S(1)}, u32[]{:S(2)}, u32[]{:S(2)}) async-start(bf16[16,4,64,128]{3,2,1,0:T(8,128)(2,1)} %broadcast_in_dim.29), calls=%async_computation | async-start | bytes 2097152 | tf_op jit(solution)/shard_map/all_to_all | solution.py:35
  42.9 27.4 %collective-permute-start = (bf16[32,64,128]{2,1,0:T(8,128)(2,1)}, bf16[32,64,128]{2,1,0:T(8,128)(2,1)}, u32[]{:S(2)}, u32[]{:S(2)}) collective-permute-start(bf16[32,64,128]{2,1,0:T(8,128)(2,1)} %get-tuple-element.16), channel_id=1, source_target_pairs={{0,8},{8,16},{16,24},{24,0},{1,9},{9,17},{17,25},{25,1},{2,10},{10... | collective-permute-start | bytes 1572872 | tf_op jit(solution)/shard_map/ppermute | solution.py:25
  46.0 26.2 %collective-permute-start.2 = (bf16[32,64,128]{2,1,0:T(8,128)(2,1)}, bf16[32,64,128]{2,1,0:T(8,128)(2,1)}, u32[]{:S(2)}, u32[]{:S(2)}) collective-permute-start(bf16[32,64,128]{2,1,0:T(8,128)(2,1)} %get-tuple-element.15), channel_id=1, source_target_pairs={{0,24},{8,0},{16,8},{24,16},{1,25},{9,1},{17,9},{25,17},{2,26},{10... | collective-permute-start | bytes 1572872 | tf_op jit(solution)/shard_map/ppermute | solution.py:25
  50.3 27.9 %all-to-all-start.1 = ((bf16[8,4,64,128]{3,2,1,0:T(8,128)(2,1)}), bf16[8,4,64,128]{3,2,1,0:T(8,128)(2,1)S(1)}, u32[]{:S(2)}, u32[]{:S(2)}) async-start(bf16[8,4,64,128]{3,2,1,0:T(8,128)(2,1)} %broadcast_in_dim.34), calls=%async_computation.1 | async-start | bytes 1048576 | tf_op jit(solution)/shard_map/all_to_all | solution.py:35
  63.8 18.4 %collective-permute-start.4 = (bf16[32,64,128]{2,1,0:T(8,128)(2,1)}, bf16[32,64,128]{2,1,0:T(8,128)(2,1)S(1)}, u32[]{:S(2)}, u32[]{:S(2)}) collective-permute-start(bf16[32,64,128]{2,1,0:T(8,128)(2,1)} %get-tuple-element.15), channel_id=1, source_target_pairs={{0,8},{8,16},{16,24},{24,0},{1,9},{9,17},{17,25},{25,1},{2,10},{10... | collective-permute-start | bytes 1572872 | tf_op jit(solution)/shard_map/ppermute | solution.py:25
  65.7 16.5 %collective-permute-start.5 = (bf16[32,64,128]{2,1,0:T(8,128)(2,1)}, bf16[32,64,128]{2,1,0:T(8,128)(2,1)}, u32[]{:S(2)}, u32[]{:S(2)}) collective-permute-start(bf16[32,64,128]{2,1,0:T(8,128)(2,1)} %get-tuple-element.16), channel_id=1, source_target_pairs={{0,24},{8,0},{16,8},{24,16},{1,25},{9,1},{17,9},{25,17},{2,26},{10... | collective-permute-start | bytes 1572872 | tf_op jit(solution)/shard_map/ppermute | solution.py:25
  70.3 21.9 %collective-permute-start.1 = (bf16[32,64,128]{2,1,0:T(8,128)(2,1)}, bf16[32,64,128]{2,1,0:T(8,128)(2,1)S(1)}, u32[]{:S(2)}, u32[]{:S(2)}) collective-permute-start(bf16[32,64,128]{2,1,0:T(8,128)(2,1)} %collective-permute-done.refs_3_), channel_id=1, source_target_pairs={{0,8},{8,16},{16,24},{24,0},{1,9},{9,17},{17,25},{25,1},{2,10},{10... | collective-permute-start | bytes 1572872 | tf_op jit(solution)/shard_map/ppermute | solution.py:25
  72.2 20.6 %collective-permute-start.3 = (bf16[32,64,128]{2,1,0:T(8,128)(2,1)}, bf16[32,64,128]{2,1,0:T(8,128)(2,1)S(1)}, u32[]{:S(2)}, u32[]{:S(2)}) collective-permute-start(bf16[32,64,128]{2,1,0:T(8,128)(2,1)} %collective-permute-done.2.refs_4_), channel_id=1, source_target_pairs={{0,24},{8,0},{16,8},{24,16},{1,25},{9,1},{17,9},{25,17},{2,26},{10... | collective-permute-start | bytes 1572872 | tf_op jit(solution)/shard_map/ppermute | solution.py:25
  96.7 4.2 %collective-permute-start.6 = (bf16[2,2,27,16,128]{4,3,2,1,0:T(8,128)(2,1)S(1)}, bf16[2,2,27,16,128]{4,3,2,1,0:T(8,128)(2,1)S(1)}, u32[]{:S(2)}, u32[]{:S(2)}) collective-permute-start(bf16[2,2,27,16,128]{4,3,2,1,0:T(8,128)(2,1)S(1)} %slice_bitcast_fusion), channel_id=1, source_target_pairs={{0,1},{1,0},{2,3},{3,2},{4,5},{5,4},{6,7},{7,6},{8,9},{9,8},{10,11... | collective-permute-start | bytes 1327112 | tf_op jit(solution)/shard_map/ppermute | solution.py:29
  101.7 6.8 %collective-permute-start.7 = (bf16[2,27,8,128]{3,2,1,0:T(8,128)(2,1)S(1)}, bf16[2,27,8,128]{3,2,1,0:T(8,128)(2,1)S(1)}, u32[]{:S(2)}, u32[]{:S(2)}) collective-permute-start(bf16[2,27,8,128]{3,2,1,0:T(8,128)(2,1)S(1)} %dynamic-slice_bitcast_fusion), channel_id=1, source_target_pairs={{0,2},{2,0},{4,6},{6,4},{1,3},{3,1},{5,7},{7,5},{8,10},{10,8},{12,... | collective-permute-start | bytes 331784 | tf_op jit(solution)/shard_map/ppermute | solution.py:29
  105.2 11.1 %all-to-all-start.2 = ((bf16[4,27,8,128]{3,2,1,0:T(8,128)(2,1)}), bf16[4,27,8,128]{3,2,1,0:T(8,128)(2,1)S(1)}, u32[]{:S(2)}, u32[]{:S(2)}) async-start(bf16[4,27,8,128]{3,2,1,0:T(8,128)(2,1)} %bitcast.12), calls=%async_computation.2 | async-start | bytes 442368 | tf_op jit(solution)/shard_map/all_to_all | solution.py:193
  108.6 13.2 %collective-permute-start.8 = (bf16[27,8,128]{2,1,0:T(8,128)(2,1)S(1)}, bf16[27,8,128]{2,1,0:T(8,128)(2,1)S(1)}, u32[]{:S(2)}, u32[]{:S(2)}) collective-permute-start(bf16[27,8,128]{2,1,0:T(8,128)(2,1)S(1)} %get-tuple-element.23), channel_id=1, source_target_pairs={{0,8},{2,10},{4,12},{6,14},{8,16},{10,18},{12,20},{14,22},{16,24},... | collective-permute-start | bytes 165896 | tf_op jit(solution)/shard_map/ppermute | solution.py:201
  111.9 12.5 %collective-permute-start.9 = (bf16[27,8,128]{2,1,0:T(8,128)(2,1)S(1)}, bf16[27,8,128]{2,1,0:T(8,128)(2,1)S(1)}, u32[]{:S(2)}, u32[]{:S(2)}) collective-permute-start(bf16[27,8,128]{2,1,0:T(8,128)(2,1)S(1)} %get-tuple-element.24), channel_id=1, source_target_pairs={{0,12},{2,14},{4,8},{6,10},{8,20},{10,22},{12,16},{14,18},{16,28},... | collective-permute-start | bytes 165896 | tf_op jit(solution)/shard_map/ppermute | solution.py:202

commit v9 on v8

--- a/solution.py
+++ b/solution.py
@@ -8,6 +8,7 @@
 from jax.sharding import Mesh, PartitionSpec as P
 
 KC = 27
+KP = 28
 CR = 2
 T = 64
 NY = 4
@@ -78,7 +79,7 @@
     b_ref = refs[2 + n_chunks]
     before = refs[3 + n_chunks:3 + n_chunks + n_before]
     out_ref, panel, acc, sems = refs[-4:]
-    core = info_ref[6]
+    core, yl = info_ref[6], info_ref[7]
     copies, at = [], 0
     for n, chunk in enumerate(chunks):
         size = chunk.shape[0]
@@ -116,14 +117,19 @@
                 d = jnp.right_shift(code, 18)
                 acc[d] = acc[d] + term
 
-    @pl.loop(0, KC)
-    def _(k):
-        for o in range(8):
-            tile = jnp.concatenate([acc[k, o * 8:(o + 1) * 8], acc[KC + k, o * 8:(o + 1) * 8]], axis=0)
-            place = (jnp.bitwise_xor(core, o % 2), o // 4, o // 2 % 2, k)
-            for earlier in before:
-                tile = tile + earlier[place].astype(F32)
-            out_ref[place] = tile.astype(BF16)
+    @pl.loop(0, KP // 2)
+    def _(m):
+        for p in range(2):
+            first_of = p * KC + 2 * m
+            for o in range(8):
+                rows = slice(o * 8, (o + 1) * 8)
+                tile = jnp.concatenate([acc[first_of, rows], acc[first_of + 1, rows]], axis=0)
+                far = jnp.bitwise_xor(yl, o // 2)
+                seat = o // 2 if p == 0 else 2 * jnp.bitwise_and(far, 1) + jnp.right_shift(far, 1)
+                place = (jnp.bitwise_xor(core, o % 2), p, seat, m)
+                for earlier in before:
+                    tile = tile + earlier[place].astype(F32)
+                out_ref[place] = tile.astype(BF16)
 
 
 def panel_sums(group, code, info, chunks, b, before=()):
@@ -135,7 +141,7 @@
         functools.partial(sum_kernel, group, len(chunks), len(before)),
         in_specs=[smem, smem] + [anyw] * len(chunks) + [vmem] * (1 + len(before)),
         out_specs=vmem,
-        out_shape=jax.ShapeDtypeStruct((2, 2, 2, KC, 16, 2 * T), BF16),
+        out_shape=jax.ShapeDtypeStruct((2, 2, NY, KP // 2, 16, 2 * T), BF16),
         scratch_shapes=[
             pltpu.VMEM((pairs, T, 2 * T), BF16),
             pltpu.VMEM((2 * KC + 1, T, 2 * T), F32),
@@ -188,20 +194,15 @@
     sums1 = panel_sums(1, code, info, [left_b, right_a], b)
     sums2 = panel_sums(2, code, info, [left2, right2], b, (sums0, sums1))
 
-    chip = sums2[0].astype(F32) + swapped(sums2[1], "core", 1).astype(F32)
-    staying = chip[..., :8, :].astype(BF16).reshape(NY, KC, 8, 2 * T)
+    swap_in = swapped(sums2[1], "core", 1)
+    staying, coming = [(sums2[0, p].astype(F32) + swap_in[p].astype(F32)).astype(BF16) for p in range(2)]
     staying = lax.all_to_all(staying, "yl", 0, 0, tiled=True)
-    coming = chip[..., 8:, :].astype(BF16)
-    bit0, bit1 = yl % 2, yl // 2
-    pick = functools.partial(lax.dynamic_index_in_dim, keepdims=False)
-    two = pick(coming, bit0, 1).astype(F32) + swapped(pick(coming, 1 - bit0, 1), "yl", 1).astype(F32)
+    two = coming[:2].astype(F32) + swapped(coming[2:], "yl", 1).astype(F32)
     count = lax.axis_size(ROW)
     ahead = [[(r * NY + y, (r + 1) % count * NY + (y ^ by)) for r in range(count) for y in range(NY)] for by in (0, 2)]
-    last = [
-        lax.ppermute(pick(two, bit1, 0).astype(BF16), ROW + ("yl",), ahead[0]),
-        lax.ppermute(pick(two, 1 - bit1, 0).astype(BF16), ROW + ("yl",), ahead[1]),
-    ]
+    last = [lax.ppermute(two[n].astype(BF16), ROW + ("yl",), ahead[n]) for n in range(2)]
     result = jnp.sum(staying.astype(F32), axis=0) + sum(part.astype(F32) for part in last)
+    result = result.reshape(KP, 8, 2 * T)[:KC]
     return jnp.stack([result[..., :T], result[..., T:]])
 
 

time: 127 us -> 127 us (level)
  no operation moved by 1% of the time
where the time goes in v9:
time: 127 us; the launch traced here: 125 us
  starting transfers between devices  67 us (53%)
  waiting for transfers between devices  31.4 us (25%)
  Pallas kernels  17.3 us (14%)
  local copies, waits for them, and re-layouts  4.86 us (4%)
  other arithmetic  4.41 us (3%)
    all_to_all x2, starting transfers between devices, spread(): return lax.all_to_all(copies, axis, 0, 0, tiled=True)  29.7 us
    all_to_all x2, waiting for transfers between devices, spread(): return lax.all_to_all(copies, axis, 0, 0, tiled=True)  21.3 us
    ppermute x6, starting transfers between devices, shifted(): lax.ppermute(value, axis, [(i, (i + by) % count) for i in range(count)])  19.5 us
    pallas_call x3, Pallas kernels, panel_sums(): pl.pallas_call(functools.partial(sum_kernel, group, len(chunks), len(befo...  13.3 us
    ppermute x2, waiting for transfers between devices, body(): lax.ppermute(two[n].astype(BF16), ROW + ('yl',), ahead[n])  8.15 us
    ppermute x2, starting transfers between devices, body(): lax.ppermute(two[n].astype(BF16), ROW + ('yl',), ahead[n])  7.72 us
    ppermute x2, starting transfers between devices, swapped(): lax.ppermute(value, axis, [(i, i ^ by) for i in range(lax.axis_size(axis))])  6.31 us
    pallas_call x1, Pallas kernels, left_products(): pl.pallas_call(left_kernel, in_specs=[vmem, pl.BlockSpec(memory_space=plt...  3.94 us
  transfers between devices with their start and end apart: 13, of which 6 were waited for; matrix products, arithmetic and copies ran while one was open for 4% of the time, Pallas kernels for 11%

profile of v9, /device:TPU:1, one launch (start us, length us, event | category | flops | bytes accessed | tf_op | source)
XLA Modules:
  0.0 125.4 jit_solution(110651233464517930)
XLA Ops:
  0.0 0.9 slice_bitcast_fusion.8
  0.9 0.1 pad_maximum_fusion.1
  1.0 1.2 broadcast_in_dim.29
  2.2 16.2 %all-to-all-start = ((bf16[16,4,64,128]{3,2,1,0:T(8,128)(2,1)}), bf16[16,4,64,128]{3,2,1,0:T(8,128)(2,1)S(1)}, u32[]{:S(2)}, u32[]{:S(2)}) async-start(bf16[16,4,64,128]{3,2,1,0:T(8,128)(2,1)} %broadcast_in_dim.29), calls=%async_computation | async-start | bytes 2097152 | tf_op jit(solution)/shard_map/all_to_all | solution.py:36
  18.4 0.7 fusion.32
  19.1 0.7 fusion.16
  19.9 0.1 copy.9
  19.9 0.1 eq.59
  20.1 0.7 iota_compare_fusion.3
  20.8 0.1 lt.51
  21.0 0.1 copy.10
  21.1 0.1 sub.87
  21.2 0.1 convert_reduce_fusion.1
  21.3 0.2 reduce-window.7
  21.5 0.1 pad_add_fusion.refs_1_
  21.6 0.2 fusion.3
  21.8 0.2 select_reduce_fusion
  22.0 19.8 %all-to-all-done = bf16[16,4,64,128]{3,2,1,0:T(8,128)(2,1)S(1)} async-done(((bf16[16,4,64,128]{3,2,1,0:T(8,128)(2,1)}), bf16[16,4,64,128]{3,2,1,0:T(8,128)(2,1)S(1)}, u32[]{:S(2)}, u32[]{:S(2)}) %all-to-all-start) | async-done | bytes 1048608 | tf_op jit(solution)/shard_map/all_to_all | solution.py:36
  41.8 1.1 fusion.33
  42.9 3.1 %collective-permute-start = (bf16[32,64,128]{2,1,0:T(8,128)(2,1)}, bf16[32,64,128]{2,1,0:T(8,128)(2,1)}, u32[]{:S(2)}, u32[]{:S(2)}) collective-permute-start(bf16[32,64,128]{2,1,0:T(8,128)(2,1)} %get-tuple-element.18), channel_id=1, source_target_pairs={{0,8},{8,16},{16,24},{24,0},{1,9},{9,17},{17,25},{25,1},{2,10},{10... | collective-permute-start | bytes 1572872 | tf_op jit(solution)/shard_map/ppermute | solution.py:26
  46.0 3.4 %collective-permute-start.2 = (bf16[32,64,128]{2,1,0:T(8,128)(2,1)}, bf16[32,64,128]{2,1,0:T(8,128)(2,1)}, u32[]{:S(2)}, u32[]{:S(2)}) collective-permute-start(bf16[32,64,128]{2,1,0:T(8,128)(2,1)} %get-tuple-element.17), channel_id=1, source_target_pairs={{0,24},{8,0},{16,8},{24,16},{1,25},{9,1},{17,9},{25,17},{2,26},{10... | collective-permute-start | bytes 1572872 | tf_op jit(solution)/shard_map/ppermute | solution.py:26
  49.4 0.9 broadcast_in_dim.34
  50.3 13.4 %all-to-all-start.1 = ((bf16[8,4,64,128]{3,2,1,0:T(8,128)(2,1)}), bf16[8,4,64,128]{3,2,1,0:T(8,128)(2,1)S(1)}, u32[]{:S(2)}, u32[]{:S(2)}) async-start(bf16[8,4,64,128]{3,2,1,0:T(8,128)(2,1)} %broadcast_in_dim.34), calls=%async_computation.1 | async-start | bytes 1048576 | tf_op jit(solution)/shard_map/all_to_all | solution.py:36
  63.8 1.9 %collective-permute-start.4 = (bf16[32,64,128]{2,1,0:T(8,128)(2,1)}, bf16[32,64,128]{2,1,0:T(8,128)(2,1)S(1)}, u32[]{:S(2)}, u32[]{:S(2)}) collective-permute-start(bf16[32,64,128]{2,1,0:T(8,128)(2,1)} %get-tuple-element.17), channel_id=1, source_target_pairs={{0,8},{8,16},{16,24},{24,0},{1,9},{9,17},{17,25},{25,1},{2,10},{10... | collective-permute-start | bytes 1572872 | tf_op jit(solution)/shard_map/ppermute | solution.py:26
  65.7 4.6 %collective-permute-start.5 = (bf16[32,64,128]{2,1,0:T(8,128)(2,1)}, bf16[32,64,128]{2,1,0:T(8,128)(2,1)}, u32[]{:S(2)}, u32[]{:S(2)}) collective-permute-start(bf16[32,64,128]{2,1,0:T(8,128)(2,1)} %get-tuple-element.18), channel_id=1, source_target_pairs={{0,24},{8,0},{16,8},{24,16},{1,25},{9,1},{17,9},{25,17},{2,26},{10... | collective-permute-start | bytes 1572872 | tf_op jit(solution)/shard_map/ppermute | solution.py:26
  70.3 0.0 collective-permute-done.refs_3_
  70.3 1.9 %collective-permute-start.1 = (bf16[32,64,128]{2,1,0:T(8,128)(2,1)}, bf16[32,64,128]{2,1,0:T(8,128)(2,1)S(1)}, u32[]{:S(2)}, u32[]{:S(2)}) collective-permute-start(bf16[32,64,128]{2,1,0:T(8,128)(2,1)} %collective-permute-done.refs_3_), channel_id=1, source_target_pairs={{0,8},{8,16},{16,24},{24,0},{1,9},{9,17},{17,25},{25,1},{2,10},{10... | collective-permute-start | bytes 1572872 | tf_op jit(solution)/shard_map/ppermute | solution.py:26
  72.2 0.0 collective-permute-done.2.refs_4_
  72.2 4.6 %collective-permute-start.3 = (bf16[32,64,128]{2,1,0:T(8,128)(2,1)}, bf16[32,64,128]{2,1,0:T(8,128)(2,1)S(1)}, u32[]{:S(2)}, u32[]{:S(2)}) collective-permute-start(bf16[32,64,128]{2,1,0:T(8,128)(2,1)} %collective-permute-done.2.refs_4_), channel_id=1, source_target_pairs={{0,24},{8,0},{16,8},{24,16},{1,25},{9,1},{17,9},{25,17},{2,26},{10... | collective-permute-start | bytes 1572872 | tf_op jit(solution)/shard_map/ppermute | solution.py:26
  76.8 1.5 %all-to-all-done.1.own_ref = bf16[8,4,64,128]{3,2,1,0:T(8,128)(2,1)S(1)} async-done(((bf16[8,4,64,128]{3,2,1,0:T(8,128)(2,1)}), bf16[8,4,64,128]{3,2,1,0:T(8,128)(2,1)S(1)}, u32[]{:S(2)}, u32[]{:S(2)}) %all-to-all-start.1) | async-done | bytes 524320 | tf_op jit(solution)/shard_map/all_to_all | solution.py:36
  78.3 3.9 %left_products.1 = bf16[2,4,8,6,64,64]{5,4,3,2,1,0:T(8,128)(2,1)S(1)} custom-call(bf16[8,4,64,128]{3,2,1,0:T(8,128)(2,1)S(1)} %all-to-all-done.1.own_ref, bf16[2,4,8,6,64,64]{5,4,3,2,1,0:T(8,128)(2,1)} %bitcast.58), custom_call_target="tpu_custom_call" | custom-call | flops 201326592 | bytes 16777216 | tf_op jit(solution)/shard_map/left_products/pallas_call | solution.py:63
  82.2 0.0 collective-permute-done.4.refs_2_
  82.2 0.0 collective-permute-done.5.refs_3_
  82.2 3.8 %panel_sums_1.1.refs_6_ = bf16[2,2,4,14,16,128]{5,4,3,2,1,0:T(8,128)(2,1)S(1)} custom-call(s32[408]{0:T(512)S(1)} %broadcast_add_fusion.refs_0_, s32[8]{0:T(128)S(1)} %pad_add_fusion.refs_1_, bf16[32,64,128]{2,1,0:T(8,128)(2,1)S(1)} %collective-permute-done.4.refs_2_, bf16[32,64,128]{2,1,0:T(8,128)(2,1)} %collective-permute-done.5.refs_3_, ...), custom_call_target="tpu_custom_call" | custom-call | flops 67108864 | bytes 8388608 | tf_op jit(solution)/shard_map/panel_sums_1/pallas_call | solution.py:140
  86.0 6.3 %panel_sums_0.1.refs_5_ = bf16[2,2,4,14,16,128]{5,4,3,2,1,0:T(8,128)(2,1)S(1)} custom-call(s32[408]{0:T(512)S(1)} %broadcast_add_fusion.refs_0_, s32[8]{0:T(128)S(1)} %pad_add_fusion.refs_1_, bf16[64,64,128]{2,1,0:T(8,128)(2,1)S(1)} %bitcast.57, bf16[32,64,128]{2,1,0:T(8,128)(2,1)} %collective-permute-done.refs_3_, ...), custom_call_target="tpu_custom_call" | custom-call | flops 134217728 | bytes 8388608 | tf_op jit(solution)/shard_map/panel_sums_0/pallas_call | solution.py:140
  92.3 0.5 collective-permute-done.3.refs_3_
  92.8 3.2 %panel_sums_2.1 = bf16[2,2,4,14,16,128]{5,4,3,2,1,0:T(8,128)(2,1)S(1)} custom-call(s32[408]{0:T(512)S(1)} %broadcast_add_fusion.refs_0_, s32[8]{0:T(128)S(1)} %pad_add_fusion.refs_1_, bf16[32,64,128]{2,1,0:T(8,128)(2,1)S(1)} %collective-permute-done.1.refs_2_, bf16[32,64,128]{2,1,0:T(8,128)(2,1)S(1)} %collective-permute-done.3.refs_3_, ...), custom_call_target="tpu_custom_call" | custom-call | flops 67108864 | bytes 8388608 | tf_op jit(solution)/shard_map/panel_sums_2/pallas_call | solution.py:140
  96.1 2.8 %collective-permute-start.6 = (bf16[2,4,14,16,128]{4,3,2,1,0:T(8,128)(2,1)S(1)}, bf16[2,4,14,16,128]{4,3,2,1,0:T(8,128)(2,1)S(1)}, u32[]{:S(2)}, u32[]{:S(2)}) collective-permute-start(bf16[2,4,14,16,128]{4,3,2,1,0:T(8,128)(2,1)S(1)} %slice_bitcast_fusion), channel_id=1, source_target_pairs={{0,1},{1,0},{2,3},{3,2},{4,5},{5,4},{6,7},{7,6},{8,9},{9,8},{10,11... | collective-permute-start | bytes 1376264 | tf_op jit(solution)/shard_map/ppermute | solution.py:30
  98.9 1.4 %collective-permute-done.6 = bf16[2,4,14,16,128]{4,3,2,1,0:T(8,128)(2,1)S(1)} collective-permute-done((bf16[2,4,14,16,128]{4,3,2,1,0:T(8,128)(2,1)S(1)}, bf16[2,4,14,16,128]{4,3,2,1,0:T(8,128)(2,1)S(1)}, u32[]{:S(2)}, u32[]{:S(2)}) %collective-permute-start.6) | collective-permute-done | bytes 458784 | tf_op jit(solution)/shard_map/ppermute | solution.py:30
  100.3 0.8 fusion.4
  101.1 3.6 %collective-permute-start.7 = (bf16[2,14,16,128]{3,2,1,0:T(8,128)(2,1)S(1)}, bf16[2,14,16,128]{3,2,1,0:T(8,128)(2,1)S(1)}, u32[]{:S(2)}, u32[]{:S(2)}) collective-permute-start(bf16[2,14,16,128]{3,2,1,0:T(8,128)(2,1)S(1)} %slice.71), channel_id=1, source_target_pairs={{0,2},{2,0},{4,6},{6,4},{1,3},{3,1},{5,7},{7,5},{8,10},{10,8},{12,... | collective-permute-start | bytes 344072 | tf_op jit(solution)/shard_map/ppermute | solution.py:30
  104.7 3.9 %all-to-all-start.2 = ((bf16[4,14,16,128]{3,2,1,0:T(8,128)(2,1)}), bf16[4,14,16,128]{3,2,1,0:T(8,128)(2,1)S(1)}, u32[]{:S(2)}, u32[]{:S(2)}) async-start(bf16[4,14,16,128]{3,2,1,0:T(8,128)(2,1)} %get-tuple-element.16), calls=%async_computation.2 | async-start | bytes 458752 | tf_op jit(solution)/shard_map/all_to_all | solution.py:199
  108.6 2.9 %collective-permute-start.8 = (bf16[14,16,128]{2,1,0:T(8,128)(2,1)S(1)}, bf16[14,16,128]{2,1,0:T(8,128)(2,1)S(1)}, u32[]{:S(2)}, u32[]{:S(2)}) collective-permute-start(bf16[14,16,128]{2,1,0:T(8,128)(2,1)S(1)} %get-tuple-element.23), channel_id=1, source_target_pairs={{0,8},{2,10},{4,12},{6,14},{8,16},{10,18},{12,20},{14,22},{16,24},... | collective-permute-start | bytes 172040 | tf_op jit(solution)/shard_map/ppermute | solution.py:203
  111.5 4.9 %collective-permute-start.9 = (bf16[14,16,128]{2,1,0:T(8,128)(2,1)S(1)}, bf16[14,16,128]{2,1,0:T(8,128)(2,1)S(1)}, u32[]{:S(2)}, u32[]{:S(2)}) collective-permute-start(bf16[14,16,128]{2,1,0:T(8,128)(2,1)S(1)} %get-tuple-element.24), channel_id=1, source_target_pairs={{0,12},{2,14},{4,8},{6,10},{8,20},{10,22},{12,16},{14,18},{16,28},... | collective-permute-start | bytes 172040 | tf_op jit(solution)/shard_map/ppermute | solution.py:203
  116.4 5.4 %collective-permute-done.8 = bf16[14,16,128]{2,1,0:T(8,128)(2,1)S(1)} collective-permute-done((bf16[14,16,128]{2,1,0:T(8,128)(2,1)S(1)}, bf16[14,16,128]{2,1,0:T(8,128)(2,1)S(1)}, u32[]{:S(2)}, u32[]{:S(2)}) %collective-permute-start.8) | collective-permute-done | bytes 57376 | tf_op jit(solution)/shard_map/ppermute | solution.py:203
  121.8 2.7 %collective-permute-done.9 = bf16[14,16,128]{2,1,0:T(8,128)(2,1)S(1)} collective-permute-done((bf16[14,16,128]{2,1,0:T(8,128)(2,1)S(1)}, bf16[14,16,128]{2,1,0:T(8,128)(2,1)S(1)}, u32[]{:S(2)}, u32[]{:S(2)}) %collective-permute-start.9) | collective-permute-done | bytes 57376 | tf_op jit(solution)/shard_map/ppermute | solution.py:203
  124.6 0.1 slice_bitcast_fusion.6
  124.7 0.7 pad_maximum_fusion
  (13 shorter events, 0.2 us)
Async XLA Ops:
  2.2 39.6 %all-to-all-start = ((bf16[16,4,64,128]{3,2,1,0:T(8,128)(2,1)}), bf16[16,4,64,128]{3,2,1,0:T(8,128)(2,1)S(1)}, u32[]{:S(2)}, u32[]{:S(2)}) async-start(bf16[16,4,64,128]{3,2,1,0:T(8,128)(2,1)} %broadcast_in_dim.29), calls=%async_computation | async-start | bytes 2097152 | tf_op jit(solution)/shard_map/all_to_all | solution.py:36
  42.9 27.4 %collective-permute-start = (bf16[32,64,128]{2,1,0:T(8,128)(2,1)}, bf16[32,64,128]{2,1,0:T(8,128)(2,1)}, u32[]{:S(2)}, u32[]{:S(2)}) collective-permute-start(bf16[32,64,128]{2,1,0:T(8,128)(2,1)} %get-tuple-element.18), channel_id=1, source_target_pairs={{0,8},{8,16},{16,24},{24,0},{1,9},{9,17},{17,25},{25,1},{2,10},{10... | collective-permute-start | bytes 1572872 | tf_op jit(solution)/shard_map/ppermute | solution.py:26
  46.0 26.2 %collective-permute-start.2 = (bf16[32,64,128]{2,1,0:T(8,128)(2,1)}, bf16[32,64,128]{2,1,0:T(8,128)(2,1)}, u32[]{:S(2)}, u32[]{:S(2)}) collective-permute-start(bf16[32,64,128]{2,1,0:T(8,128)(2,1)} %get-tuple-element.17), channel_id=1, source_target_pairs={{0,24},{8,0},{16,8},{24,16},{1,25},{9,1},{17,9},{25,17},{2,26},{10... | collective-permute-start | bytes 1572872 | tf_op jit(solution)/shard_map/ppermute | solution.py:26
  50.3 27.9 %all-to-all-start.1 = ((bf16[8,4,64,128]{3,2,1,0:T(8,128)(2,1)}), bf16[8,4,64,128]{3,2,1,0:T(8,128)(2,1)S(1)}, u32[]{:S(2)}, u32[]{:S(2)}) async-start(bf16[8,4,64,128]{3,2,1,0:T(8,128)(2,1)} %broadcast_in_dim.34), calls=%async_computation.1 | async-start | bytes 1048576 | tf_op jit(solution)/shard_map/all_to_all | solution.py:36
  63.8 18.4 %collective-permute-start.4 = (bf16[32,64,128]{2,1,0:T(8,128)(2,1)}, bf16[32,64,128]{2,1,0:T(8,128)(2,1)S(1)}, u32[]{:S(2)}, u32[]{:S(2)}) collective-permute-start(bf16[32,64,128]{2,1,0:T(8,128)(2,1)} %get-tuple-element.17), channel_id=1, source_target_pairs={{0,8},{8,16},{16,24},{24,0},{1,9},{9,17},{17,25},{25,1},{2,10},{10... | collective-permute-start | bytes 1572872 | tf_op jit(solution)/shard_map/ppermute | solution.py:26
  65.7 16.5 %collective-permute-start.5 = (bf16[32,64,128]{2,1,0:T(8,128)(2,1)}, bf16[32,64,128]{2,1,0:T(8,128)(2,1)}, u32[]{:S(2)}, u32[]{:S(2)}) collective-permute-start(bf16[32,64,128]{2,1,0:T(8,128)(2,1)} %get-tuple-element.18), channel_id=1, source_target_pairs={{0,24},{8,0},{16,8},{24,16},{1,25},{9,1},{17,9},{25,17},{2,26},{10... | collective-permute-start | bytes 1572872 | tf_op jit(solution)/shard_map/ppermute | solution.py:26
  70.3 22.1 %collective-permute-start.1 = (bf16[32,64,128]{2,1,0:T(8,128)(2,1)}, bf16[32,64,128]{2,1,0:T(8,128)(2,1)S(1)}, u32[]{:S(2)}, u32[]{:S(2)}) collective-permute-start(bf16[32,64,128]{2,1,0:T(8,128)(2,1)} %collective-permute-done.refs_3_), channel_id=1, source_target_pairs={{0,8},{8,16},{16,24},{24,0},{1,9},{9,17},{17,25},{25,1},{2,10},{10... | collective-permute-start | bytes 1572872 | tf_op jit(solution)/shard_map/ppermute | solution.py:26
  72.2 20.6 %collective-permute-start.3 = (bf16[32,64,128]{2,1,0:T(8,128)(2,1)}, bf16[32,64,128]{2,1,0:T(8,128)(2,1)S(1)}, u32[]{:S(2)}, u32[]{:S(2)}) collective-permute-start(bf16[32,64,128]{2,1,0:T(8,128)(2,1)} %collective-permute-done.2.refs_4_), channel_id=1, source_target_pairs={{0,24},{8,0},{16,8},{24,16},{1,25},{9,1},{17,9},{25,17},{2,26},{10... | collective-permute-start | bytes 1572872 | tf_op jit(solution)/shard_map/ppermute | solution.py:26
  96.1 4.2 %collective-permute-start.6 = (bf16[2,4,14,16,128]{4,3,2,1,0:T(8,128)(2,1)S(1)}, bf16[2,4,14,16,128]{4,3,2,1,0:T(8,128)(2,1)S(1)}, u32[]{:S(2)}, u32[]{:S(2)}) collective-permute-start(bf16[2,4,14,16,128]{4,3,2,1,0:T(8,128)(2,1)S(1)} %slice_bitcast_fusion), channel_id=1, source_target_pairs={{0,1},{1,0},{2,3},{3,2},{4,5},{5,4},{6,7},{7,6},{8,9},{9,8},{10,11... | collective-permute-start | bytes 1376264 | tf_op jit(solution)/shard_map/ppermute | solution.py:30
  101.1 7.4 %collective-permute-start.7 = (bf16[2,14,16,128]{3,2,1,0:T(8,128)(2,1)S(1)}, bf16[2,14,16,128]{3,2,1,0:T(8,128)(2,1)S(1)}, u32[]{:S(2)}, u32[]{:S(2)}) collective-permute-start(bf16[2,14,16,128]{3,2,1,0:T(8,128)(2,1)S(1)} %slice.71), channel_id=1, source_target_pairs={{0,2},{2,0},{4,6},{6,4},{1,3},{3,1},{5,7},{7,5},{8,10},{10,8},{12,... | collective-permute-start | bytes 344072 | tf_op jit(solution)/shard_map/ppermute | solution.py:30
  104.7 11.7 %all-to-all-start.2 = ((bf16[4,14,16,128]{3,2,1,0:T(8,128)(2,1)}), bf16[4,14,16,128]{3,2,1,0:T(8,128)(2,1)S(1)}, u32[]{:S(2)}, u32[]{:S(2)}) async-start(bf16[4,14,16,128]{3,2,1,0:T(8,128)(2,1)} %get-tuple-element.16), calls=%async_computation.2 | async-start | bytes 458752 | tf_op jit(solution)/shard_map/all_to_all | solution.py:199
  108.6 13.2 %collective-permute-start.8 = (bf16[14,16,128]{2,1,0:T(8,128)(2,1)S(1)}, bf16[14,16,128]{2,1,0:T(8,128)(2,1)S(1)}, u32[]{:S(2)}, u32[]{:S(2)}) collective-permute-start(bf16[14,16,128]{2,1,0:T(8,128)(2,1)S(1)} %get-tuple-element.23), channel_id=1, source_target_pairs={{0,8},{2,10},{4,12},{6,14},{8,16},{10,18},{12,20},{14,22},{16,24},... | collective-permute-start | bytes 172040 | tf_op jit(solution)/shard_map/ppermute | solution.py:203
  111.5 13.1 %collective-permute-start.9 = (bf16[14,16,128]{2,1,0:T(8,128)(2,1)S(1)}, bf16[14,16,128]{2,1,0:T(8,128)(2,1)S(1)}, u32[]{:S(2)}, u32[]{:S(2)}) collective-permute-start(bf16[14,16,128]{2,1,0:T(8,128)(2,1)S(1)} %get-tuple-element.24), channel_id=1, source_target_pairs={{0,12},{2,14},{4,8},{6,10},{8,20},{10,22},{12,16},{14,18},{16,28},... | collective-permute-start | bytes 172040 | tf_op jit(solution)/shard_map/ppermute | solution.py:203

commit v10 on v8

--- a/solution.py
+++ b/solution.py
@@ -198,8 +198,8 @@
     count = lax.axis_size(ROW)
     ahead = [[(r * NY + y, (r + 1) % count * NY + (y ^ by)) for r in range(count) for y in range(NY)] for by in (0, 2)]
     last = [
+        lax.ppermute(pick(two, 1 - bit1, 0).astype(BF16), ROW + ("yl",), ahead[1]),
         lax.ppermute(pick(two, bit1, 0).astype(BF16), ROW + ("yl",), ahead[0]),
-        lax.ppermute(pick(two, 1 - bit1, 0).astype(BF16), ROW + ("yl",), ahead[1]),
     ]
     result = jnp.sum(staying.astype(F32), axis=0) + sum(part.astype(F32) for part in last)
     return jnp.stack([result[..., :T], result[..., T:]])

time: 127 us -> 130 us (1.024)
  waiting for transfers between devices: 31.4 us -> 34.5 us
    ppermute x1, waiting for transfers between devices: 5.55 us -> 7.7 us  [body(): lax.ppermute(pick(two, bit1, 0).astype(BF16), ROW + ('yl',), ahead[0])]
where the time goes in v10:
time: 130 us; the launch traced here: 129 us
  starting transfers between devices  67 us (52%)
  waiting for transfers between devices  34.5 us (27%)
  Pallas kernels  17.2 us (13%)
  local copies, waits for them, and re-layouts  5.62 us (4%)
  other arithmetic  3.71 us (3%)
    all_to_all x2, starting transfers between devices, spread(): return lax.all_to_all(copies, axis, 0, 0, tiled=True)  29.7 us
    all_to_all x2, waiting for transfers between devices, spread(): return lax.all_to_all(copies, axis, 0, 0, tiled=True)  21.3 us
    ppermute x6, starting transfers between devices, shifted(): lax.ppermute(value, axis, [(i, (i + by) % count) for i in range(count)])  19.5 us
    pallas_call x3, Pallas kernels, panel_sums(): pl.pallas_call(functools.partial(sum_kernel, group, len(chunks), len(befo...  13.3 us
    ppermute x1, waiting for transfers between devices, body(): lax.ppermute(pick(two, bit1, 0).astype(BF16), ROW + ('yl',), ahead[0])  7.7 us
    ppermute x2, starting transfers between devices, swapped(): lax.ppermute(value, axis, [(i, i ^ by) for i in range(lax.axis_size(axis))])  6.55 us
    ppermute x1, starting transfers between devices, body(): lax.ppermute(pick(two, 1 - bit1, 0).astype(BF16), ROW + ('yl',), ahead[1])  5.09 us
    pallas_call x1, Pallas kernels, left_products(): pl.pallas_call(left_kernel, in_specs=[vmem, pl.BlockSpec(memory_space=plt...  3.94 us
  transfers between devices with their start and end apart: 13, of which 6 were waited for; matrix products, arithmetic and copies ran while one was open for 4% of the time, Pallas kernels for 11%

profile of v10, /device:TPU:1, one launch (start us, length us, event | category | flops | bytes accessed | tf_op | source)
XLA Modules:
  0.0 128.5 jit_solution(17470888804366763829)
XLA Ops:
  0.0 0.9 slice_bitcast_fusion.5
  0.9 0.1 pad_maximum_fusion.1
  1.0 1.2 broadcast_in_dim.29
  2.2 16.2 %all-to-all-start = ((bf16[16,4,64,128]{3,2,1,0:T(8,128)(2,1)}), bf16[16,4,64,128]{3,2,1,0:T(8,128)(2,1)S(1)}, u32[]{:S(2)}, u32[]{:S(2)}) async-start(bf16[16,4,64,128]{3,2,1,0:T(8,128)(2,1)} %broadcast_in_dim.29), calls=%async_computation | async-start | bytes 2097152 | tf_op jit(solution)/shard_map/all_to_all | solution.py:35
  18.4 0.7 fusion.33
  19.1 0.7 fusion.17
  19.9 0.1 copy.9
  19.9 0.1 eq.61
  20.1 0.7 iota_compare_fusion.3
  20.8 0.1 lt.71
  21.0 0.1 copy.10
  21.1 0.1 sub.97
  21.2 0.1 convert_reduce_fusion.1
  21.3 0.2 reduce-window.7
  21.5 0.1 pad_add_fusion.refs_1_
  21.6 0.2 fusion.3
  21.8 0.2 select_reduce_fusion
  22.0 19.8 %all-to-all-done = bf16[16,4,64,128]{3,2,1,0:T(8,128)(2,1)S(1)} async-done(((bf16[16,4,64,128]{3,2,1,0:T(8,128)(2,1)}), bf16[16,4,64,128]{3,2,1,0:T(8,128)(2,1)S(1)}, u32[]{:S(2)}, u32[]{:S(2)}) %all-to-all-start) | async-done | bytes 1048608 | tf_op jit(solution)/shard_map/all_to_all | solution.py:35
  41.8 1.1 fusion.34
  42.9 3.1 %collective-permute-start = (bf16[32,64,128]{2,1,0:T(8,128)(2,1)}, bf16[32,64,128]{2,1,0:T(8,128)(2,1)}, u32[]{:S(2)}, u32[]{:S(2)}) collective-permute-start(bf16[32,64,128]{2,1,0:T(8,128)(2,1)} %get-tuple-element.16), channel_id=1, source_target_pairs={{0,8},{8,16},{16,24},{24,0},{1,9},{9,17},{17,25},{25,1},{2,10},{10... | collective-permute-start | bytes 1572872 | tf_op jit(solution)/shard_map/ppermute | solution.py:25
  46.0 3.4 %collective-permute-start.2 = (bf16[32,64,128]{2,1,0:T(8,128)(2,1)}, bf16[32,64,128]{2,1,0:T(8,128)(2,1)}, u32[]{:S(2)}, u32[]{:S(2)}) collective-permute-start(bf16[32,64,128]{2,1,0:T(8,128)(2,1)} %get-tuple-element.15), channel_id=1, source_target_pairs={{0,24},{8,0},{16,8},{24,16},{1,25},{9,1},{17,9},{25,17},{2,26},{10... | collective-permute-start | bytes 1572872 | tf_op jit(solution)/shard_map/ppermute | solution.py:25
  49.4 0.9 broadcast_in_dim.34
  50.3 13.4 %all-to-all-start.1 = ((bf16[8,4,64,128]{3,2,1,0:T(8,128)(2,1)}), bf16[8,4,64,128]{3,2,1,0:T(8,128)(2,1)S(1)}, u32[]{:S(2)}, u32[]{:S(2)}) async-start(bf16[8,4,64,128]{3,2,1,0:T(8,128)(2,1)} %broadcast_in_dim.34), calls=%async_computation.1 | async-start | bytes 1048576 | tf_op jit(solution)/shard_map/all_to_all | solution.py:35
  63.8 1.9 %collective-permute-start.4 = (bf16[32,64,128]{2,1,0:T(8,128)(2,1)}, bf16[32,64,128]{2,1,0:T(8,128)(2,1)S(1)}, u32[]{:S(2)}, u32[]{:S(2)}) collective-permute-start(bf16[32,64,128]{2,1,0:T(8,128)(2,1)} %get-tuple-element.15), channel_id=1, source_target_pairs={{0,8},{8,16},{16,24},{24,0},{1,9},{9,17},{17,25},{25,1},{2,10},{10... | collective-permute-start | bytes 1572872 | tf_op jit(solution)/shard_map/ppermute | solution.py:25
  65.7 4.6 %collective-permute-start.5 = (bf16[32,64,128]{2,1,0:T(8,128)(2,1)}, bf16[32,64,128]{2,1,0:T(8,128)(2,1)}, u32[]{:S(2)}, u32[]{:S(2)}) collective-permute-start(bf16[32,64,128]{2,1,0:T(8,128)(2,1)} %get-tuple-element.16), channel_id=1, source_target_pairs={{0,24},{8,0},{16,8},{24,16},{1,25},{9,1},{17,9},{25,17},{2,26},{10... | collective-permute-start | bytes 1572872 | tf_op jit(solution)/shard_map/ppermute | solution.py:25
  70.3 0.0 collective-permute-done.refs_3_
  70.3 1.9 %collective-permute-start.1 = (bf16[32,64,128]{2,1,0:T(8,128)(2,1)}, bf16[32,64,128]{2,1,0:T(8,128)(2,1)S(1)}, u32[]{:S(2)}, u32[]{:S(2)}) collective-permute-start(bf16[32,64,128]{2,1,0:T(8,128)(2,1)} %collective-permute-done.refs_3_), channel_id=1, source_target_pairs={{0,8},{8,16},{16,24},{24,0},{1,9},{9,17},{17,25},{25,1},{2,10},{10... | collective-permute-start | bytes 1572872 | tf_op jit(solution)/shard_map/ppermute | solution.py:25
  72.2 0.0 collective-permute-done.2.refs_4_
  72.2 4.6 %collective-permute-start.3 = (bf16[32,64,128]{2,1,0:T(8,128)(2,1)}, bf16[32,64,128]{2,1,0:T(8,128)(2,1)S(1)}, u32[]{:S(2)}, u32[]{:S(2)}) collective-permute-start(bf16[32,64,128]{2,1,0:T(8,128)(2,1)} %collective-permute-done.2.refs_4_), channel_id=1, source_target_pairs={{0,24},{8,0},{16,8},{24,16},{1,25},{9,1},{17,9},{25,17},{2,26},{10... | collective-permute-start | bytes 1572872 | tf_op jit(solution)/shard_map/ppermute | solution.py:25
  76.8 1.5 %all-to-all-done.1.own_ref = bf16[8,4,64,128]{3,2,1,0:T(8,128)(2,1)S(1)} async-done(((bf16[8,4,64,128]{3,2,1,0:T(8,128)(2,1)}), bf16[8,4,64,128]{3,2,1,0:T(8,128)(2,1)S(1)}, u32[]{:S(2)}, u32[]{:S(2)}) %all-to-all-start.1) | async-done | bytes 524320 | tf_op jit(solution)/shard_map/all_to_all | solution.py:35
  78.3 3.9 %left_products.1 = bf16[2,4,8,6,64,64]{5,4,3,2,1,0:T(8,128)(2,1)S(1)} custom-call(bf16[8,4,64,128]{3,2,1,0:T(8,128)(2,1)S(1)} %all-to-all-done.1.own_ref, bf16[2,4,8,6,64,64]{5,4,3,2,1,0:T(8,128)(2,1)} %bitcast.48), custom_call_target="tpu_custom_call" | custom-call | flops 201326592 | bytes 16777216 | tf_op jit(solution)/shard_map/left_products/pallas_call | solution.py:62
  82.2 0.0 collective-permute-done.4.refs_2_
  82.2 4.2 %panel_sums_1.1.refs_6_ = bf16[2,2,2,27,16,128]{5,4,3,2,1,0:T(8,128)(2,1)S(1)} custom-call(s32[408]{0:T(512)S(1)} %broadcast_add_fusion.refs_0_, s32[8]{0:T(128)S(1)} %pad_add_fusion.refs_1_, bf16[32,64,128]{2,1,0:T(8,128)(2,1)S(1)} %collective-permute-done.4.refs_2_, bf16[32,64,128]{2,1,0:T(8,128)(2,1)} %collective-permute-done.5.refs_3_, ...), custom_call_target="tpu_custom_call" | custom-call | flops 67108864 | bytes 8388608 | tf_op jit(solution)/shard_map/panel_sums_1/pallas_call | solution.py:134
  86.5 5.7 %panel_sums_0.1.refs_5_ = bf16[2,2,2,27,16,128]{5,4,3,2,1,0:T(8,128)(2,1)S(1)} custom-call(s32[408]{0:T(512)S(1)} %broadcast_add_fusion.refs_0_, s32[8]{0:T(128)S(1)} %pad_add_fusion.refs_1_, bf16[64,64,128]{2,1,0:T(8,128)(2,1)S(1)} %bitcast.47, bf16[32,64,128]{2,1,0:T(8,128)(2,1)} %collective-permute-done.refs_3_, ...), custom_call_target="tpu_custom_call" | custom-call | flops 134217728 | bytes 8388608 | tf_op jit(solution)/shard_map/panel_sums_0/pallas_call | solution.py:134
  92.2 0.6 collective-permute-done.3.refs_3_
  92.8 3.3 %panel_sums_2.1 = bf16[2,2,2,27,16,128]{5,4,3,2,1,0:T(8,128)(2,1)S(1)} custom-call(s32[408]{0:T(512)S(1)} %broadcast_add_fusion.refs_0_, s32[8]{0:T(128)S(1)} %pad_add_fusion.refs_1_, bf16[32,64,128]{2,1,0:T(8,128)(2,1)S(1)} %collective-permute-done.1.refs_2_, bf16[32,64,128]{2,1,0:T(8,128)(2,1)S(1)} %collective-permute-done.3.refs_3_, ...), custom_call_target="tpu_custom_call" | custom-call | flops 67108864 | bytes 8388608 | tf_op jit(solution)/shard_map/panel_sums_2/pallas_call | solution.py:134
  96.2 3.0 %collective-permute-start.6 = (bf16[2,2,27,16,128]{4,3,2,1,0:T(8,128)(2,1)S(1)}, bf16[2,2,27,16,128]{4,3,2,1,0:T(8,128)(2,1)S(1)}, u32[]{:S(2)}, u32[]{:S(2)}) collective-permute-start(bf16[2,2,27,16,128]{4,3,2,1,0:T(8,128)(2,1)S(1)} %slice_bitcast_fusion), channel_id=1, source_target_pairs={{0,1},{1,0},{2,3},{3,2},{4,5},{5,4},{6,7},{7,6},{8,9},{9,8},{10,11... | collective-permute-start | bytes 1327112 | tf_op jit(solution)/shard_map/ppermute | solution.py:29
  99.2 1.4 %collective-permute-done.6 = bf16[2,2,27,16,128]{4,3,2,1,0:T(8,128)(2,1)S(1)} collective-permute-done((bf16[2,2,27,16,128]{4,3,2,1,0:T(8,128)(2,1)S(1)}, bf16[2,2,27,16,128]{4,3,2,1,0:T(8,128)(2,1)S(1)}, u32[]{:S(2)}, u32[]{:S(2)}) %collective-permute-start.6) | collective-permute-done | bytes 442400 | tf_op jit(solution)/shard_map/ppermute | solution.py:29
  100.6 0.1 fusion.4
  100.7 0.8 fusion.35
  101.5 3.5 %collective-permute-start.7 = (bf16[2,27,8,128]{3,2,1,0:T(8,128)(2,1)S(1)}, bf16[2,27,8,128]{3,2,1,0:T(8,128)(2,1)S(1)}, u32[]{:S(2)}, u32[]{:S(2)}) collective-permute-start(bf16[2,27,8,128]{3,2,1,0:T(8,128)(2,1)S(1)} %dynamic-slice_bitcast_fusion), channel_id=1, source_target_pairs={{0,2},{2,0},{4,6},{6,4},{1,3},{3,1},{5,7},{7,5},{8,10},{10,8},{12,... | collective-permute-start | bytes 331784 | tf_op jit(solution)/shard_map/ppermute | solution.py:29
  105.1 3.4 %all-to-all-start.2 = ((bf16[4,27,8,128]{3,2,1,0:T(8,128)(2,1)}), bf16[4,27,8,128]{3,2,1,0:T(8,128)(2,1)S(1)}, u32[]{:S(2)}, u32[]{:S(2)}) async-start(bf16[4,27,8,128]{3,2,1,0:T(8,128)(2,1)} %bitcast.12), calls=%async_computation.2 | async-start | bytes 442368 | tf_op jit(solution)/shard_map/all_to_all | solution.py:193
  108.5 5.1 %collective-permute-start.8 = (bf16[27,8,128]{2,1,0:T(8,128)(2,1)S(1)}, bf16[27,8,128]{2,1,0:T(8,128)(2,1)S(1)}, u32[]{:S(2)}, u32[]{:S(2)}) collective-permute-start(bf16[27,8,128]{2,1,0:T(8,128)(2,1)S(1)} %get-tuple-element.23), channel_id=1, source_target_pairs={{0,12},{2,14},{4,8},{6,10},{8,20},{10,22},{12,16},{14,18},{16,28},... | collective-permute-start | bytes 165896 | tf_op jit(solution)/shard_map/ppermute | solution.py:201
  113.6 2.8 %collective-permute-start.9 = (bf16[27,8,128]{2,1,0:T(8,128)(2,1)S(1)}, bf16[27,8,128]{2,1,0:T(8,128)(2,1)S(1)}, u32[]{:S(2)}, u32[]{:S(2)}) collective-permute-start(bf16[27,8,128]{2,1,0:T(8,128)(2,1)S(1)} %get-tuple-element.24), channel_id=1, source_target_pairs={{0,8},{2,10},{4,12},{6,14},{8,16},{10,18},{12,20},{14,22},{16,24},... | collective-permute-start | bytes 165896 | tf_op jit(solution)/shard_map/ppermute | solution.py:202
  116.5 3.5 %collective-permute-done.8 = bf16[27,8,128]{2,1,0:T(8,128)(2,1)S(1)} collective-permute-done((bf16[27,8,128]{2,1,0:T(8,128)(2,1)S(1)}, bf16[27,8,128]{2,1,0:T(8,128)(2,1)S(1)}, u32[]{:S(2)}, u32[]{:S(2)}) %collective-permute-start.8) | collective-permute-done | bytes 55328 | tf_op jit(solution)/shard_map/ppermute | solution.py:201
  120.0 7.7 %collective-permute-done.9 = bf16[27,8,128]{2,1,0:T(8,128)(2,1)S(1)} collective-permute-done((bf16[27,8,128]{2,1,0:T(8,128)(2,1)S(1)}, bf16[27,8,128]{2,1,0:T(8,128)(2,1)S(1)}, u32[]{:S(2)}, u32[]{:S(2)}) %collective-permute-start.9) | collective-permute-done | bytes 55328 | tf_op jit(solution)/shard_map/ppermute | solution.py:202
  127.7 0.1 slice_bitcast_fusion.3
  127.8 0.7 pad_maximum_fusion
  (14 shorter events, 0.2 us)
Async XLA Ops:
  2.2 39.6 %all-to-all-start = ((bf16[16,4,64,128]{3,2,1,0:T(8,128)(2,1)}), bf16[16,4,64,128]{3,2,1,0:T(8,128)(2,1)S(1)}, u32[]{:S(2)}, u32[]{:S(2)}) async-start(bf16[16,4,64,128]{3,2,1,0:T(8,128)(2,1)} %broadcast_in_dim.29), calls=%async_computation | async-start | bytes 2097152 | tf_op jit(solution)/shard_map/all_to_all | solution.py:35
  42.9 27.4 %collective-permute-start = (bf16[32,64,128]{2,1,0:T(8,128)(2,1)}, bf16[32,64,128]{2,1,0:T(8,128)(2,1)}, u32[]{:S(2)}, u32[]{:S(2)}) collective-permute-start(bf16[32,64,128]{2,1,0:T(8,128)(2,1)} %get-tuple-element.16), channel_id=1, source_target_pairs={{0,8},{8,16},{16,24},{24,0},{1,9},{9,17},{17,25},{25,1},{2,10},{10... | collective-permute-start | bytes 1572872 | tf_op jit(solution)/shard_map/ppermute | solution.py:25
  46.0 26.2 %collective-permute-start.2 = (bf16[32,64,128]{2,1,0:T(8,128)(2,1)}, bf16[32,64,128]{2,1,0:T(8,128)(2,1)}, u32[]{:S(2)}, u32[]{:S(2)}) collective-permute-start(bf16[32,64,128]{2,1,0:T(8,128)(2,1)} %get-tuple-element.15), channel_id=1, source_target_pairs={{0,24},{8,0},{16,8},{24,16},{1,25},{9,1},{17,9},{25,17},{2,26},{10... | collective-permute-start | bytes 1572872 | tf_op jit(solution)/shard_map/ppermute | solution.py:25
  50.3 27.9 %all-to-all-start.1 = ((bf16[8,4,64,128]{3,2,1,0:T(8,128)(2,1)}), bf16[8,4,64,128]{3,2,1,0:T(8,128)(2,1)S(1)}, u32[]{:S(2)}, u32[]{:S(2)}) async-start(bf16[8,4,64,128]{3,2,1,0:T(8,128)(2,1)} %broadcast_in_dim.34), calls=%async_computation.1 | async-start | bytes 1048576 | tf_op jit(solution)/shard_map/all_to_all | solution.py:35
  63.8 18.4 %collective-permute-start.4 = (bf16[32,64,128]{2,1,0:T(8,128)(2,1)}, bf16[32,64,128]{2,1,0:T(8,128)(2,1)S(1)}, u32[]{:S(2)}, u32[]{:S(2)}) collective-permute-start(bf16[32,64,128]{2,1,0:T(8,128)(2,1)} %get-tuple-element.15), channel_id=1, source_target_pairs={{0,8},{8,16},{16,24},{24,0},{1,9},{9,17},{17,25},{25,1},{2,10},{10... | collective-permute-start | bytes 1572872 | tf_op jit(solution)/shard_map/ppermute | solution.py:25
  65.7 16.5 %collective-permute-start.5 = (bf16[32,64,128]{2,1,0:T(8,128)(2,1)}, bf16[32,64,128]{2,1,0:T(8,128)(2,1)}, u32[]{:S(2)}, u32[]{:S(2)}) collective-permute-start(bf16[32,64,128]{2,1,0:T(8,128)(2,1)} %get-tuple-element.16), channel_id=1, source_target_pairs={{0,24},{8,0},{16,8},{24,16},{1,25},{9,1},{17,9},{25,17},{2,26},{10... | collective-permute-start | bytes 1572872 | tf_op jit(solution)/shard_map/ppermute | solution.py:25
  70.3 21.9 %collective-permute-start.1 = (bf16[32,64,128]{2,1,0:T(8,128)(2,1)}, bf16[32,64,128]{2,1,0:T(8,128)(2,1)S(1)}, u32[]{:S(2)}, u32[]{:S(2)}) collective-permute-start(bf16[32,64,128]{2,1,0:T(8,128)(2,1)} %collective-permute-done.refs_3_), channel_id=1, source_target_pairs={{0,8},{8,16},{16,24},{24,0},{1,9},{9,17},{17,25},{25,1},{2,10},{10... | collective-permute-start | bytes 1572872 | tf_op jit(solution)/shard_map/ppermute | solution.py:25
  72.2 20.6 %collective-permute-start.3 = (bf16[32,64,128]{2,1,0:T(8,128)(2,1)}, bf16[32,64,128]{2,1,0:T(8,128)(2,1)S(1)}, u32[]{:S(2)}, u32[]{:S(2)}) collective-permute-start(bf16[32,64,128]{2,1,0:T(8,128)(2,1)} %collective-permute-done.2.refs_4_), channel_id=1, source_target_pairs={{0,24},{8,0},{16,8},{24,16},{1,25},{9,1},{17,9},{25,17},{2,26},{10... | collective-permute-start | bytes 1572872 | tf_op jit(solution)/shard_map/ppermute | solution.py:25
  96.2 4.4 %collective-permute-start.6 = (bf16[2,2,27,16,128]{4,3,2,1,0:T(8,128)(2,1)S(1)}, bf16[2,2,27,16,128]{4,3,2,1,0:T(8,128)(2,1)S(1)}, u32[]{:S(2)}, u32[]{:S(2)}) collective-permute-start(bf16[2,2,27,16,128]{4,3,2,1,0:T(8,128)(2,1)S(1)} %slice_bitcast_fusion), channel_id=1, source_target_pairs={{0,1},{1,0},{2,3},{3,2},{4,5},{5,4},{6,7},{7,6},{8,9},{9,8},{10,11... | collective-permute-start | bytes 1327112 | tf_op jit(solution)/shard_map/ppermute | solution.py:29
  101.5 7.0 %collective-permute-start.7 = (bf16[2,27,8,128]{3,2,1,0:T(8,128)(2,1)S(1)}, bf16[2,27,8,128]{3,2,1,0:T(8,128)(2,1)S(1)}, u32[]{:S(2)}, u32[]{:S(2)}) collective-permute-start(bf16[2,27,8,128]{3,2,1,0:T(8,128)(2,1)S(1)} %dynamic-slice_bitcast_fusion), channel_id=1, source_target_pairs={{0,2},{2,0},{4,6},{6,4},{1,3},{3,1},{5,7},{7,5},{8,10},{10,8},{12,... | collective-permute-start | bytes 331784 | tf_op jit(solution)/shard_map/ppermute | solution.py:29
  105.1 11.4 %all-to-all-start.2 = ((bf16[4,27,8,128]{3,2,1,0:T(8,128)(2,1)}), bf16[4,27,8,128]{3,2,1,0:T(8,128)(2,1)S(1)}, u32[]{:S(2)}, u32[]{:S(2)}) async-start(bf16[4,27,8,128]{3,2,1,0:T(8,128)(2,1)} %bitcast.12), calls=%async_computation.2 | async-start | bytes 442368 | tf_op jit(solution)/shard_map/all_to_all | solution.py:193
  108.5 11.5 %collective-permute-start.8 = (bf16[27,8,128]{2,1,0:T(8,128)(2,1)S(1)}, bf16[27,8,128]{2,1,0:T(8,128)(2,1)S(1)}, u32[]{:S(2)}, u32[]{:S(2)}) collective-permute-start(bf16[27,8,128]{2,1,0:T(8,128)(2,1)S(1)} %get-tuple-element.23), channel_id=1, source_target_pairs={{0,12},{2,14},{4,8},{6,10},{8,20},{10,22},{12,16},{14,18},{16,28},... | collective-permute-start | bytes 165896 | tf_op jit(solution)/shard_map/ppermute | solution.py:201
  113.6 14.1 %collective-permute-start.9 = (bf16[27,8,128]{2,1,0:T(8,128)(2,1)S(1)}, bf16[27,8,128]{2,1,0:T(8,128)(2,1)S(1)}, u32[]{:S(2)}, u32[]{:S(2)}) collective-permute-start(bf16[27,8,128]{2,1,0:T(8,128)(2,1)S(1)} %get-tuple-element.24), channel_id=1, source_target_pairs={{0,8},{2,10},{4,12},{6,14},{8,16},{10,18},{12,20},{14,22},{16,24},... | collective-permute-start | bytes 165896 | tf_op jit(solution)/shard_map/ppermute | solution.py:202

commit v11 on v8

--- a/solution.py
+++ b/solution.py
@@ -185,8 +185,8 @@
 
     b = left_products(spread(packed, COL), a_tiles)
     sums0 = panel_sums(0, code, info, [column, left_a, right_b], b)
-    sums1 = panel_sums(1, code, info, [left_b, right_a], b)
-    sums2 = panel_sums(2, code, info, [left2, right2], b, (sums0, sums1))
+    sums1 = panel_sums(1, code, info, [left_b, right_a], b, (sums0,))
+    sums2 = panel_sums(2, code, info, [left2, right2], b, (sums1,))
 
     chip = sums2[0].astype(F32) + swapped(sums2[1], "core", 1).astype(F32)
     staying = chip[..., :8, :].astype(BF16).reshape(NY, KC, 8, 2 * T)

time: 127 us -> 127 us (level)
  transfers between devices with their start and end apart: 13 -> 13, of which waited for: 6 -> 7; matrix products, arithmetic and copies ran while one was open for 4% -> 4% of each run, Pallas kernels for 11% -> 11%
where the time goes in v11:
time: 127 us; the launch traced here: 126 us
  starting transfers between devices  66.3 us (52%)
  waiting for transfers between devices  32 us (25%)
  Pallas kernels  17.7 us (14%)
  local copies, waits for them, and re-layouts  5.57 us (4%)
  other arithmetic  3.71 us (3%)
    all_to_all x2, starting transfers between devices, spread(): return lax.all_to_all(copies, axis, 0, 0, tiled=True)  29.7 us
    all_to_all x2, waiting for transfers between devices, spread(): return lax.all_to_all(copies, axis, 0, 0, tiled=True)  21.3 us
    ppermute x6, starting transfers between devices, shifted(): lax.ppermute(value, axis, [(i, (i + by) % count) for i in range(count)])  19.5 us
    pallas_call x3, Pallas kernels, panel_sums(): pl.pallas_call(functools.partial(sum_kernel, group, len(chunks), len(befo...  13.8 us
    ppermute x2, starting transfers between devices, swapped(): lax.ppermute(value, axis, [(i, i ^ by) for i in range(lax.axis_size(axis))])  5.83 us
    ppermute x1, waiting for transfers between devices, body(): lax.ppermute(pick(two, bit1, 0).astype(BF16), ROW + ('yl',), ahead[0])  5.14 us
    ppermute x1, starting transfers between devices, body(): lax.ppermute(pick(two, 1 - bit1, 0).astype(BF16), ROW + ('yl',), ahead[1])  5.11 us
    pallas_call x1, Pallas kernels, left_products(): pl.pallas_call(left_kernel, in_specs=[vmem, pl.BlockSpec(memory_space=plt...  3.94 us
  transfers between devices with their start and end apart: 13, of which 7 were waited for; matrix products, arithmetic and copies ran while one was open for 4% of the time, Pallas kernels for 11%

profile of v11, /device:TPU:1, one launch (start us, length us, event | category | flops | bytes accessed | tf_op | source)
XLA Modules:
  0.0 125.8 jit_solution(2853204322261037055)
XLA Ops:
  0.0 0.9 slice_bitcast_fusion.5
  0.9 0.1 pad_maximum_fusion.1
  1.0 1.2 broadcast_in_dim.29
  2.2 16.2 %all-to-all-start = ((bf16[16,4,64,128]{3,2,1,0:T(8,128)(2,1)}), bf16[16,4,64,128]{3,2,1,0:T(8,128)(2,1)S(1)}, u32[]{:S(2)}, u32[]{:S(2)}) async-start(bf16[16,4,64,128]{3,2,1,0:T(8,128)(2,1)} %broadcast_in_dim.29), calls=%async_computation | async-start | bytes 2097152 | tf_op jit(solution)/shard_map/all_to_all | solution.py:35
  18.4 0.7 fusion.33
  19.1 0.7 fusion.17
  19.9 0.1 copy.9
  19.9 0.1 eq.61
  20.1 0.7 iota_compare_fusion.3
  20.8 0.1 lt.71
  21.0 0.1 copy.10
  21.1 0.1 sub.97
  21.2 0.1 convert_reduce_fusion.1
  21.3 0.2 reduce-window.7
  21.5 0.1 pad_add_fusion.refs_1_
  21.6 0.2 fusion.3
  21.8 0.2 select_reduce_fusion
  22.0 19.8 %all-to-all-done = bf16[16,4,64,128]{3,2,1,0:T(8,128)(2,1)S(1)} async-done(((bf16[16,4,64,128]{3,2,1,0:T(8,128)(2,1)}), bf16[16,4,64,128]{3,2,1,0:T(8,128)(2,1)S(1)}, u32[]{:S(2)}, u32[]{:S(2)}) %all-to-all-start) | async-done | bytes 1048608 | tf_op jit(solution)/shard_map/all_to_all | solution.py:35
  41.8 1.0 fusion.34
  42.9 3.1 %collective-permute-start = (bf16[32,64,128]{2,1,0:T(8,128)(2,1)}, bf16[32,64,128]{2,1,0:T(8,128)(2,1)}, u32[]{:S(2)}, u32[]{:S(2)}) collective-permute-start(bf16[32,64,128]{2,1,0:T(8,128)(2,1)} %get-tuple-element.16), channel_id=1, source_target_pairs={{0,8},{8,16},{16,24},{24,0},{1,9},{9,17},{17,25},{25,1},{2,10},{10... | collective-permute-start | bytes 1572872 | tf_op jit(solution)/shard_map/ppermute | solution.py:25
  46.0 3.4 %collective-permute-start.2 = (bf16[32,64,128]{2,1,0:T(8,128)(2,1)}, bf16[32,64,128]{2,1,0:T(8,128)(2,1)}, u32[]{:S(2)}, u32[]{:S(2)}) collective-permute-start(bf16[32,64,128]{2,1,0:T(8,128)(2,1)} %get-tuple-element.15), channel_id=1, source_target_pairs={{0,24},{8,0},{16,8},{24,16},{1,25},{9,1},{17,9},{25,17},{2,26},{10... | collective-permute-start | bytes 1572872 | tf_op jit(solution)/shard_map/ppermute | solution.py:25
  49.4 0.9 broadcast_in_dim.34
  50.3 13.4 %all-to-all-start.1 = ((bf16[8,4,64,128]{3,2,1,0:T(8,128)(2,1)}), bf16[8,4,64,128]{3,2,1,0:T(8,128)(2,1)S(1)}, u32[]{:S(2)}, u32[]{:S(2)}) async-start(bf16[8,4,64,128]{3,2,1,0:T(8,128)(2,1)} %broadcast_in_dim.34), calls=%async_computation.1 | async-start | bytes 1048576 | tf_op jit(solution)/shard_map/all_to_all | solution.py:35
  63.7 1.9 %collective-permute-start.4 = (bf16[32,64,128]{2,1,0:T(8,128)(2,1)}, bf16[32,64,128]{2,1,0:T(8,128)(2,1)S(1)}, u32[]{:S(2)}, u32[]{:S(2)}) collective-permute-start(bf16[32,64,128]{2,1,0:T(8,128)(2,1)} %get-tuple-element.15), channel_id=1, source_target_pairs={{0,8},{8,16},{16,24},{24,0},{1,9},{9,17},{17,25},{25,1},{2,10},{10... | collective-permute-start | bytes 1572872 | tf_op jit(solution)/shard_map/ppermute | solution.py:25
  65.6 4.6 %collective-permute-start.5 = (bf16[32,64,128]{2,1,0:T(8,128)(2,1)}, bf16[32,64,128]{2,1,0:T(8,128)(2,1)S(1)}, u32[]{:S(2)}, u32[]{:S(2)}) collective-permute-start(bf16[32,64,128]{2,1,0:T(8,128)(2,1)} %get-tuple-element.16), channel_id=1, source_target_pairs={{0,24},{8,0},{16,8},{24,16},{1,25},{9,1},{17,9},{25,17},{2,26},{10... | collective-permute-start | bytes 1572872 | tf_op jit(solution)/shard_map/ppermute | solution.py:25
  70.2 1.9 %collective-permute-start.1 = (bf16[32,64,128]{2,1,0:T(8,128)(2,1)}, bf16[32,64,128]{2,1,0:T(8,128)(2,1)S(1)}, u32[]{:S(2)}, u32[]{:S(2)}) collective-permute-start(bf16[32,64,128]{2,1,0:T(8,128)(2,1)} %collective-permute-done.refs_3_), channel_id=1, source_target_pairs={{0,8},{8,16},{16,24},{24,0},{1,9},{9,17},{17,25},{25,1},{2,10},{10... | collective-permute-start | bytes 1572872 | tf_op jit(solution)/shard_map/ppermute | solution.py:25
  72.2 4.6 %collective-permute-start.3 = (bf16[32,64,128]{2,1,0:T(8,128)(2,1)}, bf16[32,64,128]{2,1,0:T(8,128)(2,1)}, u32[]{:S(2)}, u32[]{:S(2)}) collective-permute-start(bf16[32,64,128]{2,1,0:T(8,128)(2,1)} %collective-permute-done.2.refs_4_), channel_id=1, source_target_pairs={{0,24},{8,0},{16,8},{24,16},{1,25},{9,1},{17,9},{25,17},{2,26},{10... | collective-permute-start | bytes 1572872 | tf_op jit(solution)/shard_map/ppermute | solution.py:25
  76.7 1.5 %all-to-all-done.1.own_ref = bf16[8,4,64,128]{3,2,1,0:T(8,128)(2,1)S(1)} async-done(((bf16[8,4,64,128]{3,2,1,0:T(8,128)(2,1)}), bf16[8,4,64,128]{3,2,1,0:T(8,128)(2,1)S(1)}, u32[]{:S(2)}, u32[]{:S(2)}) %all-to-all-start.1) | async-done | bytes 524320 | tf_op jit(solution)/shard_map/all_to_all | solution.py:35
  78.2 3.9 %left_products.1 = bf16[2,4,8,6,64,64]{5,4,3,2,1,0:T(8,128)(2,1)S(1)} custom-call(bf16[8,4,64,128]{3,2,1,0:T(8,128)(2,1)S(1)} %all-to-all-done.1.own_ref, bf16[2,4,8,6,64,64]{5,4,3,2,1,0:T(8,128)(2,1)} %bitcast.48), custom_call_target="tpu_custom_call" | custom-call | flops 201326592 | bytes 16777216 | tf_op jit(solution)/shard_map/left_products/pallas_call | solution.py:62
  82.2 6.0 %panel_sums_0.1.refs_5_ = bf16[2,2,2,27,16,128]{5,4,3,2,1,0:T(8,128)(2,1)S(1)} custom-call(s32[408]{0:T(512)S(1)} %broadcast_add_fusion.refs_0_, s32[8]{0:T(128)S(1)} %pad_add_fusion.refs_1_, bf16[64,64,128]{2,1,0:T(8,128)(2,1)S(1)} %bitcast.47, bf16[32,64,128]{2,1,0:T(8,128)(2,1)} %collective-permute-done.refs_3_, ...), custom_call_target="tpu_custom_call" | custom-call | flops 134217728 | bytes 8388608 | tf_op jit(solution)/shard_map/panel_sums_0/pallas_call | solution.py:134
  88.2 0.0 collective-permute-done.4.refs_2_
  88.2 0.0 collective-permute-done.5.refs_3_
  88.2 3.4 %panel_sums_1.1.refs_5_ = bf16[2,2,2,27,16,128]{5,4,3,2,1,0:T(8,128)(2,1)S(1)} custom-call(s32[408]{0:T(512)S(1)} %broadcast_add_fusion.refs_0_, s32[8]{0:T(128)S(1)} %pad_add_fusion.refs_1_, bf16[32,64,128]{2,1,0:T(8,128)(2,1)S(1)} %collective-permute-done.4.refs_2_, bf16[32,64,128]{2,1,0:T(8,128)(2,1)S(1)} %collective-permute-done.5.refs_3_, ...), custom_call_target="tpu_custom_call" | custom-call | flops 67108864 | bytes 8388608 | tf_op jit(solution)/shard_map/panel_sums_1/pallas_call | solution.py:134
  91.6 0.2 collective-permute-done.1.refs_2_
  91.8 1.0 collective-permute-done.3.refs_3_
  92.8 4.4 %panel_sums_2.1 = bf16[2,2,2,27,16,128]{5,4,3,2,1,0:T(8,128)(2,1)S(1)} custom-call(s32[408]{0:T(512)S(1)} %broadcast_add_fusion.refs_0_, s32[8]{0:T(128)S(1)} %pad_add_fusion.refs_1_, bf16[32,64,128]{2,1,0:T(8,128)(2,1)S(1)} %collective-permute-done.1.refs_2_, bf16[32,64,128]{2,1,0:T(8,128)(2,1)} %collective-permute-done.3.refs_3_, ...), custom_call_target="tpu_custom_call" | custom-call | flops 67108864 | bytes 8388608 | tf_op jit(solution)/shard_map/panel_sums_2/pallas_call | solution.py:134
  97.2 2.7 %collective-permute-start.6 = (bf16[2,2,27,16,128]{4,3,2,1,0:T(8,128)(2,1)S(1)}, bf16[2,2,27,16,128]{4,3,2,1,0:T(8,128)(2,1)S(1)}, u32[]{:S(2)}, u32[]{:S(2)}) collective-permute-start(bf16[2,2,27,16,128]{4,3,2,1,0:T(8,128)(2,1)S(1)} %slice_bitcast_fusion), channel_id=1, source_target_pairs={{0,1},{1,0},{2,3},{3,2},{4,5},{5,4},{6,7},{7,6},{8,9},{9,8},{10,11... | collective-permute-start | bytes 1327112 | tf_op jit(solution)/shard_map/ppermute | solution.py:29
  100.0 1.4 %collective-permute-done.6 = bf16[2,2,27,16,128]{4,3,2,1,0:T(8,128)(2,1)S(1)} collective-permute-done((bf16[2,2,27,16,128]{4,3,2,1,0:T(8,128)(2,1)S(1)}, bf16[2,2,27,16,128]{4,3,2,1,0:T(8,128)(2,1)S(1)}, u32[]{:S(2)}, u32[]{:S(2)}) %collective-permute-start.6) | collective-permute-done | bytes 442400 | tf_op jit(solution)/shard_map/ppermute | solution.py:29
  101.4 0.1 fusion.4
  101.5 0.8 fusion.35
  102.3 3.1 %collective-permute-start.7 = (bf16[2,27,8,128]{3,2,1,0:T(8,128)(2,1)S(1)}, bf16[2,27,8,128]{3,2,1,0:T(8,128)(2,1)S(1)}, u32[]{:S(2)}, u32[]{:S(2)}) collective-permute-start(bf16[2,27,8,128]{3,2,1,0:T(8,128)(2,1)S(1)} %dynamic-slice_bitcast_fusion), channel_id=1, source_target_pairs={{0,2},{2,0},{4,6},{6,4},{1,3},{3,1},{5,7},{7,5},{8,10},{10,8},{12,... | collective-permute-start | bytes 331784 | tf_op jit(solution)/shard_map/ppermute | solution.py:29
  105.4 3.4 %all-to-all-start.2 = ((bf16[4,27,8,128]{3,2,1,0:T(8,128)(2,1)}), bf16[4,27,8,128]{3,2,1,0:T(8,128)(2,1)S(1)}, u32[]{:S(2)}, u32[]{:S(2)}) async-start(bf16[4,27,8,128]{3,2,1,0:T(8,128)(2,1)} %bitcast.12), calls=%async_computation.2 | async-start | bytes 442368 | tf_op jit(solution)/shard_map/all_to_all | solution.py:193
  108.9 2.9 %collective-permute-start.8 = (bf16[27,8,128]{2,1,0:T(8,128)(2,1)S(1)}, bf16[27,8,128]{2,1,0:T(8,128)(2,1)S(1)}, u32[]{:S(2)}, u32[]{:S(2)}) collective-permute-start(bf16[27,8,128]{2,1,0:T(8,128)(2,1)S(1)} %get-tuple-element.23), channel_id=1, source_target_pairs={{0,8},{2,10},{4,12},{6,14},{8,16},{10,18},{12,20},{14,22},{16,24},... | collective-permute-start | bytes 165896 | tf_op jit(solution)/shard_map/ppermute | solution.py:201
  111.7 5.1 %collective-permute-start.9 = (bf16[27,8,128]{2,1,0:T(8,128)(2,1)S(1)}, bf16[27,8,128]{2,1,0:T(8,128)(2,1)S(1)}, u32[]{:S(2)}, u32[]{:S(2)}) collective-permute-start(bf16[27,8,128]{2,1,0:T(8,128)(2,1)S(1)} %get-tuple-element.24), channel_id=1, source_target_pairs={{0,12},{2,14},{4,8},{6,10},{8,20},{10,22},{12,16},{14,18},{16,28},... | collective-permute-start | bytes 165896 | tf_op jit(solution)/shard_map/ppermute | solution.py:202
  116.9 5.1 %collective-permute-done.8 = bf16[27,8,128]{2,1,0:T(8,128)(2,1)S(1)} collective-permute-done((bf16[27,8,128]{2,1,0:T(8,128)(2,1)S(1)}, bf16[27,8,128]{2,1,0:T(8,128)(2,1)S(1)}, u32[]{:S(2)}, u32[]{:S(2)}) %collective-permute-start.8) | collective-permute-done | bytes 55328 | tf_op jit(solution)/shard_map/ppermute | solution.py:201
  122.0 3.0 %collective-permute-done.9 = bf16[27,8,128]{2,1,0:T(8,128)(2,1)S(1)} collective-permute-done((bf16[27,8,128]{2,1,0:T(8,128)(2,1)S(1)}, bf16[27,8,128]{2,1,0:T(8,128)(2,1)S(1)}, u32[]{:S(2)}, u32[]{:S(2)}) %collective-permute-start.9) | collective-permute-done | bytes 55328 | tf_op jit(solution)/shard_map/ppermute | solution.py:202
  125.0 0.1 slice_bitcast_fusion.3
  125.1 0.7 pad_maximum_fusion
  (14 shorter events, 0.2 us)
Async XLA Ops:
  2.2 39.6 %all-to-all-start = ((bf16[16,4,64,128]{3,2,1,0:T(8,128)(2,1)}), bf16[16,4,64,128]{3,2,1,0:T(8,128)(2,1)S(1)}, u32[]{:S(2)}, u32[]{:S(2)}) async-start(bf16[16,4,64,128]{3,2,1,0:T(8,128)(2,1)} %broadcast_in_dim.29), calls=%async_computation | async-start | bytes 2097152 | tf_op jit(solution)/shard_map/all_to_all | solution.py:35
  42.9 27.4 %collective-permute-start = (bf16[32,64,128]{2,1,0:T(8,128)(2,1)}, bf16[32,64,128]{2,1,0:T(8,128)(2,1)}, u32[]{:S(2)}, u32[]{:S(2)}) collective-permute-start(bf16[32,64,128]{2,1,0:T(8,128)(2,1)} %get-tuple-element.16), channel_id=1, source_target_pairs={{0,8},{8,16},{16,24},{24,0},{1,9},{9,17},{17,25},{25,1},{2,10},{10... | collective-permute-start | bytes 1572872 | tf_op jit(solution)/shard_map/ppermute | solution.py:25
  46.0 26.2 %collective-permute-start.2 = (bf16[32,64,128]{2,1,0:T(8,128)(2,1)}, bf16[32,64,128]{2,1,0:T(8,128)(2,1)}, u32[]{:S(2)}, u32[]{:S(2)}) collective-permute-start(bf16[32,64,128]{2,1,0:T(8,128)(2,1)} %get-tuple-element.15), channel_id=1, source_target_pairs={{0,24},{8,0},{16,8},{24,16},{1,25},{9,1},{17,9},{25,17},{2,26},{10... | collective-permute-start | bytes 1572872 | tf_op jit(solution)/shard_map/ppermute | solution.py:25
  50.3 27.9 %all-to-all-start.1 = ((bf16[8,4,64,128]{3,2,1,0:T(8,128)(2,1)}), bf16[8,4,64,128]{3,2,1,0:T(8,128)(2,1)S(1)}, u32[]{:S(2)}, u32[]{:S(2)}) async-start(bf16[8,4,64,128]{3,2,1,0:T(8,128)(2,1)} %broadcast_in_dim.34), calls=%async_computation.1 | async-start | bytes 1048576 | tf_op jit(solution)/shard_map/all_to_all | solution.py:35
  63.7 24.4 %collective-permute-start.4 = (bf16[32,64,128]{2,1,0:T(8,128)(2,1)}, bf16[32,64,128]{2,1,0:T(8,128)(2,1)S(1)}, u32[]{:S(2)}, u32[]{:S(2)}) collective-permute-start(bf16[32,64,128]{2,1,0:T(8,128)(2,1)} %get-tuple-element.15), channel_id=1, source_target_pairs={{0,8},{8,16},{16,24},{24,0},{1,9},{9,17},{17,25},{25,1},{2,10},{10... | collective-permute-start | bytes 1572872 | tf_op jit(solution)/shard_map/ppermute | solution.py:25
  65.6 22.5 %collective-permute-start.5 = (bf16[32,64,128]{2,1,0:T(8,128)(2,1)}, bf16[32,64,128]{2,1,0:T(8,128)(2,1)S(1)}, u32[]{:S(2)}, u32[]{:S(2)}) collective-permute-start(bf16[32,64,128]{2,1,0:T(8,128)(2,1)} %get-tuple-element.16), channel_id=1, source_target_pairs={{0,24},{8,0},{16,8},{24,16},{1,25},{9,1},{17,9},{25,17},{2,26},{10... | collective-permute-start | bytes 1572872 | tf_op jit(solution)/shard_map/ppermute | solution.py:25
  70.2 21.6 %collective-permute-start.1 = (bf16[32,64,128]{2,1,0:T(8,128)(2,1)}, bf16[32,64,128]{2,1,0:T(8,128)(2,1)S(1)}, u32[]{:S(2)}, u32[]{:S(2)}) collective-permute-start(bf16[32,64,128]{2,1,0:T(8,128)(2,1)} %collective-permute-done.refs_3_), channel_id=1, source_target_pairs={{0,8},{8,16},{16,24},{24,0},{1,9},{9,17},{17,25},{25,1},{2,10},{10... | collective-permute-start | bytes 1572872 | tf_op jit(solution)/shard_map/ppermute | solution.py:25
  72.2 20.6 %collective-permute-start.3 = (bf16[32,64,128]{2,1,0:T(8,128)(2,1)}, bf16[32,64,128]{2,1,0:T(8,128)(2,1)}, u32[]{:S(2)}, u32[]{:S(2)}) collective-permute-start(bf16[32,64,128]{2,1,0:T(8,128)(2,1)} %collective-permute-done.2.refs_4_), channel_id=1, source_target_pairs={{0,24},{8,0},{16,8},{24,16},{1,25},{9,1},{17,9},{25,17},{2,26},{10... | collective-permute-start | bytes 1572872 | tf_op jit(solution)/shard_map/ppermute | solution.py:25
  97.2 4.2 %collective-permute-start.6 = (bf16[2,2,27,16,128]{4,3,2,1,0:T(8,128)(2,1)S(1)}, bf16[2,2,27,16,128]{4,3,2,1,0:T(8,128)(2,1)S(1)}, u32[]{:S(2)}, u32[]{:S(2)}) collective-permute-start(bf16[2,2,27,16,128]{4,3,2,1,0:T(8,128)(2,1)S(1)} %slice_bitcast_fusion), channel_id=1, source_target_pairs={{0,1},{1,0},{2,3},{3,2},{4,5},{5,4},{6,7},{7,6},{8,9},{9,8},{10,11... | collective-permute-start | bytes 1327112 | tf_op jit(solution)/shard_map/ppermute | solution.py:29
  102.3 6.5 %collective-permute-start.7 = (bf16[2,27,8,128]{3,2,1,0:T(8,128)(2,1)S(1)}, bf16[2,27,8,128]{3,2,1,0:T(8,128)(2,1)S(1)}, u32[]{:S(2)}, u32[]{:S(2)}) collective-permute-start(bf16[2,27,8,128]{3,2,1,0:T(8,128)(2,1)S(1)} %dynamic-slice_bitcast_fusion), channel_id=1, source_target_pairs={{0,2},{2,0},{4,6},{6,4},{1,3},{3,1},{5,7},{7,5},{8,10},{10,8},{12,... | collective-permute-start | bytes 331784 | tf_op jit(solution)/shard_map/ppermute | solution.py:29
  105.4 11.5 %all-to-all-start.2 = ((bf16[4,27,8,128]{3,2,1,0:T(8,128)(2,1)}), bf16[4,27,8,128]{3,2,1,0:T(8,128)(2,1)S(1)}, u32[]{:S(2)}, u32[]{:S(2)}) async-start(bf16[4,27,8,128]{3,2,1,0:T(8,128)(2,1)} %bitcast.12), calls=%async_computation.2 | async-start | bytes 442368 | tf_op jit(solution)/shard_map/all_to_all | solution.py:193
  108.9 13.2 %collective-permute-start.8 = (bf16[27,8,128]{2,1,0:T(8,128)(2,1)S(1)}, bf16[27,8,128]{2,1,0:T(8,128)(2,1)S(1)}, u32[]{:S(2)}, u32[]{:S(2)}) collective-permute-start(bf16[27,8,128]{2,1,0:T(8,128)(2,1)S(1)} %get-tuple-element.23), channel_id=1, source_target_pairs={{0,8},{2,10},{4,12},{6,14},{8,16},{10,18},{12,20},{14,22},{16,24},... | collective-permute-start | bytes 165896 | tf_op jit(solution)/shard_map/ppermute | solution.py:201
  111.7 13.3 %collective-permute-start.9 = (bf16[27,8,128]{2,1,0:T(8,128)(2,1)S(1)}, bf16[27,8,128]{2,1,0:T(8,128)(2,1)S(1)}, u32[]{:S(2)}, u32[]{:S(2)}) collective-permute-start(bf16[27,8,128]{2,1,0:T(8,128)(2,1)S(1)} %get-tuple-element.24), channel_id=1, source_target_pairs={{0,12},{2,14},{4,8},{6,10},{8,20},{10,22},{12,16},{14,18},{16,28},... | collective-permute-start | bytes 165896 | tf_op jit(solution)/shard_map/ppermute | solution.py:202
